TPU v7x, 32 devices: a whole 2x2x4 slice. The times are simulated.
32 devices in a mesh: groups: 2 (over x), gx: 4 (over y, core), gy: 4 (over z).
Axes of the slice: x: 2, y: 2, z: 4, core: 2. Of those that a mesh axis runs over, the one named last changes fastest.
Arguments:
- tokens: bfloat16 [64, 2, 16384], P('groups', None, 'gx'), parts along dimension 0
- norm_gain: bfloat16 [16384], P('gx'), may hold values from 0.099609375 to 1.8984375
- qkv_weight: bfloat16 [16384, 8, 18, 128], P('gx', 'gy'), may hold values from -0.046875 to 0.046875
- out_weight: bfloat16 [128, 128, 16384], P('gy', None, 'gx'), may hold values from -0.125 to 0.125
- kv_cache: bfloat16 [64, 384, 2, 8, 128], P(('groups', 'gx', 'gy')), parts along dimension 0
- lengths: int32 [64], P(('groups', 'gx', 'gy')), parts along dimension 0, may hold values from 1 to 384, as said below
- positions: int32 [64], P('groups'), parts along dimension 0, may hold values from 0 to 4095
Outputs:
- layer_out: float32 [64, 2, 16384], P(('groups', 'gy'), None, 'gx'), parts along dimension 0
There are 2 independent parts, one for each index of `groups`. A program takes and returns all parts, laid end to end along the dimension named above; an argument that names none is the same for every part. Nothing has to cross between parts.
Inputs may be any that keep to these rules, and one draw needn't show every extreme that they name: Cache slots 0 to lengths - 1 of a row hold its earlier tokens; some row has exactly 384.
All inputs are finite; a program needn't handle non-finite values.
Results may differ from a plain program's by a relative error of at most 0.025.
Values may be sent and summed in bfloat16 or wider, within the bound.
No kernel may reach another device: no remote copies, remote signals or barrier semaphores. Data moves between devices by JAX's collectives and lax.ppermute only.
A program may use at most 192 MiB of HBM per device.

v0:
```python
import math

import jax
import jax.numpy as jnp
from jax import lax
from jax.sharding import PartitionSpec as P

D = 16384


norm_eps = 1e-05
rope_base = 500000.0


def rotate(values, places):
    half_dim = values.shape[-1] // 2
    index_half = jnp.arange(half_dim, dtype=jnp.float32)
    frequency = rope_base ** (-2.0 * index_half / values.shape[-1])
    angles = places[..., None] * frequency
    cosine = jnp.cos(angles)
    sine_part = jnp.sin(angles)
    front_half = values[..., :half_dim]
    back_half = values[..., half_dim:]
    return jnp.concatenate(
        [front_half * cosine - back_half * sine_part, back_half * cosine + front_half * sine_part],
        axis=-1,
    )


def finish(projected, positions, first_row, row_count):
    group_size = projected.shape[3] - 2
    placed = lax.dynamic_slice_in_dim(positions, first_row, row_count, 0)
    places = (placed[:, None] + jnp.arange(2, dtype=jnp.int32)[None, :]).astype(jnp.float32)
    queries = rotate(projected[:, :, :, :group_size], places[:, :, None, None])
    key_new = rotate(projected[:, :, :, group_size : group_size + 1], places[:, :, None, None])
    value_new = projected[:, :, :, group_size + 1 :]
    return jnp.concatenate([queries, key_new, value_new], axis=3).astype(jnp.bfloat16)


def attend(queries, key_new, value_new, cache_rows, length):
    scale_factor = 1.0 / math.sqrt(queries.shape[-1])
    scores_old = (
        jnp.einsum(
            "rtgid,rsgd->rtgis", queries, cache_rows[:, :, 0], preferred_element_type=jnp.float32
        )
        * scale_factor
    )
    slot_ids = jnp.arange(cache_rows.shape[1], dtype=jnp.int32)
    visible = slot_ids[None, :] < length[:, None]
    scores_old = jnp.where(visible[:, None, None, None, :], scores_old, -1e30)
    scores_new = (
        jnp.einsum("rtgid,rugd->rtgiu", queries, key_new, preferred_element_type=jnp.float32)
        * scale_factor
    )
    token_ids = jnp.arange(queries.shape[1], dtype=jnp.int32)
    causal = token_ids[:, None] >= token_ids[None, :]
    scores_new = jnp.where(causal[None, :, None, None, :], scores_new, -1e30)
    highest = jnp.maximum(jnp.max(scores_old, axis=-1), jnp.max(scores_new, axis=-1))
    expo_old = jnp.exp(scores_old - highest[..., None])
    expo_new = jnp.exp(scores_new - highest[..., None])
    denominator = jnp.sum(expo_old, axis=-1) + jnp.sum(expo_new, axis=-1)
    weight_old = (expo_old / denominator[..., None]).astype(jnp.bfloat16)
    weight_new = (expo_new / denominator[..., None]).astype(jnp.bfloat16)
    attended = jnp.einsum(
        "rtgis,rsgd->rtgid", weight_old, cache_rows[:, :, 1], preferred_element_type=jnp.float32
    )
    attended = attended + jnp.einsum(
        "rtgiu,rugd->rtgid", weight_new, value_new, preferred_element_type=jnp.float32
    )
    return attended.astype(jnp.bfloat16)


def body(tokens, norm_gain, qkv_weight, out_weight, kv_cache, lengths, positions):
    rows_local = kv_cache.shape[0]
    head_devices = lax.axis_size("gy")
    width_index = lax.axis_index("gx")
    head_index = lax.axis_index("gy")
    total_rows = tokens.shape[0]
    local_width = tokens.shape[2]
    groups_local = qkv_weight.shape[1]
    group_width = qkv_weight.shape[2]
    head_dim = qkv_weight.shape[3]
    group_size = group_width - 2
    tokens_wide = tokens.astype(jnp.float32)
    hidden = (tokens_wide * norm_gain.astype(jnp.float32)).astype(jnp.bfloat16)
    squares = jnp.sum(tokens_wide * tokens_wide, axis=-1)
    block_rows = rows_local * head_devices
    partial_value = jnp.dot(
        hidden.reshape(total_rows * 2, local_width),
        qkv_weight.reshape(local_width, -1),
        preferred_element_type=jnp.float32,
    )
    partial_value = partial_value.reshape(total_rows, 2, groups_local, group_width, head_dim)
    block_sum, block_squares = (
        lax.psum_scatter(partial_value, "gx", scatter_dimension=0, tiled=True),
        lax.psum_scatter(squares, "gx", scatter_dimension=0, tiled=True),
    )
    inv_rms = lax.rsqrt(block_squares / D + norm_eps)
    ready = finish(
        block_sum * inv_rms[:, :, None, None, None], positions, width_index * block_rows, block_rows
    )
    packed = lax.all_to_all(ready, "gy", split_axis=0, concat_axis=2, tiled=True)
    queries = packed[:, :, :, :group_size]
    key_new = packed[:, :, :, group_size]
    value_new = packed[:, :, :, group_size + 1]
    attended = attend(queries, key_new, value_new, kv_cache, lengths)
    regrouped = lax.all_to_all(attended, "gy", split_axis=2, concat_axis=0, tiled=True)
    out_flat = out_weight.reshape(-1, local_width)
    row_piece = lax.all_gather(regrouped, "gx", axis=0, tiled=True)
    piece_rows = row_piece.shape[0]
    product = jnp.dot(
        row_piece.reshape(piece_rows * 2, -1), out_flat, preferred_element_type=jnp.float32
    )
    terms = product.reshape(piece_rows, 2, local_width)
    own_sum = lax.psum_scatter(terms, "gy", scatter_dimension=0, tiled=True)
    row_share = total_rows // head_devices
    residual = lax.dynamic_slice_in_dim(tokens, head_index * row_share, row_share, 0).astype(
        jnp.float32
    )
    return residual + own_sum


def solution(mesh):
    return jax.shard_map(
        body,
        mesh=mesh,
        in_specs=(
            P("groups", None, "gx"),
            P("gx"),
            P("gx", "gy", None, None),
            P("gy", None, "gx"),
            P(("groups", "gx", "gy"), None, None, None, None),
            P(("groups", "gx", "gy")),
            P("groups"),
        ),
        out_specs=P(("groups", "gy"), None, "gx"),
        check_vma=False,
    )
```

profile of v0, /device:TPU:0, one launch (start us, length us, event | category | flops | bytes accessed | tf_op | source)
XLA Modules:
  0.0 225.2 jit_solution(11655905521266195650)
XLA Ops:
  6.5 91.1 %copy.60 = bf16[4096,2,18,128]{0,3,2,1:T(8,128)(2,1)} copy(bf16[4096,2,18,128]{3,1,2,0:T(2,128)(2,1)} %param.9) | data formatting | bytes 75497472 | tf_op args[2]
  97.7 1.1 fusion.13
  98.8 17.5 %fusion = f32[32,2,2,18,128]{4,0,3,2,1:T(8,128)} fusion(bf16[4096,2,18,128]{0,3,2,1:T(8,128)(2,1)} %copy.60, bf16[32,2,4096,1,1]{2,1,0,4,3:T(2,128)(2,1)S(1)} %get-tuple-element.8), kind=kOutput, calls=%fused_computation | convolution fusion | flops 2415919104 | bytes 39452672 | tf_op jit(solution)/shard_map/dot_general | solution.py:88
  116.3 0.1 copy.62
  116.4 0.6 dynamic-slice
  117.7 0.1 dynamic_slice.7
  117.7 8.3 %all-reduce = f32[32,2]{0,1:T(2,128)S(1)} all-reduce(f32[32,2]{0,1:T(2,128)S(1)} %copy.62), channel_id=3, replica_groups=mesh['groups'=2,'gx'=4,'gy'=4] {'gx'}, use_global_device_ids=true, to_apply=%region_2.0.clone | all-reduce | flops 64 | bytes 512
  126.1 0.1 fusion.29
  126.2 0.1 multiply_cosine_fusion
  126.3 2.2 fusion.30
  128.6 16.3 %reduce-scatter.4.cloned.1.call-done = f32[8,2,2,18,128]{4,0,3,2,1:T(8,128)} async-done(((f32[32,2,2,18,128]{4,0,3,2,1:T(8,128)}), f32[8,2,2,18,128]{4,0,3,2,1:T(8,128)}) %reduce-scatter.4.cloned.1.call-update) | async-done | bytes 294928 | tf_op jit(solution)/shard_map/reduce_scatter | solution.py:95
  144.9 1.0 broadcast_multiply_fusion
  146.0 0.1 subtract_convert_fusion.1
  146.0 0.1 subtract_convert_fusion
  146.2 0.1 pad_maximum_fusion
  146.3 0.8 copy.63
  147.1 4.6 %all-to-all-start = ((bf16[8,2,2,18,128]{4,2,3,1,0:T(2,128)(2,1)}), bf16[8,2,2,18,128]{4,2,3,1,0:T(2,128)(2,1)S(1)}, u32[]{:S(2)}, u32[]{:S(2)}) async-start(bf16[8,2,2,18,128]{4,2,3,1,0:T(2,128)(2,1)} %copy.63), calls=%async_computation.1 | async-start | bytes 294912 | tf_op jit(solution)/shard_map/all_to_all | solution.py:102
  151.8 6.2 %all-to-all-done = bf16[8,2,2,18,128]{4,2,3,1,0:T(2,128)(2,1)S(1)} async-done(((bf16[8,2,2,18,128]{4,2,3,1,0:T(2,128)(2,1)}), bf16[8,2,2,18,128]{4,2,3,1,0:T(2,128)(2,1)S(1)}, u32[]{:S(2)}, u32[]{:S(2)}) %all-to-all-start) | async-done | bytes 147488 | tf_op jit(solution)/shard_map/all_to_all | solution.py:102
  158.0 0.4 fusion.33
  158.5 0.8 fusion.32
  159.2 0.3 fusion.14
  159.6 0.1 fusion.23
  159.7 0.2 convolution_bitcast_fusion
  159.9 0.5 fusion.9
  160.5 8.6 %all_to_all.36 = bf16[2,2,8,16,128]{4,3,1,0,2:T(8,128)(2,1)S(1)} all-to-all(bf16[2,2,8,16,128]{4,3,1,0,2:T(8,128)(2,1)S(1)} %copy.71), channel_id=1, replica_groups=mesh['groups'=2,'gx'=4,'gy'=4] {'gy'}, dimensions={2} | all-to-all | bytes 262144 | tf_op jit(solution)/shard_map/all_to_all | solution.py:107
  169.1 6.5 %all_gather.3 = bf16[32,2,2,16,128]{4,3,2,1,0:T(8,128)(2,1)S(1)} all-gather(bf16[8,2,2,16,128]{4,3,2,1,0:T(8,128)(2,1)S(1)} %bitcast.81), channel_id=1, replica_groups=mesh['groups'=2,'gx'=4,'gy'=4] {'gx'}, dimensions={0}, use_global_device_ids=true | all-gather | bytes 655360 | tf_op jit(solution)/shard_map/all_gather | solution.py:109
  175.6 0.1 reshape.103
  175.7 14.6 %fusion.16 = f32[32,2,4096]{2,0,1:T(8,128)} fusion(bf16[4096,4096,1]{1,0,2:T(8,128)(2,1)} %bitcast.76, bf16[32,2,4096]{2,1,0:T(2,128)(2,1)S(1)} %reshape.103), kind=kOutput, calls=%fused_computation.24 | convolution fusion | flops 2147483648 | bytes 35127296 | tf_op jit(solution)/shard_map/dot_general | solution.py:111
  190.4 1.0 constant_dynamic-slice_fusion
  191.4 25.0 %reduce-scatter.6.cloned.1.call-done = f32[8,2,4096]{2,0,1:T(8,128)} async-done(((f32[32,2,4096]{2,0,1:T(8,128)}), f32[8,2,4096]{2,0,1:T(8,128)}) %reduce-scatter.6.cloned.1.call-update) | async-done | bytes 262160 | tf_op jit(solution)/shard_map/reduce_scatter | solution.py:115
  216.4 1.0 convert_add_fusion
  217.4 0.9 copy.75
  (27 shorter events, 0.3 us)
Async XLA Ops:
  6.5 91.1 %copy-start.1 = (bf16[4096]{0:T(1024)(128)(2,1)S(1)}, bf16[4096]{0:T(1024)(128)(2,1)}, u32[]{:S(2)}) copy-start(bf16[4096]{0:T(1024)(128)(2,1)} %param.8) | copy-start | bytes 24580
  6.5 91.1 %copy-start = (bf16[32,2,4096]{2,1,0:T(2,128)(2,1)S(1)}, bf16[32,2,4096]{2,1,0:T(2,128)(2,1)}, u32[]{:S(2)}) copy-start(bf16[32,2,4096]{2,1,0:T(2,128)(2,1)} %param.7) | copy-start | bytes 1572868
  6.5 138.4 %reduce-scatter.4.cloned.1.call-start = ((), (), s32[]{:S(2)}) async-start(), calls=%async_computation.4 | async-start | bytes 1474560 | tf_op jit(solution)/shard_map/reduce_scatter | solution.py:95
  98.8 17.7 %copy-start.4 = (u32[32]{0:T(128)S(1)}, u32[32]{0:T(128)}, u32[]{:S(2)}) copy-start(u32[32]{0:T(128)} %constant.39) | copy-start | bytes 388
  98.8 18.9 %copy-start.3 = (s32[32]{0:T(128)S(1)}, s32[32]{0:T(128)}, u32[]{:S(2)}) copy-start(s32[32]{0:T(128)} %param.13) | copy-start | bytes 388
  128.5 23.1 %copy-start.2 = (s32[2]{0:T(128)S(1)}, s32[2]{0:T(128)}, u32[]{:S(2)}) copy-start(s32[2]{0:T(128)} %param.12) | copy-start | bytes 28
  147.1 10.8 %all-to-all-start = ((bf16[8,2,2,18,128]{4,2,3,1,0:T(2,128)(2,1)}), bf16[8,2,2,18,128]{4,2,3,1,0:T(2,128)(2,1)S(1)}, u32[]{:S(2)}, u32[]{:S(2)}) async-start(bf16[8,2,2,18,128]{4,2,3,1,0:T(2,128)(2,1)} %copy.63), calls=%async_computation.1 | async-start | bytes 294912 | tf_op jit(solution)/shard_map/all_to_all | solution.py:102
  151.7 64.7 %reduce-scatter.6.cloned.1.call-start = ((), (), s32[]{:S(2)}) async-start(), calls=%async_computation.5 | async-start | bytes 1310720 | tf_op jit(solution)/shard_map/reduce_scatter | solution.py:115
Sparse Core Ops, SparseCore 0:
  116.4 28.4 reduce-scatter.3
  190.5 25.8 reduce-scatter.5
where the time goes:
time: 228 us; the launch traced here: 225 us
  local copies, waits for them, and re-layouts  97 us (43%)
  waiting for transfers between devices  47.6 us (21%)
  matrix products  34.1 us (15%)
  blocking collectives  23.5 us (10%)
  between operations  14.2 us (6%)
  starting transfers between devices  4.59 us (2%)
  other arithmetic  4.22 us (2%)
    unnamed x12, local copies, waits for them, and re-layouts  91.7 us
    reduce_scatter x1, waiting for transfers between devices, body(): own_sum = lax.psum_scatter(terms, 'gy', scatter_dimension=0, tiled=True)  25 us
    dot_general x1, matrix products, body(): jnp.dot(hidden.reshape(total_rows * 2, local_width), qkv_weight.reshape(l...  17.5 us
    reduce_scatter x1, waiting for transfers between devices, body(): lax.psum_scatter(partial_value, 'gx', scatter_dimension=0, tiled=True)  16.3 us
    dot_general x1, matrix products, body(): jnp.dot(row_piece.reshape(piece_rows * 2, -1), out_flat, preferred_elemen...  14.6 us
    all_to_all x1, blocking collectives, body(): lax.all_to_all(attended, 'gy', split_axis=2, concat_axis=0, tiled=True)  8.61 us
    unnamed x1, blocking collectives  8.34 us
    all_gather x1, blocking collectives, body(): row_piece = lax.all_gather(regrouped, 'gx', axis=0, tiled=True)  6.51 us
  transfers between devices with their start and end apart: 3, of which 3 were waited for; matrix products, arithmetic and copies ran while one was open for 2% of the time, Pallas kernels for 0%

commit v1 on v0

--- a/solution.py
+++ b/solution.py
@@ -1,8 +1,11 @@
+import functools
 import math
 
 import jax
 import jax.numpy as jnp
 from jax import lax
+from jax.experimental import pallas as pl
+from jax.experimental.pallas import tpu as pltpu
 from jax.sharding import PartitionSpec as P
 
 D = 16384
@@ -70,35 +73,211 @@
     return attended.astype(jnp.bfloat16)
 
 
+def shift_pairs(count, shift):
+    return [(i, (i + shift) % count) for i in range(count)]
+
+
+def pick_block(features):
+    block = features
+    while block > 1024 and block % 2 == 0:
+        block //= 2
+    return block
+
+
+def project_kernel(axis_size, index_ref, tokens_ref, gain_ref, weight_ref, *rest):
+    outs, (spread_ref, total_ref, square_ref) = rest[:axis_size], rest[axis_size:]
+    step = pl.program_id(0)
+    token_count, block = tokens_ref.shape
+    heads, groups, head_dim = weight_ref.shape[1:]
+    tokens_wide = tokens_ref[...].astype(jnp.float32)
+    hidden = (tokens_wide * gain_ref[...].astype(jnp.float32)).astype(jnp.bfloat16)
+    lanes = 128
+    wide = lanes * groups
+    place = lax.broadcasted_iota(jnp.int32, (lanes, wide * groups), 0)
+    column = lax.broadcasted_iota(jnp.int32, (lanes, wide * groups), 1)
+    group_of = column // wide
+    spread = (column - group_of * wide == place * groups + group_of).astype(jnp.bfloat16)
+    squares = jnp.zeros((token_count, lanes), jnp.float32)
+    for i in range(block // lanes):
+        piece = tokens_wide[:, i * lanes : (i + 1) * lanes]
+        squares = squares + piece * piece
+        out = jnp.dot(
+            hidden[:, i * lanes : (i + 1) * lanes], spread, preferred_element_type=jnp.float32
+        ).astype(jnp.bfloat16)
+        for g in range(groups):
+            spread_ref[g * token_count : (g + 1) * token_count, i * wide : (i + 1) * wide] = out[
+                :, g * wide : (g + 1) * wide
+            ]
+
+    @pl.when(step == 0)
+    def _():
+        square_ref[...] = squares
+
+    @pl.when(step > 0)
+    def _():
+        square_ref[...] += squares
+
+    for pair in range(heads // 2):
+        weights = jnp.concatenate(
+            [weight_ref[:, 2 * pair + i].reshape(block * groups, head_dim) for i in range(2)],
+            axis=1,
+        )
+        term = jnp.dot(spread_ref[...], weights, preferred_element_type=jnp.float32)
+
+        @pl.when(step == 0)
+        def _():
+            total_ref[pair] = term
+
+        @pl.when(step > 0)
+        def _():
+            total_ref[pair] += term
+
+    @pl.when(step == pl.num_programs(0) - 1)
+    def _():
+        rows = token_count // axis_size
+        lane = lax.broadcasted_iota(jnp.int32, (rows, lanes), 1)
+        for shift in range(axis_size):
+            first = lax.rem(index_ref[0] + shift, axis_size) * rows
+            first = pl.multiple_of(first, rows)
+            own = outs[shift]
+            for g in range(groups):
+                for pair in range(heads // 2):
+                    own[g, :, pair * 2 * head_dim : (pair + 1) * 2 * head_dim] = total_ref[
+                        pair, pl.ds(g * token_count + first, rows), :
+                    ].astype(own.dtype)
+                total = jnp.sum(square_ref[pl.ds(first, rows), :], axis=1, keepdims=True)
+                high = total.astype(jnp.bfloat16).astype(jnp.float32)
+                middle = (total - high).astype(jnp.bfloat16).astype(jnp.float32)
+                low = total - high - middle
+                own[g, :, heads * head_dim :] = jnp.where(
+                    lane == 0, high, jnp.where(lane == 1, middle, jnp.where(lane == 2, low, 0.0))
+                ).astype(own.dtype)
+
+
+def project(tokens, norm_gain, qkv_weight, axis_size, index):
+    token_count, features = tokens.shape
+    _, groups, heads, head_dim = qkv_weight.shape
+    block = pick_block(features)
+    rows = token_count // axis_size
+    width = heads * head_dim + 128
+    return pl.pallas_call(
+        functools.partial(project_kernel, axis_size),
+        grid_spec=pltpu.PrefetchScalarGridSpec(
+            num_scalar_prefetch=1,
+            grid=(features // block,),
+            in_specs=[
+                pl.BlockSpec((token_count, block), lambda k, _: (0, k)),
+                pl.BlockSpec((1, block), lambda k, _: (0, k)),
+                pl.BlockSpec((block, heads, groups, head_dim), lambda k, _: (k, 0, 0, 0)),
+            ],
+            out_specs=[pl.BlockSpec((groups, rows, width), lambda k, _: (0, 0, 0))] * axis_size,
+            scratch_shapes=[
+                pltpu.VMEM((groups * token_count, block * groups), jnp.bfloat16),
+                pltpu.VMEM((heads // 2, groups * token_count, 2 * head_dim), jnp.float32),
+                pltpu.VMEM((token_count, 128), jnp.float32),
+            ],
+        ),
+        out_shape=[
+            jax.ShapeDtypeStruct((groups, rows, width), jnp.bfloat16 if s else jnp.float32)
+            for s in range(axis_size)
+        ],
+        compiler_params=pltpu.CompilerParams(vmem_limit_bytes=48 * 2**20),
+        cost_estimate=pl.CostEstimate(
+            flops=2 * qkv_weight.size * token_count,
+            bytes_accessed=qkv_weight.size * 2,
+            transcendentals=0,
+        ),
+        name="project",
+    )(index[None], tokens, norm_gain[None, :], jnp.transpose(qkv_weight, (0, 2, 1, 3)))
+
+
+def outward_kernel(axis_size, index_ref, attended_ref, weight_ref, *rest):
+    outs, total_ref = rest[:axis_size], rest[axis_size]
+    token_count, depth = attended_ref.shape
+    rows = token_count // axis_size
+    block = pick_block(depth)
+    for k in range(depth // block):
+        term = jnp.dot(
+            attended_ref[:, k * block : (k + 1) * block],
+            weight_ref[k * block : (k + 1) * block, :],
+            preferred_element_type=jnp.float32,
+        )
+        if k == 0:
+            total_ref[...] = term
+        else:
+            total_ref[...] += term
+    for shift in range(axis_size):
+        first = pl.multiple_of(lax.rem(index_ref[0] + shift, axis_size) * rows, rows)
+        outs[shift][...] = total_ref[pl.ds(first, rows), :].astype(outs[shift].dtype)
+
+
+def outward(attended, out_flat, axis_size, index):
+    token_count, depth = attended.shape
+    width = out_flat.shape[1]
+    block = pick_block(width)
+    rows = token_count // axis_size
+    return pl.pallas_call(
+        functools.partial(outward_kernel, axis_size),
+        grid_spec=pltpu.PrefetchScalarGridSpec(
+            num_scalar_prefetch=1,
+            grid=(width // block,),
+            in_specs=[
+                pl.BlockSpec((token_count, depth), lambda j, _: (0, 0)),
+                pl.BlockSpec((depth, block), lambda j, _: (0, j)),
+            ],
+            out_specs=[pl.BlockSpec((rows, block), lambda j, _: (0, j))] * axis_size,
+            scratch_shapes=[pltpu.VMEM((token_count, block), jnp.float32)],
+        ),
+        out_shape=[
+            jax.ShapeDtypeStruct((rows, width), jnp.bfloat16 if s else jnp.float32)
+            for s in range(axis_size)
+        ],
+        compiler_params=pltpu.CompilerParams(vmem_limit_bytes=48 * 2**20),
+        cost_estimate=pl.CostEstimate(
+            flops=2 * out_flat.size * token_count,
+            bytes_accessed=out_flat.size * 2,
+            transcendentals=0,
+        ),
+        name="outward",
+    )(index[None], attended, out_flat)
+
+
+def sum_pieces(pieces, axis):
+    count = len(pieces)
+    total = pieces[0]
+    landed = [lax.ppermute(pieces[s], axis, shift_pairs(count, s)) for s in range(1, count)]
+    for piece in landed:
+        total = total + piece.astype(jnp.float32)
+    return total
+
+
 def body(tokens, norm_gain, qkv_weight, out_weight, kv_cache, lengths, positions):
     rows_local = kv_cache.shape[0]
+    width_devices = lax.axis_size("gx")
     head_devices = lax.axis_size("gy")
     width_index = lax.axis_index("gx")
     head_index = lax.axis_index("gy")
     total_rows = tokens.shape[0]
     local_width = tokens.shape[2]
-    groups_local = qkv_weight.shape[1]
-    group_width = qkv_weight.shape[2]
-    head_dim = qkv_weight.shape[3]
+    groups_local, group_width, head_dim = qkv_weight.shape[1:]
     group_size = group_width - 2
-    tokens_wide = tokens.astype(jnp.float32)
-    hidden = (tokens_wide * norm_gain.astype(jnp.float32)).astype(jnp.bfloat16)
-    squares = jnp.sum(tokens_wide * tokens_wide, axis=-1)
     block_rows = rows_local * head_devices
-    partial_value = jnp.dot(
-        hidden.reshape(total_rows * 2, local_width),
-        qkv_weight.reshape(local_width, -1),
-        preferred_element_type=jnp.float32,
-    )
-    partial_value = partial_value.reshape(total_rows, 2, groups_local, group_width, head_dim)
-    block_sum, block_squares = (
-        lax.psum_scatter(partial_value, "gx", scatter_dimension=0, tiled=True),
-        lax.psum_scatter(squares, "gx", scatter_dimension=0, tiled=True),
-    )
+    pieces = project(
+        tokens.reshape(total_rows * 2, local_width),
+        norm_gain,
+        qkv_weight,
+        width_devices,
+        width_index,
+    )
+    block_sum = sum_pieces(pieces, "gx")
+    flat = group_width * head_dim
+    block_squares = jnp.sum(block_sum[0, :, flat : flat + 3], axis=-1)
     inv_rms = lax.rsqrt(block_squares / D + norm_eps)
-    ready = finish(
-        block_sum * inv_rms[:, :, None, None, None], positions, width_index * block_rows, block_rows
-    )
+    projected = (block_sum[:, :, :flat] * inv_rms[None, :, None]).reshape(
+        groups_local, block_rows, 2, group_width, head_dim
+    )
+    projected = jnp.transpose(projected, (1, 2, 0, 3, 4))
+    ready = finish(projected, positions, width_index * block_rows, block_rows)
     packed = lax.all_to_all(ready, "gy", split_axis=0, concat_axis=2, tiled=True)
     queries = packed[:, :, :, :group_size]
     key_new = packed[:, :, :, group_size]
@@ -108,12 +287,9 @@
     out_flat = out_weight.reshape(-1, local_width)
     row_piece = lax.all_gather(regrouped, "gx", axis=0, tiled=True)
     piece_rows = row_piece.shape[0]
-    product = jnp.dot(
-        row_piece.reshape(piece_rows * 2, -1), out_flat, preferred_element_type=jnp.float32
-    )
-    terms = product.reshape(piece_rows, 2, local_width)
-    own_sum = lax.psum_scatter(terms, "gy", scatter_dimension=0, tiled=True)
+    parts = outward(row_piece.reshape(piece_rows * 2, -1), out_flat, head_devices, head_index)
     row_share = total_rows // head_devices
+    own_sum = sum_pieces(parts, "gy").reshape(row_share, 2, local_width)
     residual = lax.dynamic_slice_in_dim(tokens, head_index * row_share, row_share, 0).astype(
         jnp.float32
     )

time: 228 us -> 99.9 us (0.44)
  local copies, waits for them, and re-layouts: 97 us -> 7.54 us
  Pallas kernels: 0 us -> 38.5 us
  matrix products: 34.1 us -> 1.98 us
  waiting for transfers between devices: 47.6 us -> 24.4 us
  blocking collectives: 23.5 us -> 6.65 us
  between operations: 14.2 us -> 0.2 us
  starting transfers between devices: 4.59 us -> 16.6 us
    unnamed x12 -> x6, local copies, waits for them, and re-layouts: 91.7 us -> 0.29 us
    reduce_scatter x2 -> x0, waiting for transfers between devices: 41.4 us -> none  [the longest x1 25 us: body(): own_sum = lax.psum_scatter(terms, 'gy', scatter_dimension=0, tiled=True)]
    pallas_call x0 -> x2, Pallas kernels: none -> 38.5 us  [the longest x1 25.8 us: project(): pl.pallas_call(functools.partial(project_kernel, axis_size), grid_spec=pl...]
    dot_general x2 -> x0, matrix products: 32.1 us -> none  [the longest x1 17.5 us: body(): jnp.dot(hidden.reshape(total_rows * 2, local_width), qkv_weight.reshape(l...]
    ppermute x0 -> x6, waiting for transfers between devices: none -> 11.6 us  [sum_pieces(): lax.ppermute(pieces[s], axis, shift_pairs(count, s))]
    all_to_all x1 -> x0, blocking collectives: 8.61 us -> none  [body(): lax.all_to_all(attended, 'gy', split_axis=2, concat_axis=0, tiled=True)]
    ppermute x0 -> x6, starting transfers between devices: none -> 8.36 us  [sum_pieces(): lax.ppermute(pieces[s], axis, shift_pairs(count, s))]
    unnamed x1 -> x0, blocking collectives: 8.34 us -> none
  transfers between devices with their start and end apart: 3 -> 8, of which waited for: 3 -> 5; matrix products, arithmetic and copies ran while one was open for 2% -> 4% of each run, Pallas kernels for 0% -> 0%
where the time goes in v1:
time: 99.9 us; the launch traced here: 99.1 us
  Pallas kernels  38.5 us (39%)
  waiting for transfers between devices  24.4 us (24%)
  starting transfers between devices  16.6 us (17%)
  local copies, waits for them, and re-layouts  7.54 us (8%)
  blocking collectives  6.65 us (7%)
  other arithmetic  3.28 us (3%)
  matrix products  1.98 us (2%)
    pallas_call x1, Pallas kernels, project(): pl.pallas_call(functools.partial(project_kernel, axis_size), grid_spec=pl...  25.8 us
    pallas_call x1, Pallas kernels, outward(): pl.pallas_call(functools.partial(outward_kernel, axis_size), grid_spec=pl...  12.6 us
    ppermute x6, waiting for transfers between devices, sum_pieces(): lax.ppermute(pieces[s], axis, shift_pairs(count, s))  11.6 us
    ppermute x6, starting transfers between devices, sum_pieces(): lax.ppermute(pieces[s], axis, shift_pairs(count, s))  8.36 us
    all_to_all x1, waiting for transfers between devices, body(): lax.all_to_all(ready, 'gy', split_axis=0, concat_axis=2, tiled=True)  6.77 us
    all_gather x1, blocking collectives, body(): row_piece = lax.all_gather(regrouped, 'gx', axis=0, tiled=True)  6.65 us
    all_to_all x1, waiting for transfers between devices, body(): lax.all_to_all(attended, 'gy', split_axis=2, concat_axis=0, tiled=True)  6.04 us
    all_to_all x1, starting transfers between devices, body(): lax.all_to_all(ready, 'gy', split_axis=0, concat_axis=2, tiled=True)  4.87 us
  transfers between devices with their start and end apart: 8, of which 5 were waited for; matrix products, arithmetic and copies ran while one was open for 4% of the time, Pallas kernels for 0%

profile of v1, /device:TPU:0, one launch (start us, length us, event | category | flops | bytes accessed | tf_op | source)
XLA Modules:
  0.0 99.1 jit_solution(1822973862972205846)
XLA Ops:
  0.0 1.2 %reshape.97.tokens_ref = bf16[64,4096]{1,0:T(8,128)(2,1)S(1)} reshape(bf16[32,2,4096]{2,1,0:T(2,128)(2,1)} %param.7) | data formatting | bytes 1048576 | tf_op jit(solution)/shard_map/reshape | solution.py:266
  1.2 0.7 broadcast_in_dim.33.gain_ref
  2.0 25.8 %project.1 = (f32[2,16,2432]{2,1,0:T(8,128)S(1)}, bf16[2,16,2432]{2,1,0:T(8,128)(2,1)S(1)}, bf16[2,16,2432]{2,1,0:T(8,128)(2,1)S(1)}, bf16[2,16,2432]{2,1,0:T(8,128)(2,1)S(1)}) custom-call(s32[1]{0:T(128)} %bitcast.1.index_ref, bf16[64,4096]{1,0:T(8,128)(2,1)S(1)} %reshape.97.tokens_ref, bf16[1,4096]{1,0:T(2,128)(2,1)S(1)} %broadcast_in_dim.33.gain_ref, ...), custom_call_target="tpu_custom_call" | custom-call | flops 2415919104 | bytes 37748736 | tf_op jit(solution)/shard_map/project/pallas_call | solution.py:163
  27.8 0.5 collective-permute-start
  28.3 2.6 %collective-permute-start.1 = (bf16[2,16,2432]{2,1,0:T(8,128)(2,1)S(1)}, bf16[2,16,2432]{2,1,0:T(8,128)(2,1)S(1)}, u32[]{:S(2)}, u32[]{:S(2)}) collective-permute-start(bf16[2,16,2432]{2,1,0:T(8,128)(2,1)S(1)} %get-tuple-element.15), channel_id=1, source_target_pairs={{0,8},{4,12},{8,0},{12,4},{1,9},{5,13},{9,1},{13,5},{2,10},{6,14},... | collective-permute-start | bytes 466952 | tf_op jit(solution)/shard_map/ppermute | solution.py:248
  30.9 1.4 %collective-permute-start.2 = (bf16[2,16,2432]{2,1,0:T(8,128)(2,1)S(1)}, bf16[2,16,2432]{2,1,0:T(8,128)(2,1)S(1)}, u32[]{:S(2)}, u32[]{:S(2)}) collective-permute-start(bf16[2,16,2432]{2,1,0:T(8,128)(2,1)S(1)} %get-tuple-element.16), channel_id=1, source_target_pairs={{0,12},{4,0},{8,4},{12,8},{1,13},{5,1},{9,5},{13,9},{2,14},{6,2},{... | collective-permute-start | bytes 466952 | tf_op jit(solution)/shard_map/ppermute | solution.py:248
  32.5 3.2 %fusion.20 = (bf16[2,384,1,8,128]{4,3,2,1,0:T(8,128)(2,1)}, bf16[2,384,1,8,128]{4,3,2,1,0:T(8,128)(2,1)S(1)}) fusion(bf16[2,384,2,8,128]{4,3,2,1,0:T(8,128)(2,1)} %param.11), kind=kLoop, calls=%fused_computation.48 | loop fusion | bytes 6291456 | tf_op jit(solution)/shard_map/slice | solution.py:68
  35.7 0.2 multiply_cosine_fusion
  35.9 2.1 %collective-permute-done.2 = bf16[2,16,2432]{2,1,0:T(8,128)(2,1)S(1)} collective-permute-done((bf16[2,16,2432]{2,1,0:T(8,128)(2,1)S(1)}, bf16[2,16,2432]{2,1,0:T(8,128)(2,1)S(1)}, u32[]{:S(2)}, u32[]{:S(2)}) %collective-permute-start.2) | collective-permute-done | bytes 155680 | tf_op jit(solution)/shard_map/ppermute | solution.py:248
  38.4 0.2 subtract_convert_fusion
  38.8 0.8 copy.20
  39.6 4.9 %all-to-all-start = ((bf16[8,2,2,18,128]{4,2,3,1,0:T(2,128)(2,1)}), bf16[8,2,2,18,128]{4,2,3,1,0:T(2,128)(2,1)S(1)}, u32[]{:S(2)}, u32[]{:S(2)}) async-start(bf16[8,2,2,18,128]{4,2,3,1,0:T(2,128)(2,1)} %copy.20), calls=%async_computation | async-start | bytes 294912 | tf_op jit(solution)/shard_map/all_to_all | solution.py:281
  44.6 6.8 %all-to-all-done = bf16[8,2,2,18,128]{4,2,3,1,0:T(2,128)(2,1)S(1)} async-done(((bf16[8,2,2,18,128]{4,2,3,1,0:T(2,128)(2,1)}), bf16[8,2,2,18,128]{4,2,3,1,0:T(2,128)(2,1)S(1)}, u32[]{:S(2)}, u32[]{:S(2)}) %all-to-all-start) | async-done | bytes 147488 | tf_op jit(solution)/shard_map/all_to_all | solution.py:281
  51.4 0.8 fusion.22
  52.2 0.4 fusion.23
  52.8 0.3 fusion.10
  53.1 0.2 convolution_bitcast_fusion
  53.3 0.3 copy-done
  53.6 0.5 fusion.7
  54.2 0.7 copy.28
  54.8 3.3 %all-to-all-start.1 = ((bf16[2,2,8,16,128]{4,3,1,0,2:T(8,128)(2,1)}), bf16[2,2,8,16,128]{4,3,1,0,2:T(8,128)(2,1)S(1)}, u32[]{:S(2)}, u32[]{:S(2)}) async-start(bf16[2,2,8,16,128]{4,3,1,0,2:T(8,128)(2,1)} %copy.28), calls=%async_computation.1 | async-start | bytes 262144 | tf_op jit(solution)/shard_map/all_to_all | solution.py:286
  58.2 6.0 %all-to-all-done.1 = bf16[2,2,8,16,128]{4,3,1,0,2:T(8,128)(2,1)S(1)} async-done(((bf16[2,2,8,16,128]{4,3,1,0,2:T(8,128)(2,1)}), bf16[2,2,8,16,128]{4,3,1,0,2:T(8,128)(2,1)S(1)}, u32[]{:S(2)}, u32[]{:S(2)}) %all-to-all-start.1) | async-done | bytes 131104 | tf_op jit(solution)/shard_map/all_to_all | solution.py:286
  64.2 6.6 %all_gather.3 = bf16[32,2,2,16,128]{4,3,2,1,0:T(8,128)(2,1)S(1)} all-gather(bf16[8,2,2,16,128]{4,3,2,1,0:T(8,128)(2,1)S(1)} %bitcast.72), channel_id=1, replica_groups=mesh['groups'=2,'gx'=4,'gy'=4] {'gx'}, dimensions={0}, use_global_device_ids=true | all-gather | bytes 655360 | tf_op jit(solution)/shard_map/all_gather | solution.py:288
  70.9 0.2 reshape.99.attended_ref
  71.1 12.6 %outward.1 = (f32[16,4096]{1,0:T(8,128)S(1)}, bf16[16,4096]{1,0:T(8,128)(2,1)S(1)}, bf16[16,4096]{1,0:T(8,128)(2,1)S(1)}, bf16[16,4096]{1,0:T(8,128)(2,1)S(1)}) custom-call(s32[1]{0:T(128)} %bitcast.index_ref, bf16[64,4096]{1,0:T(8,128)(2,1)S(1)} %reshape.99.attended_ref, bf16[4096,4096]{1,0:T(8,128)(2,1)} %bitcast.64), custom_call_target="tpu_custom_call" | custom-call | flops 2147483648 | bytes 33554432 | tf_op jit(solution)/shard_map/outward/pallas_call | solution.py:219
  83.7 1.2 %collective-permute-start.3 = (bf16[16,4096]{1,0:T(8,128)(2,1)S(1)}, bf16[16,4096]{1,0:T(8,128)(2,1)S(1)}, u32[]{:S(2)}, u32[]{:S(2)}) collective-permute-start(bf16[16,4096]{1,0:T(8,128)(2,1)S(1)} %get-tuple-element.18), channel_id=1, source_target_pairs={{0,1},{1,2},{2,3},{3,0},{4,5},{5,6},{6,7},{7,4},{8,9},{9,10},{10,1... | collective-permute-start | bytes 393224 | tf_op jit(solution)/shard_map/ppermute | solution.py:248
  84.9 1.3 %collective-permute-start.4 = (bf16[16,4096]{1,0:T(8,128)(2,1)S(1)}, bf16[16,4096]{1,0:T(8,128)(2,1)S(1)}, u32[]{:S(2)}, u32[]{:S(2)}) collective-permute-start(bf16[16,4096]{1,0:T(8,128)(2,1)S(1)} %get-tuple-element.19), channel_id=1, source_target_pairs={{0,2},{1,3},{2,0},{3,1},{4,6},{5,7},{6,4},{7,5},{8,10},{9,11},{10,... | collective-permute-start | bytes 393224 | tf_op jit(solution)/shard_map/ppermute | solution.py:248
  86.2 1.4 %collective-permute-start.5 = (bf16[16,4096]{1,0:T(8,128)(2,1)S(1)}, bf16[16,4096]{1,0:T(8,128)(2,1)S(1)}, u32[]{:S(2)}, u32[]{:S(2)}) collective-permute-start(bf16[16,4096]{1,0:T(8,128)(2,1)S(1)} %get-tuple-element.20), channel_id=1, source_target_pairs={{0,3},{1,0},{2,1},{3,2},{4,7},{5,4},{6,5},{7,6},{8,11},{9,8},{10,9... | collective-permute-start | bytes 393224 | tf_op jit(solution)/shard_map/ppermute | solution.py:248
  87.6 4.4 %collective-permute-done.3 = bf16[16,4096]{1,0:T(8,128)(2,1)S(1)} collective-permute-done((bf16[16,4096]{1,0:T(8,128)(2,1)S(1)}, bf16[16,4096]{1,0:T(8,128)(2,1)S(1)}, u32[]{:S(2)}, u32[]{:S(2)}) %collective-permute-start.3) | collective-permute-done | bytes 131104 | tf_op jit(solution)/shard_map/ppermute | solution.py:248
  92.0 5.0 %collective-permute-done.4 = bf16[16,4096]{1,0:T(8,128)(2,1)S(1)} collective-permute-done((bf16[16,4096]{1,0:T(8,128)(2,1)S(1)}, bf16[16,4096]{1,0:T(8,128)(2,1)S(1)}, u32[]{:S(2)}, u32[]{:S(2)}) %collective-permute-start.4) | collective-permute-done | bytes 131104 | tf_op jit(solution)/shard_map/ppermute | solution.py:248
  97.2 0.2 reshape.101
  97.3 1.8 %convert_add_fusion.2 = f32[8,2,4096]{2,1,0:T(2,128)} fusion(f32[8,2,4096]{2,1,0:T(2,128)S(1)} %reshape.101, bf16[32,2,4096]{2,1,0:T(2,128)(2,1)} %param.7, s32[]{:T(128)S(6)} %select_n.17), kind=kLoop, calls=%fused_computation.24 | loop fusion | flops 131072 | bytes 655364 | tf_op jit(solution)/shard_map/add | solution.py:296
  (29 shorter events, 1.1 us)
Async XLA Ops:
  2.0 30.4 %copy-start.2 = (s32[32]{0:T(128)S(1)}, s32[32]{0:T(128)}, u32[]{:S(2)}) copy-start(s32[32]{0:T(128)} %param.13) | copy-start | bytes 388
  27.8 8.1 %collective-permute-start = (bf16[2,16,2432]{2,1,0:T(8,128)(2,1)S(1)}, bf16[2,16,2432]{2,1,0:T(8,128)(2,1)S(1)}, u32[]{:S(2)}, u32[]{:S(2)}) collective-permute-start(bf16[2,16,2432]{2,1,0:T(8,128)(2,1)S(1)} %get-tuple-element.14), channel_id=1, source_target_pairs={{0,4},{4,8},{8,12},{12,0},{1,5},{5,9},{9,13},{13,1},{2,6},{6,10},{... | collective-permute-start | bytes 466952 | tf_op jit(solution)/shard_map/ppermute | solution.py:248
  28.3 7.6 %collective-permute-start.1 = (bf16[2,16,2432]{2,1,0:T(8,128)(2,1)S(1)}, bf16[2,16,2432]{2,1,0:T(8,128)(2,1)S(1)}, u32[]{:S(2)}, u32[]{:S(2)}) collective-permute-start(bf16[2,16,2432]{2,1,0:T(8,128)(2,1)S(1)} %get-tuple-element.15), channel_id=1, source_target_pairs={{0,8},{4,12},{8,0},{12,4},{1,9},{5,13},{9,1},{13,5},{2,10},{6,14},... | collective-permute-start | bytes 466952 | tf_op jit(solution)/shard_map/ppermute | solution.py:248
  30.9 7.1 %collective-permute-start.2 = (bf16[2,16,2432]{2,1,0:T(8,128)(2,1)S(1)}, bf16[2,16,2432]{2,1,0:T(8,128)(2,1)S(1)}, u32[]{:S(2)}, u32[]{:S(2)}) collective-permute-start(bf16[2,16,2432]{2,1,0:T(8,128)(2,1)S(1)} %get-tuple-element.16), channel_id=1, source_target_pairs={{0,12},{4,0},{8,4},{12,8},{1,13},{5,1},{9,5},{13,9},{2,14},{6,2},{... | collective-permute-start | bytes 466952 | tf_op jit(solution)/shard_map/ppermute | solution.py:248
  38.2 6.3 %copy-start.1 = (s32[2]{0:T(128)S(1)}, s32[2]{0:T(128)}, u32[]{:S(2)}) copy-start(s32[2]{0:T(128)} %param.12) | copy-start | bytes 28
  39.6 11.7 %all-to-all-start = ((bf16[8,2,2,18,128]{4,2,3,1,0:T(2,128)(2,1)}), bf16[8,2,2,18,128]{4,2,3,1,0:T(2,128)(2,1)S(1)}, u32[]{:S(2)}, u32[]{:S(2)}) async-start(bf16[8,2,2,18,128]{4,2,3,1,0:T(2,128)(2,1)} %copy.20), calls=%async_computation | async-start | bytes 294912 | tf_op jit(solution)/shard_map/all_to_all | solution.py:281
  52.2 1.4 %copy-start = (bf16[2,384,1,8,128]{4,3,2,1,0:T(8,128)(2,1)S(1)}, bf16[2,384,1,8,128]{4,3,2,1,0:T(8,128)(2,1)}, u32[]{:S(2)}) copy-start(bf16[2,384,1,8,128]{4,3,2,1,0:T(8,128)(2,1)} %get-tuple-element.21) | copy-start | bytes 4718596
  54.8 9.4 %all-to-all-start.1 = ((bf16[2,2,8,16,128]{4,3,1,0,2:T(8,128)(2,1)}), bf16[2,2,8,16,128]{4,3,1,0,2:T(8,128)(2,1)S(1)}, u32[]{:S(2)}, u32[]{:S(2)}) async-start(bf16[2,2,8,16,128]{4,3,1,0,2:T(8,128)(2,1)} %copy.28), calls=%async_computation.1 | async-start | bytes 262144 | tf_op jit(solution)/shard_map/all_to_all | solution.py:286
  83.7 8.3 %collective-permute-start.3 = (bf16[16,4096]{1,0:T(8,128)(2,1)S(1)}, bf16[16,4096]{1,0:T(8,128)(2,1)S(1)}, u32[]{:S(2)}, u32[]{:S(2)}) collective-permute-start(bf16[16,4096]{1,0:T(8,128)(2,1)S(1)} %get-tuple-element.18), channel_id=1, source_target_pairs={{0,1},{1,2},{2,3},{3,0},{4,5},{5,6},{6,7},{7,4},{8,9},{9,10},{10,1... | collective-permute-start | bytes 393224 | tf_op jit(solution)/shard_map/ppermute | solution.py:248
  84.9 12.2 %collective-permute-start.4 = (bf16[16,4096]{1,0:T(8,128)(2,1)S(1)}, bf16[16,4096]{1,0:T(8,128)(2,1)S(1)}, u32[]{:S(2)}, u32[]{:S(2)}) collective-permute-start(bf16[16,4096]{1,0:T(8,128)(2,1)S(1)} %get-tuple-element.19), channel_id=1, source_target_pairs={{0,2},{1,3},{2,0},{3,1},{4,6},{5,7},{6,4},{7,5},{8,10},{9,11},{10,... | collective-permute-start | bytes 393224 | tf_op jit(solution)/shard_map/ppermute | solution.py:248
  86.2 10.9 %collective-permute-start.5 = (bf16[16,4096]{1,0:T(8,128)(2,1)S(1)}, bf16[16,4096]{1,0:T(8,128)(2,1)S(1)}, u32[]{:S(2)}, u32[]{:S(2)}) collective-permute-start(bf16[16,4096]{1,0:T(8,128)(2,1)S(1)} %get-tuple-element.20), channel_id=1, source_target_pairs={{0,3},{1,0},{2,1},{3,2},{4,7},{5,4},{6,5},{7,6},{8,11},{9,8},{10,9... | collective-permute-start | bytes 393224 | tf_op jit(solution)/shard_map/ppermute | solution.py:248

commit v2 on v1

--- a/solution.py
+++ b/solution.py
@@ -13,6 +13,8 @@
 
 norm_eps = 1e-05
 rope_base = 500000.0
+PROJECT_BLOCK = 512
+PROJECT_SLOTS = 3
 
 
 def rotate(values, places):
@@ -84,99 +86,124 @@
     return block
 
 
-def project_kernel(axis_size, index_ref, tokens_ref, gain_ref, weight_ref, *rest):
-    outs, (spread_ref, total_ref, square_ref) = rest[:axis_size], rest[axis_size:]
-    step = pl.program_id(0)
-    token_count, block = tokens_ref.shape
-    heads, groups, head_dim = weight_ref.shape[1:]
-    tokens_wide = tokens_ref[...].astype(jnp.float32)
-    hidden = (tokens_wide * gain_ref[...].astype(jnp.float32)).astype(jnp.bfloat16)
+def split_squares(total, lanes):
+    high = total.astype(jnp.bfloat16).astype(jnp.float32)
+    middle = (total - high).astype(jnp.bfloat16).astype(jnp.float32)
+    low = total - high - middle
+    lane = lax.broadcasted_iota(jnp.int32, (total.shape[0], lanes), 1)
+    return jnp.where(
+        lane == 0, high, jnp.where(lane == 1, middle, jnp.where(lane == 2, low, 0.0))
+    )
+
+
+def project_kernel(axis_size, block, slots, index_ref, tokens_ref, gain_ref, weight_ref, *rest):
+    outs, rest = rest[:axis_size], rest[axis_size:]
+    hidden_ref, spread_ref, total_ref, sum_ref, gain_wide, buffer, arrived = rest
+    total_rows, pair_rows, features = tokens_ref.shape
+    token_count = total_rows * pair_rows
+    pairs, mix, head_dim = weight_ref.shape[1:]
+    groups = mix // 2
+    steps = features // block
     lanes = 128
-    wide = lanes * groups
-    place = lax.broadcasted_iota(jnp.int32, (lanes, wide * groups), 0)
-    column = lax.broadcasted_iota(jnp.int32, (lanes, wide * groups), 1)
-    group_of = column // wide
-    spread = (column - group_of * wide == place * groups + group_of).astype(jnp.bfloat16)
+
+    def fetch(step, slot):
+        return pltpu.make_async_copy(
+            weight_ref.at[pl.ds(step * block, block)], buffer.at[slot], arrived.at[slot]
+        )
+
+    for step in range(min(slots, steps)):
+        fetch(step, step).start()
+
+    wide = lanes * mix
+    place = lax.broadcasted_iota(jnp.int32, (lanes, wide), 0)
+    column = lax.broadcasted_iota(jnp.int32, (lanes, wide), 1)
+    repeat = (column // mix == place).astype(jnp.bfloat16)
+    member_of = lax.rem(lax.broadcasted_iota(jnp.int32, (token_count, wide), 1), mix)
+    members = [(member_of == m).astype(jnp.bfloat16) for m in range(mix)]
+    gain_wide[...] = gain_ref[...].astype(jnp.float32)
     squares = jnp.zeros((token_count, lanes), jnp.float32)
-    for i in range(block // lanes):
-        piece = tokens_wide[:, i * lanes : (i + 1) * lanes]
-        squares = squares + piece * piece
-        out = jnp.dot(
-            hidden[:, i * lanes : (i + 1) * lanes], spread, preferred_element_type=jnp.float32
-        ).astype(jnp.bfloat16)
+    group = 4
+    for i in range(0, features // lanes, group):
+        for j in range(group):
+            at = (i + j) * lanes
+            piece = tokens_ref[:, :, at : at + lanes].reshape(token_count, lanes)
+            piece = piece.astype(jnp.float32)
+            squares = squares + piece * piece
+            hidden_ref[j * token_count : (j + 1) * token_count, :] = (
+                piece * gain_wide[i + j : i + j + 1, :]
+            ).astype(jnp.bfloat16)
+        repeated = jnp.dot(hidden_ref[...], repeat, preferred_element_type=jnp.float32)
+        repeated = repeated.astype(jnp.bfloat16)
+        for j in range(group):
+            for m in range(mix):
+                spread_ref[
+                    m * token_count : (m + 1) * token_count, (i + j) * wide : (i + j + 1) * wide
+                ] = repeated[j * token_count : (j + 1) * token_count, :] * members[m]
+    total_ref[...] = jnp.zeros_like(total_ref)
+
+    @pl.loop(0, steps)
+    def _(step):
+        slot = lax.rem(step, slots)
+        fetch(step, slot).wait()
+        left = spread_ref.at[:, pl.ds(pl.multiple_of(step * block * mix, 128), block * mix)]
+        for first in range(0, pairs, 4):
+            count = min(4, pairs - first)
+            weights = [
+                buffer[slot, :, first + i].reshape(block * mix, head_dim) for i in range(count)
+            ]
+            weights = jnp.concatenate(weights, axis=1) if count > 1 else weights[0]
+            total_ref[:, first * head_dim : (first + count) * head_dim] += jnp.dot(
+                left[...], weights, preferred_element_type=jnp.float32
+            )
+
+        @pl.when(step + slots < steps)
+        def _():
+            fetch(step + slots, slot).start()
+
+    rows = token_count // axis_size
+    sum_ref[...] = split_squares(jnp.sum(squares, axis=1, keepdims=True), lanes)
+    for shift in range(axis_size):
+        owner = lax.rem(index_ref[0] + shift, axis_size)
+        first = pl.multiple_of(owner * rows, rows)
+        own = outs[shift]
         for g in range(groups):
-            spread_ref[g * token_count : (g + 1) * token_count, i * wide : (i + 1) * wide] = out[
-                :, g * wide : (g + 1) * wide
-            ]
-
-    @pl.when(step == 0)
-    def _():
-        square_ref[...] = squares
-
-    @pl.when(step > 0)
-    def _():
-        square_ref[...] += squares
-
-    for pair in range(heads // 2):
-        weights = jnp.concatenate(
-            [weight_ref[:, 2 * pair + i].reshape(block * groups, head_dim) for i in range(2)],
-            axis=1,
-        )
-        term = jnp.dot(spread_ref[...], weights, preferred_element_type=jnp.float32)
-
-        @pl.when(step == 0)
-        def _():
-            total_ref[pair] = term
-
-        @pl.when(step > 0)
-        def _():
-            total_ref[pair] += term
-
-    @pl.when(step == pl.num_programs(0) - 1)
-    def _():
-        rows = token_count // axis_size
-        lane = lax.broadcasted_iota(jnp.int32, (rows, lanes), 1)
-        for shift in range(axis_size):
-            first = lax.rem(index_ref[0] + shift, axis_size) * rows
-            first = pl.multiple_of(first, rows)
-            own = outs[shift]
-            for g in range(groups):
-                for pair in range(heads // 2):
-                    own[g, :, pair * 2 * head_dim : (pair + 1) * 2 * head_dim] = total_ref[
-                        pair, pl.ds(g * token_count + first, rows), :
-                    ].astype(own.dtype)
-                total = jnp.sum(square_ref[pl.ds(first, rows), :], axis=1, keepdims=True)
-                high = total.astype(jnp.bfloat16).astype(jnp.float32)
-                middle = (total - high).astype(jnp.bfloat16).astype(jnp.float32)
-                low = total - high - middle
-                own[g, :, heads * head_dim :] = jnp.where(
-                    lane == 0, high, jnp.where(lane == 1, middle, jnp.where(lane == 2, low, 0.0))
-                ).astype(own.dtype)
+            for head in range(2 * pairs):
+                start = ((head % 2) * groups + g) * token_count
+                lane = (head // 2) * head_dim
+                own[g, :, head * head_dim : (head + 1) * head_dim] = total_ref[
+                    pl.ds(start + first, rows), lane : lane + head_dim
+                ].astype(own.dtype)
+            own[g, :, 2 * pairs * head_dim :] = sum_ref[pl.ds(first, rows), :].astype(own.dtype)
 
 
 def project(tokens, norm_gain, qkv_weight, axis_size, index):
-    token_count, features = tokens.shape
-    _, groups, heads, head_dim = qkv_weight.shape
-    block = pick_block(features)
+    features, groups, heads, head_dim = qkv_weight.shape
+    token_count = tokens.shape[0] * tokens.shape[1]
+    mix = 2 * groups
+    pairs = heads // 2
+    block = min(features, PROJECT_BLOCK)
+    slots = PROJECT_SLOTS
     rows = token_count // axis_size
     width = heads * head_dim + 128
+    weight = jnp.transpose(qkv_weight, (0, 2, 1, 3)).reshape(features, pairs, mix, head_dim)
     return pl.pallas_call(
-        functools.partial(project_kernel, axis_size),
-        grid_spec=pltpu.PrefetchScalarGridSpec(
-            num_scalar_prefetch=1,
-            grid=(features // block,),
-            in_specs=[
-                pl.BlockSpec((token_count, block), lambda k, _: (0, k)),
-                pl.BlockSpec((1, block), lambda k, _: (0, k)),
-                pl.BlockSpec((block, heads, groups, head_dim), lambda k, _: (k, 0, 0, 0)),
-            ],
-            out_specs=[pl.BlockSpec((groups, rows, width), lambda k, _: (0, 0, 0))] * axis_size,
-            scratch_shapes=[
-                pltpu.VMEM((groups * token_count, block * groups), jnp.bfloat16),
-                pltpu.VMEM((heads // 2, groups * token_count, 2 * head_dim), jnp.float32),
-                pltpu.VMEM((token_count, 128), jnp.float32),
-            ],
-        ),
+        functools.partial(project_kernel, axis_size, block, slots),
+        in_specs=[
+            pl.BlockSpec(memory_space=pltpu.SMEM),
+            pl.BlockSpec(memory_space=pltpu.VMEM),
+            pl.BlockSpec(memory_space=pltpu.VMEM),
+            pl.BlockSpec(memory_space=pl.ANY),
+        ],
+        out_specs=[pl.BlockSpec(memory_space=pltpu.VMEM)] * axis_size,
+        scratch_shapes=[
+            pltpu.VMEM((4 * token_count, 128), jnp.bfloat16),
+            pltpu.VMEM((mix * token_count, features * mix), jnp.bfloat16),
+            pltpu.VMEM((mix * token_count, pairs * head_dim), jnp.float32),
+            pltpu.VMEM((token_count, 128), jnp.float32),
+            pltpu.VMEM((features // 128, 128), jnp.float32),
+            pltpu.VMEM((slots, block, pairs, mix, head_dim), jnp.bfloat16),
+            pltpu.SemaphoreType.DMA((slots,)),
+        ],
         out_shape=[
             jax.ShapeDtypeStruct((groups, rows, width), jnp.bfloat16 if s else jnp.float32)
             for s in range(axis_size)
@@ -188,7 +215,7 @@
             transcendentals=0,
         ),
         name="project",
-    )(index[None], tokens, norm_gain[None, :], jnp.transpose(qkv_weight, (0, 2, 1, 3)))
+    )(index[None], tokens, norm_gain.reshape(-1, 128), weight)
 
 
 def outward_kernel(axis_size, index_ref, attended_ref, weight_ref, *rest):
@@ -263,7 +290,7 @@
     group_size = group_width - 2
     block_rows = rows_local * head_devices
     pieces = project(
-        tokens.reshape(total_rows * 2, local_width),
+        tokens,
         norm_gain,
         qkv_weight,
         width_devices,

time: 99.9 us -> 90 us (0.901)
  Pallas kernels: 38.5 us -> 28.8 us
    pallas_call x1, Pallas kernels: 25.8 us -> 16.2 us  [project(): pl.pallas_call(functools.partial(project_kernel, axis_size, block, slots)...]
    unnamed x6 -> x10, local copies, waits for them, and re-layouts: 0.29 us -> 2.02 us
    reshape x1 -> x0, local copies, waits for them, and re-layouts: 1.24 us -> none  [body(): tokens.reshape(total_rows * 2, local_width)]
where the time goes in v2:
time: 90 us; the launch traced here: 89.2 us
  Pallas kernels  28.8 us (32%)
  waiting for transfers between devices  24.4 us (27%)
  starting transfers between devices  16.6 us (18%)
  local copies, waits for them, and re-layouts  7.33 us (8%)
  blocking collectives  6.65 us (7%)
  other arithmetic  3.28 us (4%)
  matrix products  1.98 us (2%)
    pallas_call x1, Pallas kernels, project(): pl.pallas_call(functools.partial(project_kernel, axis_size, block, slots)...  16.2 us
    pallas_call x1, Pallas kernels, outward(): pl.pallas_call(functools.partial(outward_kernel, axis_size), grid_spec=pl...  12.6 us
    ppermute x6, waiting for transfers between devices, sum_pieces(): lax.ppermute(pieces[s], axis, shift_pairs(count, s))  11.6 us
    ppermute x6, starting transfers between devices, sum_pieces(): lax.ppermute(pieces[s], axis, shift_pairs(count, s))  8.36 us
    all_to_all x1, waiting for transfers between devices, body(): lax.all_to_all(ready, 'gy', split_axis=0, concat_axis=2, tiled=True)  6.78 us
    all_gather x1, blocking collectives, body(): row_piece = lax.all_gather(regrouped, 'gx', axis=0, tiled=True)  6.65 us
    all_to_all x1, waiting for transfers between devices, body(): lax.all_to_all(attended, 'gy', split_axis=2, concat_axis=0, tiled=True)  6.04 us
    all_to_all x1, starting transfers between devices, body(): lax.all_to_all(ready, 'gy', split_axis=0, concat_axis=2, tiled=True)  4.89 us
  transfers between devices with their start and end apart: 8, of which 5 were waited for; matrix products, arithmetic and copies ran while one was open for 4% of the time, Pallas kernels for 0%

profile of v2, /device:TPU:0, one launch (start us, length us, event | category | flops | bytes accessed | tf_op | source)
XLA Modules:
  0.0 89.2 jit_solution(1111324780222678354)
XLA Ops:
  0.0 1.0 %copy-done = bf16[32,2,4096]{2,1,0:T(2,128)(2,1)S(1)} copy-done((bf16[32,2,4096]{2,1,0:T(2,128)(2,1)S(1)}, bf16[32,2,4096]{2,1,0:T(2,128)(2,1)}, u32[]{:S(2)}) %copy-start) | copy-done | bytes 524312
  1.0 0.7 copy-done.1
  1.7 16.2 %project.1 = (f32[2,16,2432]{2,1,0:T(8,128)S(1)}, bf16[2,16,2432]{2,1,0:T(8,128)(2,1)S(1)}, bf16[2,16,2432]{2,1,0:T(8,128)(2,1)S(1)}, bf16[2,16,2432]{2,1,0:T(8,128)(2,1)S(1)}) custom-call(s32[1]{0:T(128)} %bitcast.1.index_ref, bf16[32,2,4096]{2,1,0:T(2,128)(2,1)S(1)} %copy-done, bf16[32,128]{1,0:T(8,128)(2,1)S(1)} %bitcast.66, ...), custom_call_target="tpu_custom_call" | custom-call | flops 2415919104 | bytes 37748736 | tf_op jit(solution)/shard_map/project/pallas_call | solution.py:189
  17.9 0.5 collective-permute-start
  18.4 2.6 %collective-permute-start.1 = (bf16[2,16,2432]{2,1,0:T(8,128)(2,1)S(1)}, bf16[2,16,2432]{2,1,0:T(8,128)(2,1)S(1)}, u32[]{:S(2)}, u32[]{:S(2)}) collective-permute-start(bf16[2,16,2432]{2,1,0:T(8,128)(2,1)S(1)} %get-tuple-element.15), channel_id=1, source_target_pairs={{0,8},{4,12},{8,0},{12,4},{1,9},{5,13},{9,1},{13,5},{2,10},{6,14},... | collective-permute-start | bytes 466952 | tf_op jit(solution)/shard_map/ppermute | solution.py:275
  21.0 1.4 %collective-permute-start.2 = (bf16[2,16,2432]{2,1,0:T(8,128)(2,1)S(1)}, bf16[2,16,2432]{2,1,0:T(8,128)(2,1)S(1)}, u32[]{:S(2)}, u32[]{:S(2)}) collective-permute-start(bf16[2,16,2432]{2,1,0:T(8,128)(2,1)S(1)} %get-tuple-element.16), channel_id=1, source_target_pairs={{0,12},{4,0},{8,4},{12,8},{1,13},{5,1},{9,5},{13,9},{2,14},{6,2},{... | collective-permute-start | bytes 466952 | tf_op jit(solution)/shard_map/ppermute | solution.py:275
  22.6 3.2 %fusion.20 = (bf16[2,384,1,8,128]{4,3,2,1,0:T(8,128)(2,1)}, bf16[2,384,1,8,128]{4,3,2,1,0:T(8,128)(2,1)S(1)}) fusion(bf16[2,384,2,8,128]{4,3,2,1,0:T(8,128)(2,1)} %param.11), kind=kLoop, calls=%fused_computation.48 | loop fusion | bytes 6291456 | tf_op jit(solution)/shard_map/slice | solution.py:70
  25.8 0.2 multiply_cosine_fusion
  26.1 2.1 %collective-permute-done.2 = bf16[2,16,2432]{2,1,0:T(8,128)(2,1)S(1)} collective-permute-done((bf16[2,16,2432]{2,1,0:T(8,128)(2,1)S(1)}, bf16[2,16,2432]{2,1,0:T(8,128)(2,1)S(1)}, u32[]{:S(2)}, u32[]{:S(2)}) %collective-permute-start.2) | collective-permute-done | bytes 155680 | tf_op jit(solution)/shard_map/ppermute | solution.py:275
  28.5 0.2 subtract_convert_fusion
  28.9 0.8 copy.20
  29.8 4.9 %all-to-all-start = ((bf16[8,2,2,18,128]{4,2,3,1,0:T(2,128)(2,1)}), bf16[8,2,2,18,128]{4,2,3,1,0:T(2,128)(2,1)S(1)}, u32[]{:S(2)}, u32[]{:S(2)}) async-start(bf16[8,2,2,18,128]{4,2,3,1,0:T(2,128)(2,1)} %copy.20), calls=%async_computation | async-start | bytes 294912 | tf_op jit(solution)/shard_map/all_to_all | solution.py:308
  34.7 6.8 %all-to-all-done = bf16[8,2,2,18,128]{4,2,3,1,0:T(2,128)(2,1)S(1)} async-done(((bf16[8,2,2,18,128]{4,2,3,1,0:T(2,128)(2,1)}), bf16[8,2,2,18,128]{4,2,3,1,0:T(2,128)(2,1)S(1)}, u32[]{:S(2)}, u32[]{:S(2)}) %all-to-all-start) | async-done | bytes 147488 | tf_op jit(solution)/shard_map/all_to_all | solution.py:308
  41.6 0.8 fusion.22
  42.3 0.4 fusion.23
  42.9 0.3 fusion.10
  43.2 0.2 convolution_bitcast_fusion
  43.5 0.3 copy-done.2
  43.7 0.5 fusion.7
  44.3 0.7 copy.28
  45.0 3.3 %all-to-all-start.1 = ((bf16[2,2,8,16,128]{4,3,1,0,2:T(8,128)(2,1)}), bf16[2,2,8,16,128]{4,3,1,0,2:T(8,128)(2,1)S(1)}, u32[]{:S(2)}, u32[]{:S(2)}) async-start(bf16[2,2,8,16,128]{4,3,1,0,2:T(8,128)(2,1)} %copy.28), calls=%async_computation.1 | async-start | bytes 262144 | tf_op jit(solution)/shard_map/all_to_all | solution.py:313
  48.3 6.0 %all-to-all-done.1 = bf16[2,2,8,16,128]{4,3,1,0,2:T(8,128)(2,1)S(1)} async-done(((bf16[2,2,8,16,128]{4,3,1,0,2:T(8,128)(2,1)}), bf16[2,2,8,16,128]{4,3,1,0,2:T(8,128)(2,1)S(1)}, u32[]{:S(2)}, u32[]{:S(2)}) %all-to-all-start.1) | async-done | bytes 131104 | tf_op jit(solution)/shard_map/all_to_all | solution.py:313
  54.3 6.6 %all_gather.3 = bf16[32,2,2,16,128]{4,3,2,1,0:T(8,128)(2,1)S(1)} all-gather(bf16[8,2,2,16,128]{4,3,2,1,0:T(8,128)(2,1)S(1)} %bitcast.76), channel_id=1, replica_groups=mesh['groups'=2,'gx'=4,'gy'=4] {'gx'}, dimensions={0}, use_global_device_ids=true | all-gather | bytes 655360 | tf_op jit(solution)/shard_map/all_gather | solution.py:315
  61.0 0.2 reshape.103.attended_ref
  61.2 12.6 %outward.1 = (f32[16,4096]{1,0:T(8,128)S(1)}, bf16[16,4096]{1,0:T(8,128)(2,1)S(1)}, bf16[16,4096]{1,0:T(8,128)(2,1)S(1)}, bf16[16,4096]{1,0:T(8,128)(2,1)S(1)}) custom-call(s32[1]{0:T(128)} %bitcast.index_ref, bf16[64,4096]{1,0:T(8,128)(2,1)S(1)} %reshape.103.attended_ref, bf16[4096,4096]{1,0:T(8,128)(2,1)} %bitcast.68), custom_call_target="tpu_custom_call" | custom-call | flops 2147483648 | bytes 33554432 | tf_op jit(solution)/shard_map/outward/pallas_call | solution.py:246
  73.9 1.2 %collective-permute-start.3 = (bf16[16,4096]{1,0:T(8,128)(2,1)S(1)}, bf16[16,4096]{1,0:T(8,128)(2,1)S(1)}, u32[]{:S(2)}, u32[]{:S(2)}) collective-permute-start(bf16[16,4096]{1,0:T(8,128)(2,1)S(1)} %get-tuple-element.18), channel_id=1, source_target_pairs={{0,1},{1,2},{2,3},{3,0},{4,5},{5,6},{6,7},{7,4},{8,9},{9,10},{10,1... | collective-permute-start | bytes 393224 | tf_op jit(solution)/shard_map/ppermute | solution.py:275
  75.0 1.3 %collective-permute-start.4 = (bf16[16,4096]{1,0:T(8,128)(2,1)S(1)}, bf16[16,4096]{1,0:T(8,128)(2,1)S(1)}, u32[]{:S(2)}, u32[]{:S(2)}) collective-permute-start(bf16[16,4096]{1,0:T(8,128)(2,1)S(1)} %get-tuple-element.19), channel_id=1, source_target_pairs={{0,2},{1,3},{2,0},{3,1},{4,6},{5,7},{6,4},{7,5},{8,10},{9,11},{10,... | collective-permute-start | bytes 393224 | tf_op jit(solution)/shard_map/ppermute | solution.py:275
  76.3 1.4 %collective-permute-start.5 = (bf16[16,4096]{1,0:T(8,128)(2,1)S(1)}, bf16[16,4096]{1,0:T(8,128)(2,1)S(1)}, u32[]{:S(2)}, u32[]{:S(2)}) collective-permute-start(bf16[16,4096]{1,0:T(8,128)(2,1)S(1)} %get-tuple-element.20), channel_id=1, source_target_pairs={{0,3},{1,0},{2,1},{3,2},{4,7},{5,4},{6,5},{7,6},{8,11},{9,8},{10,9... | collective-permute-start | bytes 393224 | tf_op jit(solution)/shard_map/ppermute | solution.py:275
  77.8 4.4 %collective-permute-done.3 = bf16[16,4096]{1,0:T(8,128)(2,1)S(1)} collective-permute-done((bf16[16,4096]{1,0:T(8,128)(2,1)S(1)}, bf16[16,4096]{1,0:T(8,128)(2,1)S(1)}, u32[]{:S(2)}, u32[]{:S(2)}) %collective-permute-start.3) | collective-permute-done | bytes 131104 | tf_op jit(solution)/shard_map/ppermute | solution.py:275
  82.2 5.0 %collective-permute-done.4 = bf16[16,4096]{1,0:T(8,128)(2,1)S(1)} collective-permute-done((bf16[16,4096]{1,0:T(8,128)(2,1)S(1)}, bf16[16,4096]{1,0:T(8,128)(2,1)S(1)}, u32[]{:S(2)}, u32[]{:S(2)}) %collective-permute-start.4) | collective-permute-done | bytes 131104 | tf_op jit(solution)/shard_map/ppermute | solution.py:275
  87.3 0.2 reshape.105
  87.4 1.8 %convert_add_fusion.2 = f32[8,2,4096]{2,1,0:T(2,128)} fusion(f32[8,2,4096]{2,1,0:T(2,128)S(1)} %reshape.105, bf16[32,2,4096]{2,1,0:T(2,128)(2,1)} %tokens_ref.1, s32[]{:T(128)S(6)} %select_n.17), kind=kLoop, calls=%fused_computation.24 | loop fusion | flops 131072 | bytes 655364 | tf_op jit(solution)/shard_map/add | solution.py:323
  (31 shorter events, 1.1 us)
Async XLA Ops:
  0.0 1.0 %copy-start = (bf16[32,2,4096]{2,1,0:T(2,128)(2,1)S(1)}, bf16[32,2,4096]{2,1,0:T(2,128)(2,1)}, u32[]{:S(2)}) copy-start(bf16[32,2,4096]{2,1,0:T(2,128)(2,1)} %tokens_ref.1) | copy-start | bytes 1572868
  1.0 0.7 copy-start.1
  1.7 20.7 %copy-start.4 = (s32[32]{0:T(128)S(1)}, s32[32]{0:T(128)}, u32[]{:S(2)}) copy-start(s32[32]{0:T(128)} %param.13) | copy-start | bytes 388
  17.9 8.1 %collective-permute-start = (bf16[2,16,2432]{2,1,0:T(8,128)(2,1)S(1)}, bf16[2,16,2432]{2,1,0:T(8,128)(2,1)S(1)}, u32[]{:S(2)}, u32[]{:S(2)}) collective-permute-start(bf16[2,16,2432]{2,1,0:T(8,128)(2,1)S(1)} %get-tuple-element.14), channel_id=1, source_target_pairs={{0,4},{4,8},{8,12},{12,0},{1,5},{5,9},{9,13},{13,1},{2,6},{6,10},{... | collective-permute-start | bytes 466952 | tf_op jit(solution)/shard_map/ppermute | solution.py:275
  18.4 7.6 %collective-permute-start.1 = (bf16[2,16,2432]{2,1,0:T(8,128)(2,1)S(1)}, bf16[2,16,2432]{2,1,0:T(8,128)(2,1)S(1)}, u32[]{:S(2)}, u32[]{:S(2)}) collective-permute-start(bf16[2,16,2432]{2,1,0:T(8,128)(2,1)S(1)} %get-tuple-element.15), channel_id=1, source_target_pairs={{0,8},{4,12},{8,0},{12,4},{1,9},{5,13},{9,1},{13,5},{2,10},{6,14},... | collective-permute-start | bytes 466952 | tf_op jit(solution)/shard_map/ppermute | solution.py:275
  21.0 7.1 %collective-permute-start.2 = (bf16[2,16,2432]{2,1,0:T(8,128)(2,1)S(1)}, bf16[2,16,2432]{2,1,0:T(8,128)(2,1)S(1)}, u32[]{:S(2)}, u32[]{:S(2)}) collective-permute-start(bf16[2,16,2432]{2,1,0:T(8,128)(2,1)S(1)} %get-tuple-element.16), channel_id=1, source_target_pairs={{0,12},{4,0},{8,4},{12,8},{1,13},{5,1},{9,5},{13,9},{2,14},{6,2},{... | collective-permute-start | bytes 466952 | tf_op jit(solution)/shard_map/ppermute | solution.py:275
  28.3 6.3 %copy-start.3 = (s32[2]{0:T(128)S(1)}, s32[2]{0:T(128)}, u32[]{:S(2)}) copy-start(s32[2]{0:T(128)} %param.12) | copy-start | bytes 28
  29.8 11.7 %all-to-all-start = ((bf16[8,2,2,18,128]{4,2,3,1,0:T(2,128)(2,1)}), bf16[8,2,2,18,128]{4,2,3,1,0:T(2,128)(2,1)S(1)}, u32[]{:S(2)}, u32[]{:S(2)}) async-start(bf16[8,2,2,18,128]{4,2,3,1,0:T(2,128)(2,1)} %copy.20), calls=%async_computation | async-start | bytes 294912 | tf_op jit(solution)/shard_map/all_to_all | solution.py:308
  42.3 1.4 %copy-start.2 = (bf16[2,384,1,8,128]{4,3,2,1,0:T(8,128)(2,1)S(1)}, bf16[2,384,1,8,128]{4,3,2,1,0:T(8,128)(2,1)}, u32[]{:S(2)}) copy-start(bf16[2,384,1,8,128]{4,3,2,1,0:T(8,128)(2,1)} %get-tuple-element.21) | copy-start | bytes 4718596
  45.0 9.4 %all-to-all-start.1 = ((bf16[2,2,8,16,128]{4,3,1,0,2:T(8,128)(2,1)}), bf16[2,2,8,16,128]{4,3,1,0,2:T(8,128)(2,1)S(1)}, u32[]{:S(2)}, u32[]{:S(2)}) async-start(bf16[2,2,8,16,128]{4,3,1,0,2:T(8,128)(2,1)} %copy.28), calls=%async_computation.1 | async-start | bytes 262144 | tf_op jit(solution)/shard_map/all_to_all | solution.py:313
  73.9 8.3 %collective-permute-start.3 = (bf16[16,4096]{1,0:T(8,128)(2,1)S(1)}, bf16[16,4096]{1,0:T(8,128)(2,1)S(1)}, u32[]{:S(2)}, u32[]{:S(2)}) collective-permute-start(bf16[16,4096]{1,0:T(8,128)(2,1)S(1)} %get-tuple-element.18), channel_id=1, source_target_pairs={{0,1},{1,2},{2,3},{3,0},{4,5},{5,6},{6,7},{7,4},{8,9},{9,10},{10,1... | collective-permute-start | bytes 393224 | tf_op jit(solution)/shard_map/ppermute | solution.py:275
  75.0 12.2 %collective-permute-start.4 = (bf16[16,4096]{1,0:T(8,128)(2,1)S(1)}, bf16[16,4096]{1,0:T(8,128)(2,1)S(1)}, u32[]{:S(2)}, u32[]{:S(2)}) collective-permute-start(bf16[16,4096]{1,0:T(8,128)(2,1)S(1)} %get-tuple-element.19), channel_id=1, source_target_pairs={{0,2},{1,3},{2,0},{3,1},{4,6},{5,7},{6,4},{7,5},{8,10},{9,11},{10,... | collective-permute-start | bytes 393224 | tf_op jit(solution)/shard_map/ppermute | solution.py:275
  76.3 10.9 %collective-permute-start.5 = (bf16[16,4096]{1,0:T(8,128)(2,1)S(1)}, bf16[16,4096]{1,0:T(8,128)(2,1)S(1)}, u32[]{:S(2)}, u32[]{:S(2)}) collective-permute-start(bf16[16,4096]{1,0:T(8,128)(2,1)S(1)} %get-tuple-element.20), channel_id=1, source_target_pairs={{0,3},{1,0},{2,1},{3,2},{4,7},{5,4},{6,5},{7,6},{8,11},{9,8},{10,9... | collective-permute-start | bytes 393224 | tf_op jit(solution)/shard_map/ppermute | solution.py:275

commit v3 on v2

--- a/solution.py
+++ b/solution.py
@@ -15,64 +15,7 @@
 rope_base = 500000.0
 PROJECT_BLOCK = 512
 PROJECT_SLOTS = 3
-
-
-def rotate(values, places):
-    half_dim = values.shape[-1] // 2
-    index_half = jnp.arange(half_dim, dtype=jnp.float32)
-    frequency = rope_base ** (-2.0 * index_half / values.shape[-1])
-    angles = places[..., None] * frequency
-    cosine = jnp.cos(angles)
-    sine_part = jnp.sin(angles)
-    front_half = values[..., :half_dim]
-    back_half = values[..., half_dim:]
-    return jnp.concatenate(
-        [front_half * cosine - back_half * sine_part, back_half * cosine + front_half * sine_part],
-        axis=-1,
-    )
-
-
-def finish(projected, positions, first_row, row_count):
-    group_size = projected.shape[3] - 2
-    placed = lax.dynamic_slice_in_dim(positions, first_row, row_count, 0)
-    places = (placed[:, None] + jnp.arange(2, dtype=jnp.int32)[None, :]).astype(jnp.float32)
-    queries = rotate(projected[:, :, :, :group_size], places[:, :, None, None])
-    key_new = rotate(projected[:, :, :, group_size : group_size + 1], places[:, :, None, None])
-    value_new = projected[:, :, :, group_size + 1 :]
-    return jnp.concatenate([queries, key_new, value_new], axis=3).astype(jnp.bfloat16)
-
-
-def attend(queries, key_new, value_new, cache_rows, length):
-    scale_factor = 1.0 / math.sqrt(queries.shape[-1])
-    scores_old = (
-        jnp.einsum(
-            "rtgid,rsgd->rtgis", queries, cache_rows[:, :, 0], preferred_element_type=jnp.float32
-        )
-        * scale_factor
-    )
-    slot_ids = jnp.arange(cache_rows.shape[1], dtype=jnp.int32)
-    visible = slot_ids[None, :] < length[:, None]
-    scores_old = jnp.where(visible[:, None, None, None, :], scores_old, -1e30)
-    scores_new = (
-        jnp.einsum("rtgid,rugd->rtgiu", queries, key_new, preferred_element_type=jnp.float32)
-        * scale_factor
-    )
-    token_ids = jnp.arange(queries.shape[1], dtype=jnp.int32)
-    causal = token_ids[:, None] >= token_ids[None, :]
-    scores_new = jnp.where(causal[None, :, None, None, :], scores_new, -1e30)
-    highest = jnp.maximum(jnp.max(scores_old, axis=-1), jnp.max(scores_new, axis=-1))
-    expo_old = jnp.exp(scores_old - highest[..., None])
-    expo_new = jnp.exp(scores_new - highest[..., None])
-    denominator = jnp.sum(expo_old, axis=-1) + jnp.sum(expo_new, axis=-1)
-    weight_old = (expo_old / denominator[..., None]).astype(jnp.bfloat16)
-    weight_new = (expo_new / denominator[..., None]).astype(jnp.bfloat16)
-    attended = jnp.einsum(
-        "rtgis,rsgd->rtgid", weight_old, cache_rows[:, :, 1], preferred_element_type=jnp.float32
-    )
-    attended = attended + jnp.einsum(
-        "rtgiu,rugd->rtgid", weight_new, value_new, preferred_element_type=jnp.float32
-    )
-    return attended.astype(jnp.bfloat16)
+SMALL_LIMIT = 12 * 2**20
 
 
 def shift_pairs(count, shift):
@@ -215,18 +158,189 @@
             transcendentals=0,
         ),
         name="project",
-    )(index[None], tokens, norm_gain.reshape(-1, 128), weight)
-
-
-def outward_kernel(axis_size, index_ref, attended_ref, weight_ref, *rest):
-    outs, total_ref = rest[:axis_size], rest[axis_size]
-    token_count, depth = attended_ref.shape
+    )(index, tokens, norm_gain.reshape(-1, 128), weight)
+
+
+SMEM = pl.BlockSpec(memory_space=pltpu.SMEM)
+VMEM = pl.BlockSpec(memory_space=pltpu.VMEM)
+
+
+def wrap(place, count):
+    return lax.rem(place, count)
+
+
+def finish_kernel(
+    width_devices, head_devices, token_size, head_dim, index_ref, cosine_ref, sine_ref, *rest
+):
+    parts, rest = rest[:width_devices], rest[width_devices:]
+    outs, (turned_ref, piece_ref) = rest[:head_devices], rest[head_devices:]
+    groups, rows, width = parts[0].shape
+    heads = width // head_dim - 1
+    group_size = heads - 2
+    pad = (piece_ref.shape[0] - group_size * token_size) // 2
+
+    def added(g, lane):
+        total = parts[0][g, :, lane : lane + head_dim]
+        for part in parts[1:]:
+            total = total + part[g, :, lane : lane + head_dim].astype(jnp.float32)
+        return total
+
+    squares = jnp.sum(added(0, heads * head_dim), axis=1, keepdims=True)
+    inv_rms = lax.rsqrt(squares / D + norm_eps)
+    start = pl.multiple_of(index_ref[0] * rows, rows)
+    cosine = cosine_ref[pl.ds(start, rows), :]
+    sine = sine_ref[pl.ds(start, rows), :]
+    for g in range(groups):
+        for head in range(heads):
+            value = added(g, head * head_dim) * inv_rms
+            if head <= group_size:
+                value = value * cosine + pltpu.roll(value, head_dim // 2, 1) * sine
+            turned_ref[g, head] = value.reshape(head_devices, token_size, head_dim)
+    piece_ref[...] = jnp.zeros_like(piece_ref)
+    for shift in range(head_devices):
+        owner = wrap(index_ref[1] + shift, head_devices)
+        for g in range(groups):
+            for head in range(heads):
+                at = head * token_size
+                if head >= group_size:
+                    at = group_size * token_size + (head - group_size) * pad
+                piece_ref[at : at + token_size, :] = turned_ref[g, head, owner]
+            outs[shift][g] = piece_ref[...].astype(jnp.bfloat16)
+
+
+def finish(parts, cosine, sine, index, head_devices, token_size, head_dim):
+    groups, rows, width = parts[0].shape
+    heads = width // head_dim - 1
+    piece_rows = (heads - 2) * token_size + 2 * (-(-token_size // 16) * 16)
+    return pl.pallas_call(
+        functools.partial(finish_kernel, len(parts), head_devices, token_size, head_dim),
+        in_specs=[SMEM] + [VMEM] * (2 + len(parts)),
+        out_specs=[VMEM] * head_devices,
+        out_shape=[jax.ShapeDtypeStruct((groups, piece_rows, head_dim), jnp.bfloat16)]
+        * head_devices,
+        scratch_shapes=[
+            pltpu.VMEM((groups, heads, head_devices, token_size, head_dim), jnp.float32),
+            pltpu.VMEM((piece_rows, head_dim), jnp.float32),
+        ],
+        compiler_params=pltpu.CompilerParams(vmem_limit_bytes=SMALL_LIMIT),
+        name="finish",
+    )(index, cosine, sine, *parts)
+
+
+def attend_kernel(head_devices, query_rows, index_ref, length_ref, cache_ref, *rest):
+    pieces, outs = rest[:head_devices], rest[head_devices:]
+    groups, piece_rows, head_dim = pieces[0].shape
+    rows_local, _, _, slots, _ = cache_ref.shape
+    pad = (piece_rows - query_rows) // 2
+    token_size = 2 * rows_local
+    scale = 1.0 / math.sqrt(head_dim)
+    token_old = lax.rem(lax.broadcasted_iota(jnp.int32, (query_rows, slots), 0), token_size)
+    slot = lax.broadcasted_iota(jnp.int32, (query_rows, slots), 1)
+    length = jnp.zeros((query_rows, slots), jnp.int32)
+    for r in range(rows_local):
+        length = jnp.where(token_old // 2 == r, length_ref[r], length)
+    visible = slot < length
+    token = lax.rem(lax.broadcasted_iota(jnp.int32, (query_rows, pad), 0), token_size)
+    other = lax.broadcasted_iota(jnp.int32, (query_rows, pad), 1)
+    causal = (other // 2 == token // 2) & (other <= token)
+    row_out = lax.rem(lax.broadcasted_iota(jnp.int32, (query_rows, head_dim), 0), token_size) // 2
+    last = (((1,), (1,)), ((), ()))
+    for shift in range(head_devices):
+        source = wrap(index_ref[1] + head_devices - shift, head_devices)
+        for g in range(groups):
+            group = source * groups + g
+            queries = pieces[shift][g, :query_rows, :]
+            key_new = pieces[shift][g, query_rows : query_rows + pad, :]
+            value_new = pieces[shift][g, query_rows + pad :, :]
+            old = None
+            for r in range(rows_local):
+                term = lax.dot_general(
+                    queries, cache_ref[r, 0, group], last, preferred_element_type=jnp.float32
+                )
+                old = term if old is None else jnp.where(token_old // 2 == r, term, old)
+            old = jnp.where(visible, old * scale, -1e30)
+            new = lax.dot_general(queries, key_new, last, preferred_element_type=jnp.float32)
+            new = jnp.where(causal, new * scale, -1e30)
+            highest = jnp.maximum(
+                jnp.max(old, axis=1, keepdims=True), jnp.max(new, axis=1, keepdims=True)
+            )
+            old = jnp.exp(old - highest)
+            new = jnp.exp(new - highest)
+            total = jnp.sum(old, axis=1, keepdims=True) + jnp.sum(new, axis=1, keepdims=True)
+            old = (old / total).astype(jnp.bfloat16)
+            new = (new / total).astype(jnp.bfloat16)
+            attended = None
+            for r in range(rows_local):
+                term = jnp.dot(old, cache_ref[r, 1, group], preferred_element_type=jnp.float32)
+                attended = term if attended is None else jnp.where(row_out == r, term, attended)
+            attended = attended + jnp.dot(new, value_new, preferred_element_type=jnp.float32)
+            outs[shift][g] = attended.astype(jnp.bfloat16)
+
+
+def attend(pieces, cache, lengths, index, query_rows):
+    groups, _, head_dim = pieces[0].shape
+    return pl.pallas_call(
+        functools.partial(attend_kernel, len(pieces), query_rows),
+        in_specs=[SMEM, SMEM] + [VMEM] * (1 + len(pieces)),
+        out_specs=[VMEM] * len(pieces),
+        out_shape=[jax.ShapeDtypeStruct((groups, query_rows, head_dim), jnp.bfloat16)]
+        * len(pieces),
+        compiler_params=pltpu.CompilerParams(vmem_limit_bytes=SMALL_LIMIT),
+        name="attend",
+    )(index, lengths, cache, *pieces)
+
+
+def gather_kernel(token_size, index_ref, *rest):
+    pieces, (out_ref, block_ref) = rest[:-2], rest[-2:]
+    count = len(pieces)
+    groups, query_rows, head_dim = pieces[0].shape
+    heads = query_rows // token_size
+    for shift in range(count):
+        source = wrap(index_ref[1] + shift, count)
+        for g in range(groups):
+            wide = pieces[shift][g].astype(jnp.float32)
+            for head in range(heads):
+                lane = (g * heads + head) * head_dim
+                block_ref[source, :, lane : lane + head_dim] = wide[
+                    head * token_size : (head + 1) * token_size, :
+                ]
+    for lane in range(0, groups * heads * head_dim, head_dim):
+        part = block_ref[:, :, lane : lane + head_dim].reshape(count * token_size, head_dim)
+        out_ref[:, lane : lane + head_dim] = part.astype(jnp.bfloat16)
+
+
+def gather(pieces, index, token_size):
+    groups, query_rows, head_dim = pieces[0].shape
+    width = groups * (query_rows // token_size) * head_dim
+    return pl.pallas_call(
+        functools.partial(gather_kernel, token_size),
+        in_specs=[SMEM] + [VMEM] * len(pieces),
+        out_specs=VMEM,
+        out_shape=jax.ShapeDtypeStruct((len(pieces) * token_size, width), jnp.bfloat16),
+        scratch_shapes=[pltpu.VMEM((len(pieces), token_size, width), jnp.float32)],
+        compiler_params=pltpu.CompilerParams(vmem_limit_bytes=SMALL_LIMIT),
+        name="gather",
+    )(index, *pieces)
+
+
+def outward_kernel(block_count, axis_size, index_ref, *rest):
+    blocks, weight_ref, rest = rest[:block_count], rest[block_count], rest[block_count + 1 :]
+    outs, (left_ref, total_ref) = rest[:axis_size], rest[axis_size:]
+    token_count, depth = left_ref.shape
+    size = token_count // block_count
+
+    @pl.when(pl.program_id(0) == 0)
+    def _():
+        for shift in range(block_count):
+            source = wrap(index_ref[0] + block_count - shift, block_count)
+            left_ref[pl.ds(pl.multiple_of(source * size, size), size), :] = blocks[shift][...]
+
     rows = token_count // axis_size
-    block = pick_block(depth)
-    for k in range(depth // block):
+    step = pick_block(depth)
+    for k in range(0, depth, step):
         term = jnp.dot(
-            attended_ref[:, k * block : (k + 1) * block],
-            weight_ref[k * block : (k + 1) * block, :],
+            left_ref[:, k : k + step],
+            weight_ref[k : k + step, :],
             preferred_element_type=jnp.float32,
         )
         if k == 0:
@@ -234,93 +348,114 @@
         else:
             total_ref[...] += term
     for shift in range(axis_size):
-        first = pl.multiple_of(lax.rem(index_ref[0] + shift, axis_size) * rows, rows)
+        first = pl.multiple_of(wrap(index_ref[1] + shift, axis_size) * rows, rows)
         outs[shift][...] = total_ref[pl.ds(first, rows), :].astype(outs[shift].dtype)
 
 
-def outward(attended, out_flat, axis_size, index):
-    token_count, depth = attended.shape
-    width = out_flat.shape[1]
+def outward(blocks, weight, axis_size, index):
+    size, depth = blocks[0].shape
+    token_count = size * len(blocks)
+    width = weight.shape[1]
     block = pick_block(width)
     rows = token_count // axis_size
     return pl.pallas_call(
-        functools.partial(outward_kernel, axis_size),
-        grid_spec=pltpu.PrefetchScalarGridSpec(
-            num_scalar_prefetch=1,
-            grid=(width // block,),
-            in_specs=[
-                pl.BlockSpec((token_count, depth), lambda j, _: (0, 0)),
-                pl.BlockSpec((depth, block), lambda j, _: (0, j)),
-            ],
-            out_specs=[pl.BlockSpec((rows, block), lambda j, _: (0, j))] * axis_size,
-            scratch_shapes=[pltpu.VMEM((token_count, block), jnp.float32)],
-        ),
+        functools.partial(outward_kernel, len(blocks), axis_size),
+        grid=(width // block,),
+        in_specs=[SMEM]
+        + [VMEM] * len(blocks)
+        + [pl.BlockSpec((depth, block), lambda j: (0, j))],
+        out_specs=[pl.BlockSpec((rows, block), lambda j: (0, j))] * axis_size,
+        scratch_shapes=[
+            pltpu.VMEM((token_count, depth), jnp.bfloat16),
+            pltpu.VMEM((token_count, block), jnp.float32),
+        ],
         out_shape=[
             jax.ShapeDtypeStruct((rows, width), jnp.bfloat16 if s else jnp.float32)
             for s in range(axis_size)
         ],
         compiler_params=pltpu.CompilerParams(vmem_limit_bytes=48 * 2**20),
         cost_estimate=pl.CostEstimate(
-            flops=2 * out_flat.size * token_count,
-            bytes_accessed=out_flat.size * 2,
+            flops=2 * weight.size * token_count,
+            bytes_accessed=weight.size * 2,
             transcendentals=0,
         ),
         name="outward",
-    )(index[None], attended, out_flat)
-
-
-def sum_pieces(pieces, axis):
+    )(index, *blocks, weight)
+
+
+def close_kernel(index_ref, tokens_ref, *rest):
+    parts, out_ref = rest[:-1], rest[-1]
+    rows, tokens, _ = out_ref.shape
+    lanes = 128
+    width = parts[0].shape[1]
+    for lane in range(0, out_ref.shape[2], lanes):
+        column, at = lane // width, lane % width
+        total = None
+        for part in parts[column * len(parts) * width // out_ref.shape[2] :][
+            : len(parts) * width // out_ref.shape[2]
+        ]:
+            term = part[:, at : at + lanes].astype(jnp.float32)
+            total = term if total is None else total + term
+        residual = tokens_ref[:, :, lane : lane + lanes].astype(jnp.float32)
+        out_ref[:, :, lane : lane + lanes] = residual + total.reshape(rows, tokens, lanes)
+
+
+def close(tokens, parts, head_devices, index):
+    rows = tokens.shape[0] // head_devices
+    shape = (rows,) + tokens.shape[1:]
+    return pl.pallas_call(
+        close_kernel,
+        grid_spec=pltpu.PrefetchScalarGridSpec(
+            num_scalar_prefetch=1,
+            grid=(1,),
+            in_specs=[pl.BlockSpec(shape, lambda i, index: (index[1], 0, 0))]
+            + [pl.BlockSpec(part.shape, lambda i, index: (0, 0)) for part in parts],
+            out_specs=pl.BlockSpec(shape, lambda i, index: (0, 0, 0)),
+        ),
+        out_shape=jax.ShapeDtypeStruct(shape, jnp.float32),
+        compiler_params=pltpu.CompilerParams(vmem_limit_bytes=SMALL_LIMIT),
+        name="close",
+    )(index, tokens, *parts)
+
+
+def exchange(pieces, axis, sign=1):
     count = len(pieces)
-    total = pieces[0]
-    landed = [lax.ppermute(pieces[s], axis, shift_pairs(count, s)) for s in range(1, count)]
-    for piece in landed:
-        total = total + piece.astype(jnp.float32)
-    return total
+    return [pieces[0]] + [
+        lax.ppermute(pieces[s], axis, shift_pairs(count, sign * s)) for s in range(1, count)
+    ]
 
 
 def body(tokens, norm_gain, qkv_weight, out_weight, kv_cache, lengths, positions):
     rows_local = kv_cache.shape[0]
     width_devices = lax.axis_size("gx")
     head_devices = lax.axis_size("gy")
-    width_index = lax.axis_index("gx")
-    head_index = lax.axis_index("gy")
-    total_rows = tokens.shape[0]
+    index = jnp.stack([lax.axis_index("gx"), lax.axis_index("gy")])
     local_width = tokens.shape[2]
-    groups_local, group_width, head_dim = qkv_weight.shape[1:]
-    group_size = group_width - 2
-    block_rows = rows_local * head_devices
-    pieces = project(
-        tokens,
-        norm_gain,
-        qkv_weight,
-        width_devices,
-        width_index,
-    )
-    block_sum = sum_pieces(pieces, "gx")
-    flat = group_width * head_dim
-    block_squares = jnp.sum(block_sum[0, :, flat : flat + 3], axis=-1)
-    inv_rms = lax.rsqrt(block_squares / D + norm_eps)
-    projected = (block_sum[:, :, :flat] * inv_rms[None, :, None]).reshape(
-        groups_local, block_rows, 2, group_width, head_dim
-    )
-    projected = jnp.transpose(projected, (1, 2, 0, 3, 4))
-    ready = finish(projected, positions, width_index * block_rows, block_rows)
-    packed = lax.all_to_all(ready, "gy", split_axis=0, concat_axis=2, tiled=True)
-    queries = packed[:, :, :, :group_size]
-    key_new = packed[:, :, :, group_size]
-    value_new = packed[:, :, :, group_size + 1]
-    attended = attend(queries, key_new, value_new, kv_cache, lengths)
-    regrouped = lax.all_to_all(attended, "gy", split_axis=2, concat_axis=0, tiled=True)
+    head_dim = qkv_weight.shape[3]
+    group_size = qkv_weight.shape[2] - 2
+    token_size = rows_local * 2
+
+    half = head_dim // 2
+    frequency = rope_base ** (-2.0 * jnp.arange(half, dtype=jnp.float32) / head_dim)
+    places = (positions[:, None] + jnp.arange(2, dtype=jnp.int32)[None, :]).astype(jnp.float32)
+    angles = places.reshape(-1, 1) * frequency
+    cosine = jnp.cos(angles)
+    sine = jnp.sin(angles)
+    cosine = jnp.concatenate([cosine, cosine], axis=1)
+    sine = jnp.concatenate([-sine, sine], axis=1)
+    cache = jnp.transpose(kv_cache, (0, 2, 3, 1, 4))
+
+    parts = project(tokens, norm_gain, qkv_weight, width_devices, index)
+    parts = exchange(parts, "gx")
+    pieces = finish(parts, cosine, sine, index, head_devices, token_size, head_dim)
+    pieces = exchange(pieces, "gy")
+    attended = attend(pieces, cache, lengths, index, group_size * token_size)
+    attended = exchange(attended, "gy", -1)
+    block = gather(attended, index, token_size)
+    blocks = exchange([block] * width_devices, "gx")
     out_flat = out_weight.reshape(-1, local_width)
-    row_piece = lax.all_gather(regrouped, "gx", axis=0, tiled=True)
-    piece_rows = row_piece.shape[0]
-    parts = outward(row_piece.reshape(piece_rows * 2, -1), out_flat, head_devices, head_index)
-    row_share = total_rows // head_devices
-    own_sum = sum_pieces(parts, "gy").reshape(row_share, 2, local_width)
-    residual = lax.dynamic_slice_in_dim(tokens, head_index * row_share, row_share, 0).astype(
-        jnp.float32
-    )
-    return residual + own_sum
+    sums = outward(blocks, out_flat, head_devices, index)
+    return close(tokens, exchange(sums, "gy"), head_devices, index)
 
 
 def solution(mesh):

time: 90 us -> 86.1 us (0.957)
  Pallas kernels: 28.8 us -> 36.6 us
  blocking collectives: 6.65 us -> 0 us
  other arithmetic: 3.28 us -> 0.44 us
  local copies, waits for them, and re-layouts: 7.33 us -> 4.56 us
  matrix products: 1.98 us -> 0 us
  starting transfers between devices: 16.6 us -> 18.4 us
  waiting for transfers between devices: 24.4 us -> 25.8 us
    ppermute x6 -> x15, waiting for transfers between devices: 11.6 us -> 25.8 us  [exchange(): lax.ppermute(pieces[s], axis, shift_pairs(count, sign * s))]
    all_to_all x2 -> x0, waiting for transfers between devices: 12.8 us -> none  [the longest x1 6.78 us: body(): lax.all_to_all(ready, 'gy', split_axis=0, concat_axis=2, tiled=True)]
    ppermute x6 -> x15, starting transfers between devices: 8.36 us -> 18.4 us  [exchange(): lax.ppermute(pieces[s], axis, shift_pairs(count, sign * s))]
    all_to_all x2 -> x0, starting transfers between devices: 8.21 us -> none  [the longest x1 4.89 us: body(): lax.all_to_all(ready, 'gy', split_axis=0, concat_axis=2, tiled=True)]
    pallas_call x1 -> x5, Pallas kernels: 12.6 us -> 19.8 us  [the longest x1 12.7 us: outward(): pl.pallas_call(functools.partial(outward_kernel, len(blocks), axis_size),...]
    all_gather x1 -> x0, blocking collectives: 6.65 us -> none  [body(): row_piece = lax.all_gather(regrouped, 'gx', axis=0, tiled=True)]
    slice x3 -> x0, local copies, waits for them, and re-layouts: 3.28 us -> none  [the longest x1 3.24 us: attend(): cache_rows[:, :, 1]]
    unnamed x10 -> x11, local copies, waits for them, and re-layouts: 2.02 us -> 4.45 us
  transfers between devices with their start and end apart: 8 -> 15, of which waited for: 5 -> 13; matrix products, arithmetic and copies ran while one was open for 4% -> 4% of each run, Pallas kernels for 0% -> 0%
where the time goes in v3:
time: 86.1 us; the launch traced here: 85.9 us
  Pallas kernels  36.6 us (43%)
  waiting for transfers between devices  25.8 us (30%)
  starting transfers between devices  18.4 us (21%)
  local copies, waits for them, and re-layouts  4.56 us (5%)
    ppermute x15, waiting for transfers between devices, exchange(): lax.ppermute(pieces[s], axis, shift_pairs(count, sign * s))  25.8 us
    ppermute x15, starting transfers between devices, exchange(): lax.ppermute(pieces[s], axis, shift_pairs(count, sign * s))  18.4 us
    pallas_call x1, Pallas kernels, project(): pl.pallas_call(functools.partial(project_kernel, axis_size, block, slots)...  16.8 us
    pallas_call x1, Pallas kernels, outward(): pl.pallas_call(functools.partial(outward_kernel, len(blocks), axis_size),...  12.7 us
    unnamed x11, local copies, waits for them, and re-layouts  4.45 us
    pallas_call x1, Pallas kernels, attend(): pl.pallas_call(functools.partial(attend_kernel, len(pieces), query_rows),...  4.12 us
  transfers between devices with their start and end apart: 15, of which 13 were waited for; matrix products, arithmetic and copies ran while one was open for 4% of the time, Pallas kernels for 0%

profile of v3, /device:TPU:0, one launch (start us, length us, event | category | flops | bytes accessed | tf_op | source)
XLA Modules:
  0.0 85.9 jit_solution(5713857560438262167)
XLA Ops:
  0.1 1.0 %copy-done = bf16[32,2,4096]{2,1,0:T(2,128)(2,1)S(1)} copy-done((bf16[32,2,4096]{2,1,0:T(2,128)(2,1)S(1)}, bf16[32,2,4096]{2,1,0:T(2,128)(2,1)}, u32[]{:S(2)}) %copy-start) | copy-done | bytes 524312
  1.1 0.7 copy-done.2
  1.8 16.8 %project.1 = (f32[2,16,2432]{2,1,0:T(8,128)S(1)}, bf16[2,16,2432]{2,1,0:T(8,128)(2,1)S(1)}, bf16[2,16,2432]{2,1,0:T(8,128)(2,1)S(1)}, bf16[2,16,2432]{2,1,0:T(8,128)(2,1)S(1)}) custom-call(s32[2]{0:T(128)S(1)} %pad_add_fusion.index_ref, bf16[32,2,4096]{2,1,0:T(2,128)(2,1)S(1)} %copy-done, bf16[32,128]{1,0:T(8,128)(2,1)S(1)} %bitcast.11, ...), custom_call_target="tpu_custom_call" | custom-call | flops 2415919104 | bytes 37748736 | tf_op jit(solution)/shard_map/project/pallas_call | solution.py:132
  18.6 0.5 collective-permute-start
  19.1 2.6 %collective-permute-start.1 = (bf16[2,16,2432]{2,1,0:T(8,128)(2,1)S(1)}, bf16[2,16,2432]{2,1,0:T(8,128)(2,1)S(1)}, u32[]{:S(2)}, u32[]{:S(2)}) collective-permute-start(bf16[2,16,2432]{2,1,0:T(8,128)(2,1)S(1)} %get-tuple-element.23), channel_id=1, source_target_pairs={{0,8},{4,12},{8,0},{12,4},{1,9},{5,13},{9,1},{13,5},{2,10},{6,14},... | collective-permute-start | bytes 466952 | tf_op jit(solution)/shard_map/ppermute | solution.py:424
  21.7 1.4 %collective-permute-start.2 = (bf16[2,16,2432]{2,1,0:T(8,128)(2,1)S(1)}, bf16[2,16,2432]{2,1,0:T(8,128)(2,1)S(1)}, u32[]{:S(2)}, u32[]{:S(2)}) collective-permute-start(bf16[2,16,2432]{2,1,0:T(8,128)(2,1)S(1)} %get-tuple-element.24), channel_id=1, source_target_pairs={{0,12},{4,0},{8,4},{12,8},{1,13},{5,1},{9,5},{13,9},{2,14},{6,2},{... | collective-permute-start | bytes 466952 | tf_op jit(solution)/shard_map/ppermute | solution.py:424
  23.6 1.1 %collective-permute-done.rest_1_ = bf16[2,16,2432]{2,1,0:T(8,128)(2,1)S(1)} collective-permute-done((bf16[2,16,2432]{2,1,0:T(8,128)(2,1)S(1)}, bf16[2,16,2432]{2,1,0:T(8,128)(2,1)S(1)}, u32[]{:S(2)}, u32[]{:S(2)}) %collective-permute-start) | collective-permute-done | bytes 155680 | tf_op jit(solution)/shard_map/ppermute | solution.py:424
  24.7 1.9 %collective-permute-done.1.rest_2_ = bf16[2,16,2432]{2,1,0:T(8,128)(2,1)S(1)} collective-permute-done((bf16[2,16,2432]{2,1,0:T(8,128)(2,1)S(1)}, bf16[2,16,2432]{2,1,0:T(8,128)(2,1)S(1)}, u32[]{:S(2)}, u32[]{:S(2)}) %collective-permute-start.1) | collective-permute-done | bytes 155680 | tf_op jit(solution)/shard_map/ppermute | solution.py:424
  26.5 2.2 %collective-permute-done.2.rest_3_ = bf16[2,16,2432]{2,1,0:T(8,128)(2,1)S(1)} collective-permute-done((bf16[2,16,2432]{2,1,0:T(8,128)(2,1)S(1)}, bf16[2,16,2432]{2,1,0:T(8,128)(2,1)S(1)}, u32[]{:S(2)}, u32[]{:S(2)}) %collective-permute-start.2) | collective-permute-done | bytes 155680 | tf_op jit(solution)/shard_map/ppermute | solution.py:424
  28.8 1.0 %finish.1 = (bf16[2,96,128]{2,1,0:T(8,128)(2,1)S(1)}, bf16[2,96,128]{2,1,0:T(8,128)(2,1)S(1)}, bf16[2,96,128]{2,1,0:T(8,128)(2,1)S(1)}, bf16[2,96,128]{2,1,0:T(8,128)(2,1)S(1)}) custom-call(s32[2]{0:T(128)S(1)} %pad_add_fusion.index_ref, f32[64,128]{1,0:T(8,128)S(1)} %get-tuple-element.40.cosine_ref, f32[64,128]{1,0:T(8,128)S(1)} %get-tuple-element.41.sine_ref, ...), custom_call_target="tpu_custom_call" | custom-call | tf_op jit(solution)/shard_map/finish/pallas_call | solution.py:215
  29.8 1.6 %collective-permute-start.3 = (bf16[2,96,128]{2,1,0:T(8,128)(2,1)S(1)}, bf16[2,96,128]{2,1,0:T(8,128)(2,1)S(1)}, u32[]{:S(2)}, u32[]{:S(2)}) collective-permute-start(bf16[2,96,128]{2,1,0:T(8,128)(2,1)S(1)} %get-tuple-element.26), channel_id=1, source_target_pairs={{0,1},{1,2},{2,3},{3,0},{4,5},{5,6},{6,7},{7,4},{8,9},{9,10},{10,1... | collective-permute-start | bytes 147464 | tf_op jit(solution)/shard_map/ppermute | solution.py:424
  31.4 2.6 %collective-permute-start.4 = (bf16[2,96,128]{2,1,0:T(8,128)(2,1)S(1)}, bf16[2,96,128]{2,1,0:T(8,128)(2,1)S(1)}, u32[]{:S(2)}, u32[]{:S(2)}) collective-permute-start(bf16[2,96,128]{2,1,0:T(8,128)(2,1)S(1)} %get-tuple-element.27), channel_id=1, source_target_pairs={{0,2},{1,3},{2,0},{3,1},{4,6},{5,7},{6,4},{7,5},{8,10},{9,11},{10,... | collective-permute-start | bytes 147464 | tf_op jit(solution)/shard_map/ppermute | solution.py:424
  34.0 1.3 %collective-permute-start.5 = (bf16[2,96,128]{2,1,0:T(8,128)(2,1)S(1)}, bf16[2,96,128]{2,1,0:T(8,128)(2,1)S(1)}, u32[]{:S(2)}, u32[]{:S(2)}) collective-permute-start(bf16[2,96,128]{2,1,0:T(8,128)(2,1)S(1)} %get-tuple-element.28), channel_id=1, source_target_pairs={{0,3},{1,0},{2,1},{3,2},{4,7},{5,4},{6,5},{7,6},{8,11},{9,8},{10,9... | collective-permute-start | bytes 147464 | tf_op jit(solution)/shard_map/ppermute | solution.py:424
  35.3 2.7 %copy.11 = bf16[2,384,2,8,128]{4,1,3,2,0:T(8,128)(2,1)S(1)} copy(bf16[2,384,2,8,128]{4,3,2,1,0:T(8,128)(2,1)} %param.11) | data formatting | bytes 6291456 | tf_op args[4]
  38.3 0.3 collective-permute-done.5.rest_3_
  38.6 4.1 %attend.1 = (bf16[2,64,128]{2,1,0:T(8,128)(2,1)S(1)}, bf16[2,64,128]{2,1,0:T(8,128)(2,1)S(1)}, bf16[2,64,128]{2,1,0:T(8,128)(2,1)S(1)}, bf16[2,64,128]{2,1,0:T(8,128)(2,1)S(1)}) custom-call(s32[2]{0:T(128)S(1)} %pad_add_fusion.index_ref, s32[2]{0:T(128)S(1)} %copy-done.3, bf16[2,2,8,384,128]{4,3,2,1,0:T(8,128)(2,1)S(1)} %bitcast.10, ...), custom_call_target="tpu_custom_call" | custom-call | tf_op jit(solution)/shard_map/attend/pallas_call | solution.py:282
  42.7 2.7 %collective-permute-start.6 = (bf16[2,64,128]{2,1,0:T(8,128)(2,1)S(1)}, bf16[2,64,128]{2,1,0:T(8,128)(2,1)S(1)}, u32[]{:S(2)}, u32[]{:S(2)}) collective-permute-start(bf16[2,64,128]{2,1,0:T(8,128)(2,1)S(1)} %get-tuple-element.30), channel_id=1, source_target_pairs={{0,3},{1,0},{2,1},{3,2},{4,7},{5,4},{6,5},{7,6},{8,11},{9,8},{10,9... | collective-permute-start | bytes 98312 | tf_op jit(solution)/shard_map/ppermute | solution.py:424
  45.5 0.6 collective-permute-start.8
  46.0 1.0 %collective-permute-done.6.rest_1_ = bf16[2,64,128]{2,1,0:T(8,128)(2,1)S(1)} collective-permute-done((bf16[2,64,128]{2,1,0:T(8,128)(2,1)S(1)}, bf16[2,64,128]{2,1,0:T(8,128)(2,1)S(1)}, u32[]{:S(2)}, u32[]{:S(2)}) %collective-permute-start.6) | collective-permute-done | bytes 32800 | tf_op jit(solution)/shard_map/ppermute | solution.py:424
  47.0 3.2 %collective-permute-done.7.rest_2_ = bf16[2,64,128]{2,1,0:T(8,128)(2,1)S(1)} collective-permute-done((bf16[2,64,128]{2,1,0:T(8,128)(2,1)S(1)}, bf16[2,64,128]{2,1,0:T(8,128)(2,1)S(1)}, u32[]{:S(2)}, u32[]{:S(2)}) %collective-permute-start.7) | collective-permute-done | bytes 32800 | tf_op jit(solution)/shard_map/ppermute | solution.py:424
  50.2 1.0 %collective-permute-done.8.rest_3_ = bf16[2,64,128]{2,1,0:T(8,128)(2,1)S(1)} collective-permute-done((bf16[2,64,128]{2,1,0:T(8,128)(2,1)S(1)}, bf16[2,64,128]{2,1,0:T(8,128)(2,1)S(1)}, u32[]{:S(2)}, u32[]{:S(2)}) %collective-permute-start.8) | collective-permute-done | bytes 32800 | tf_op jit(solution)/shard_map/ppermute | solution.py:424
  51.2 0.6 gather.1.rest_0_
  51.9 0.8 collective-permute-start.10
  52.8 2.7 %collective-permute-done.11.rest_3_ = bf16[16,4096]{1,0:T(8,128)(2,1)S(1)} collective-permute-done((bf16[16,4096]{1,0:T(8,128)(2,1)S(1)}, bf16[16,4096]{1,0:T(8,128)(2,1)S(1)}, u32[]{:S(2)}, u32[]{:S(2)}) %collective-permute-start.11) | collective-permute-done | bytes 131104 | tf_op jit(solution)/shard_map/ppermute | solution.py:424
  55.5 3.3 %collective-permute-done.10.rest_2_ = bf16[16,4096]{1,0:T(8,128)(2,1)S(1)} collective-permute-done((bf16[16,4096]{1,0:T(8,128)(2,1)S(1)}, bf16[16,4096]{1,0:T(8,128)(2,1)S(1)}, u32[]{:S(2)}, u32[]{:S(2)}) %collective-permute-start.10) | collective-permute-done | bytes 131104 | tf_op jit(solution)/shard_map/ppermute | solution.py:424
  58.8 0.9 %collective-permute-done.9.rest_1_ = bf16[16,4096]{1,0:T(8,128)(2,1)S(1)} collective-permute-done((bf16[16,4096]{1,0:T(8,128)(2,1)S(1)}, bf16[16,4096]{1,0:T(8,128)(2,1)S(1)}, u32[]{:S(2)}, u32[]{:S(2)}) %collective-permute-start.9) | collective-permute-done | bytes 131104 | tf_op jit(solution)/shard_map/ppermute | solution.py:424
  59.7 12.7 %outward.1 = (f32[16,4096]{1,0:T(8,128)S(1)}, bf16[16,4096]{1,0:T(8,128)(2,1)S(1)}, bf16[16,4096]{1,0:T(8,128)(2,1)S(1)}, bf16[16,4096]{1,0:T(8,128)(2,1)S(1)}) custom-call(s32[2]{0:T(128)S(1)} %pad_add_fusion.index_ref, bf16[16,4096]{1,0:T(8,128)(2,1)S(1)} %gather.1.rest_0_, bf16[16,4096]{1,0:T(8,128)(2,1)S(1)} %collective-permute-done.9.rest_1_, ...), custom_call_target="tpu_custom_call" | custom-call | flops 2147483648 | bytes 33554432 | tf_op jit(solution)/shard_map/outward/pallas_call | solution.py:361
  72.5 1.2 %collective-permute-start.13 = (bf16[16,4096]{1,0:T(8,128)(2,1)S(1)}, bf16[16,4096]{1,0:T(8,128)(2,1)S(1)}, u32[]{:S(2)}, u32[]{:S(2)}) collective-permute-start(bf16[16,4096]{1,0:T(8,128)(2,1)S(1)} %get-tuple-element.35), channel_id=1, source_target_pairs={{0,2},{1,3},{2,0},{3,1},{4,6},{5,7},{6,4},{7,5},{8,10},{9,11},{10,... | collective-permute-start | bytes 393224 | tf_op jit(solution)/shard_map/ppermute | solution.py:424
  73.7 2.8 %collective-permute-start.14 = (bf16[16,4096]{1,0:T(8,128)(2,1)S(1)}, bf16[16,4096]{1,0:T(8,128)(2,1)S(1)}, u32[]{:S(2)}, u32[]{:S(2)}) collective-permute-start(bf16[16,4096]{1,0:T(8,128)(2,1)S(1)} %get-tuple-element.36), channel_id=1, source_target_pairs={{0,3},{1,0},{2,1},{3,2},{4,7},{5,4},{6,5},{7,6},{8,11},{9,8},{10,9... | collective-permute-start | bytes 393224 | tf_op jit(solution)/shard_map/ppermute | solution.py:424
  76.5 4.2 %collective-permute-done.12.rest_1_ = bf16[16,4096]{1,0:T(8,128)(2,1)S(1)} collective-permute-done((bf16[16,4096]{1,0:T(8,128)(2,1)S(1)}, bf16[16,4096]{1,0:T(8,128)(2,1)S(1)}, u32[]{:S(2)}, u32[]{:S(2)}) %collective-permute-start.12) | collective-permute-done | bytes 131104 | tf_op jit(solution)/shard_map/ppermute | solution.py:424
  80.8 3.7 %collective-permute-done.13.rest_2_ = bf16[16,4096]{1,0:T(8,128)(2,1)S(1)} collective-permute-done((bf16[16,4096]{1,0:T(8,128)(2,1)S(1)}, bf16[16,4096]{1,0:T(8,128)(2,1)S(1)}, u32[]{:S(2)}, u32[]{:S(2)}) %collective-permute-start.13) | collective-permute-done | bytes 131104 | tf_op jit(solution)/shard_map/ppermute | solution.py:424
  84.5 1.4 %close.1 = f32[8,2,4096]{2,1,0:T(2,128)} custom-call(s32[2]{0:T(128)S(1)} %pad_add_fusion.index_ref, bf16[32,2,4096]{2,1,0:T(2,128)(2,1)S(1)} %copy-done.1, f32[16,4096]{1,0:T(8,128)S(1)} %get-tuple-element.33.rest_0_, bf16[16,4096]{1,0:T(8,128)(2,1)S(1)} %collective-permute-done.12.rest_1_, bf16[16,4096]{1,0:T(8,128)(2,1)S(1)} %collective-permute-done.13.rest_2_, ...), custom_call_target="tpu_custom_call" | custom-call | tf_op jit(solution)/shard_map/close/pallas_call | solution.py:406
  (21 shorter events, 1.2 us)
Async XLA Ops:
  0.0 23.1 %copy-start.4 = (s32[32]{0:T(128)S(1)}, s32[32]{0:T(128)}, u32[]{:S(2)}) copy-start(s32[32]{0:T(128)} %param.13) | copy-start | bytes 388
  0.0 38.6 %copy-start.3 = (s32[2]{0:T(128)S(1)}, s32[2]{0:T(128)}, u32[]{:S(2)}) copy-start(s32[2]{0:T(128)} %length_ref.1) | copy-start | bytes 28
  0.1 1.0 %copy-start = (bf16[32,2,4096]{2,1,0:T(2,128)(2,1)S(1)}, bf16[32,2,4096]{2,1,0:T(2,128)(2,1)}, u32[]{:S(2)}) copy-start(bf16[32,2,4096]{2,1,0:T(2,128)(2,1)} %tokens_ref.3) | copy-start | bytes 1572868
  1.1 0.7 copy-start.2
  1.8 82.7 %copy-start.1 = (bf16[32,2,4096]{2,1,0:T(2,128)(2,1)S(1)}, bf16[32,2,4096]{2,1,0:T(2,128)(2,1)}, u32[]{:S(2)}) copy-start(bf16[32,2,4096]{2,1,0:T(2,128)(2,1)} %tokens_ref.3) | copy-start | bytes 1572868
  18.6 6.1 %collective-permute-start = (bf16[2,16,2432]{2,1,0:T(8,128)(2,1)S(1)}, bf16[2,16,2432]{2,1,0:T(8,128)(2,1)S(1)}, u32[]{:S(2)}, u32[]{:S(2)}) collective-permute-start(bf16[2,16,2432]{2,1,0:T(8,128)(2,1)S(1)} %get-tuple-element.22), channel_id=1, source_target_pairs={{0,4},{4,8},{8,12},{12,0},{1,5},{5,9},{9,13},{13,1},{2,6},{6,10},{... | collective-permute-start | bytes 466952 | tf_op jit(solution)/shard_map/ppermute | solution.py:424
  19.1 7.5 %collective-permute-start.1 = (bf16[2,16,2432]{2,1,0:T(8,128)(2,1)S(1)}, bf16[2,16,2432]{2,1,0:T(8,128)(2,1)S(1)}, u32[]{:S(2)}, u32[]{:S(2)}) collective-permute-start(bf16[2,16,2432]{2,1,0:T(8,128)(2,1)S(1)} %get-tuple-element.23), channel_id=1, source_target_pairs={{0,8},{4,12},{8,0},{12,4},{1,9},{5,13},{9,1},{13,5},{2,10},{6,14},... | collective-permute-start | bytes 466952 | tf_op jit(solution)/shard_map/ppermute | solution.py:424
  21.7 7.1 %collective-permute-start.2 = (bf16[2,16,2432]{2,1,0:T(8,128)(2,1)S(1)}, bf16[2,16,2432]{2,1,0:T(8,128)(2,1)S(1)}, u32[]{:S(2)}, u32[]{:S(2)}) collective-permute-start(bf16[2,16,2432]{2,1,0:T(8,128)(2,1)S(1)} %get-tuple-element.24), channel_id=1, source_target_pairs={{0,12},{4,0},{8,4},{12,8},{1,13},{5,1},{9,5},{13,9},{2,14},{6,2},{... | collective-permute-start | bytes 466952 | tf_op jit(solution)/shard_map/ppermute | solution.py:424
  29.8 8.3 %collective-permute-start.3 = (bf16[2,96,128]{2,1,0:T(8,128)(2,1)S(1)}, bf16[2,96,128]{2,1,0:T(8,128)(2,1)S(1)}, u32[]{:S(2)}, u32[]{:S(2)}) collective-permute-start(bf16[2,96,128]{2,1,0:T(8,128)(2,1)S(1)} %get-tuple-element.26), channel_id=1, source_target_pairs={{0,1},{1,2},{2,3},{3,0},{4,5},{5,6},{6,7},{7,4},{8,9},{9,10},{10,1... | collective-permute-start | bytes 147464 | tf_op jit(solution)/shard_map/ppermute | solution.py:424
  31.4 6.9 %collective-permute-start.4 = (bf16[2,96,128]{2,1,0:T(8,128)(2,1)S(1)}, bf16[2,96,128]{2,1,0:T(8,128)(2,1)S(1)}, u32[]{:S(2)}, u32[]{:S(2)}) collective-permute-start(bf16[2,96,128]{2,1,0:T(8,128)(2,1)S(1)} %get-tuple-element.27), channel_id=1, source_target_pairs={{0,2},{1,3},{2,0},{3,1},{4,6},{5,7},{6,4},{7,5},{8,10},{9,11},{10,... | collective-permute-start | bytes 147464 | tf_op jit(solution)/shard_map/ppermute | solution.py:424
  34.0 4.6 %collective-permute-start.5 = (bf16[2,96,128]{2,1,0:T(8,128)(2,1)S(1)}, bf16[2,96,128]{2,1,0:T(8,128)(2,1)S(1)}, u32[]{:S(2)}, u32[]{:S(2)}) collective-permute-start(bf16[2,96,128]{2,1,0:T(8,128)(2,1)S(1)} %get-tuple-element.28), channel_id=1, source_target_pairs={{0,3},{1,0},{2,1},{3,2},{4,7},{5,4},{6,5},{7,6},{8,11},{9,8},{10,9... | collective-permute-start | bytes 147464 | tf_op jit(solution)/shard_map/ppermute | solution.py:424
  42.7 4.3 %collective-permute-start.6 = (bf16[2,64,128]{2,1,0:T(8,128)(2,1)S(1)}, bf16[2,64,128]{2,1,0:T(8,128)(2,1)S(1)}, u32[]{:S(2)}, u32[]{:S(2)}) collective-permute-start(bf16[2,64,128]{2,1,0:T(8,128)(2,1)S(1)} %get-tuple-element.30), channel_id=1, source_target_pairs={{0,3},{1,0},{2,1},{3,2},{4,7},{5,4},{6,5},{7,6},{8,11},{9,8},{10,9... | collective-permute-start | bytes 98312 | tf_op jit(solution)/shard_map/ppermute | solution.py:424
  45.4 4.8 %collective-permute-start.7 = (bf16[2,64,128]{2,1,0:T(8,128)(2,1)S(1)}, bf16[2,64,128]{2,1,0:T(8,128)(2,1)S(1)}, u32[]{:S(2)}, u32[]{:S(2)}) collective-permute-start(bf16[2,64,128]{2,1,0:T(8,128)(2,1)S(1)} %get-tuple-element.31), channel_id=1, source_target_pairs={{0,2},{1,3},{2,0},{3,1},{4,6},{5,7},{6,4},{7,5},{8,10},{9,11},{10,... | collective-permute-start | bytes 98312 | tf_op jit(solution)/shard_map/ppermute | solution.py:424
  45.5 5.7 %collective-permute-start.8 = (bf16[2,64,128]{2,1,0:T(8,128)(2,1)S(1)}, bf16[2,64,128]{2,1,0:T(8,128)(2,1)S(1)}, u32[]{:S(2)}, u32[]{:S(2)}) collective-permute-start(bf16[2,64,128]{2,1,0:T(8,128)(2,1)S(1)} %get-tuple-element.32), channel_id=1, source_target_pairs={{0,1},{1,2},{2,3},{3,0},{4,5},{5,6},{6,7},{7,4},{8,9},{9,10},{10,1... | collective-permute-start | bytes 98312 | tf_op jit(solution)/shard_map/ppermute | solution.py:424
  51.8 3.7 %collective-permute-start.11 = (bf16[16,4096]{1,0:T(8,128)(2,1)S(1)}, bf16[16,4096]{1,0:T(8,128)(2,1)S(1)}, u32[]{:S(2)}, u32[]{:S(2)}) collective-permute-start(bf16[16,4096]{1,0:T(8,128)(2,1)S(1)} %gather.1.rest_0_), channel_id=1, source_target_pairs={{0,12},{4,0},{8,4},{12,8},{1,13},{5,1},{9,5},{13,9},{2,14},{6,2},{... | collective-permute-start | bytes 393224 | tf_op jit(solution)/shard_map/ppermute | solution.py:424
  51.9 7.0 %collective-permute-start.10 = (bf16[16,4096]{1,0:T(8,128)(2,1)S(1)}, bf16[16,4096]{1,0:T(8,128)(2,1)S(1)}, u32[]{:S(2)}, u32[]{:S(2)}) collective-permute-start(bf16[16,4096]{1,0:T(8,128)(2,1)S(1)} %gather.1.rest_0_), channel_id=1, source_target_pairs={{0,8},{4,12},{8,0},{12,4},{1,9},{5,13},{9,1},{13,5},{2,10},{6,14},... | collective-permute-start | bytes 393224 | tf_op jit(solution)/shard_map/ppermute | solution.py:424
  52.6 7.1 %collective-permute-start.9 = (bf16[16,4096]{1,0:T(8,128)(2,1)S(1)}, bf16[16,4096]{1,0:T(8,128)(2,1)S(1)}, u32[]{:S(2)}, u32[]{:S(2)}) collective-permute-start(bf16[16,4096]{1,0:T(8,128)(2,1)S(1)} %gather.1.rest_0_), channel_id=1, source_target_pairs={{0,4},{4,8},{8,12},{12,0},{1,5},{5,9},{9,13},{13,1},{2,6},{6,10},{... | collective-permute-start | bytes 393224 | tf_op jit(solution)/shard_map/ppermute | solution.py:424
  72.4 8.3 %collective-permute-start.12 = (bf16[16,4096]{1,0:T(8,128)(2,1)S(1)}, bf16[16,4096]{1,0:T(8,128)(2,1)S(1)}, u32[]{:S(2)}, u32[]{:S(2)}) collective-permute-start(bf16[16,4096]{1,0:T(8,128)(2,1)S(1)} %get-tuple-element.34), channel_id=1, source_target_pairs={{0,1},{1,2},{2,3},{3,0},{4,5},{5,6},{6,7},{7,4},{8,9},{9,10},{10,1... | collective-permute-start | bytes 393224 | tf_op jit(solution)/shard_map/ppermute | solution.py:424
  72.5 12.0 %collective-permute-start.13 = (bf16[16,4096]{1,0:T(8,128)(2,1)S(1)}, bf16[16,4096]{1,0:T(8,128)(2,1)S(1)}, u32[]{:S(2)}, u32[]{:S(2)}) collective-permute-start(bf16[16,4096]{1,0:T(8,128)(2,1)S(1)} %get-tuple-element.35), channel_id=1, source_target_pairs={{0,2},{1,3},{2,0},{3,1},{4,6},{5,7},{6,4},{7,5},{8,10},{9,11},{10,... | collective-permute-start | bytes 393224 | tf_op jit(solution)/shard_map/ppermute | solution.py:424
  73.7 10.8 %collective-permute-start.14 = (bf16[16,4096]{1,0:T(8,128)(2,1)S(1)}, bf16[16,4096]{1,0:T(8,128)(2,1)S(1)}, u32[]{:S(2)}, u32[]{:S(2)}) collective-permute-start(bf16[16,4096]{1,0:T(8,128)(2,1)S(1)} %get-tuple-element.36), channel_id=1, source_target_pairs={{0,3},{1,0},{2,1},{3,2},{4,7},{5,4},{6,5},{7,6},{8,11},{9,8},{10,9... | collective-permute-start | bytes 393224 | tf_op jit(solution)/shard_map/ppermute | solution.py:424

commit v4 on v3

--- a/solution.py
+++ b/solution.py
@@ -16,17 +16,20 @@
 PROJECT_BLOCK = 512
 PROJECT_SLOTS = 3
 SMALL_LIMIT = 12 * 2**20
+OUTWARD_SHARE = 8
+OUTWARD_STEP = 512
+OUTWARD_SLOTS = 6
+OUTWARD_LIMIT = 20 * 2**20
+HELD_SHARES = (4, 4, 6)
+PAIR_GROUP = 4
 
 
 def shift_pairs(count, shift):
     return [(i, (i + shift) % count) for i in range(count)]
 
 
-def pick_block(features):
-    block = features
-    while block > 1024 and block % 2 == 0:
-        block //= 2
-    return block
+def in_hbm(array):
+    return pltpu.with_memory_space_constraint(array, pltpu.HBM)
 
 
 def split_squares(total, lanes):
@@ -39,9 +42,19 @@
     )
 
 
-def project_kernel(axis_size, block, slots, index_ref, tokens_ref, gain_ref, weight_ref, *rest):
+def project_kernel(axis_size, block, slots, index_ref, tokens_hbm, gain_hbm, weight_ref, *rest):
     outs, rest = rest[:axis_size], rest[axis_size:]
-    hidden_ref, spread_ref, total_ref, sum_ref, gain_wide, buffer, arrived = rest
+    (
+        hidden_ref,
+        spread_ref,
+        total_ref,
+        sum_ref,
+        gain_wide,
+        tokens_ref,
+        gain_ref,
+        buffer,
+        arrived,
+    ) = rest
     total_rows, pair_rows, features = tokens_ref.shape
     token_count = total_rows * pair_rows
     pairs, mix, head_dim = weight_ref.shape[1:]
@@ -54,6 +67,12 @@
             weight_ref.at[pl.ds(step * block, block)], buffer.at[slot], arrived.at[slot]
         )
 
+    early = [
+        pltpu.make_async_copy(tokens_hbm, tokens_ref, arrived.at[slots]),
+        pltpu.make_async_copy(gain_hbm, gain_ref, arrived.at[slots + 1]),
+    ]
+    for copy in early:
+        copy.start()
     for step in range(min(slots, steps)):
         fetch(step, step).start()
 
@@ -63,6 +82,8 @@
     repeat = (column // mix == place).astype(jnp.bfloat16)
     member_of = lax.rem(lax.broadcasted_iota(jnp.int32, (token_count, wide), 1), mix)
     members = [(member_of == m).astype(jnp.bfloat16) for m in range(mix)]
+    for copy in early:
+        copy.wait()
     gain_wide[...] = gain_ref[...].astype(jnp.float32)
     squares = jnp.zeros((token_count, lanes), jnp.float32)
     group = 4
@@ -89,8 +110,8 @@
         slot = lax.rem(step, slots)
         fetch(step, slot).wait()
         left = spread_ref.at[:, pl.ds(pl.multiple_of(step * block * mix, 128), block * mix)]
-        for first in range(0, pairs, 4):
-            count = min(4, pairs - first)
+        for first in range(0, pairs, PAIR_GROUP):
+            count = min(PAIR_GROUP, pairs - first)
             weights = [
                 buffer[slot, :, first + i].reshape(block * mix, head_dim) for i in range(count)
             ]
@@ -133,9 +154,9 @@
         functools.partial(project_kernel, axis_size, block, slots),
         in_specs=[
             pl.BlockSpec(memory_space=pltpu.SMEM),
-            pl.BlockSpec(memory_space=pltpu.VMEM),
-            pl.BlockSpec(memory_space=pltpu.VMEM),
-            pl.BlockSpec(memory_space=pl.ANY),
+            pl.BlockSpec(memory_space=pltpu.HBM),
+            pl.BlockSpec(memory_space=pltpu.HBM),
+            pl.BlockSpec(memory_space=pltpu.HBM),
         ],
         out_specs=[pl.BlockSpec(memory_space=pltpu.VMEM)] * axis_size,
         scratch_shapes=[
@@ -144,8 +165,10 @@
             pltpu.VMEM((mix * token_count, pairs * head_dim), jnp.float32),
             pltpu.VMEM((token_count, 128), jnp.float32),
             pltpu.VMEM((features // 128, 128), jnp.float32),
+            pltpu.VMEM(tokens.shape, tokens.dtype),
+            pltpu.VMEM((features // 128, 128), norm_gain.dtype),
             pltpu.VMEM((slots, block, pairs, mix, head_dim), jnp.bfloat16),
-            pltpu.SemaphoreType.DMA((slots,)),
+            pltpu.SemaphoreType.DMA((slots + 2,)),
         ],
         out_shape=[
             jax.ShapeDtypeStruct((groups, rows, width), jnp.bfloat16 if s else jnp.float32)
@@ -158,7 +181,7 @@
             transcendentals=0,
         ),
         name="project",
-    )(index, tokens, norm_gain.reshape(-1, 128), weight)
+    )(index, *[in_hbm(array) for array in (tokens, norm_gain.reshape(-1, 128), weight)])
 
 
 SMEM = pl.BlockSpec(memory_space=pltpu.SMEM)
@@ -170,7 +193,7 @@
 
 
 def finish_kernel(
-    width_devices, head_devices, token_size, head_dim, index_ref, cosine_ref, sine_ref, *rest
+    width_devices, head_devices, token_size, head_dim, index_ref, _, cosine_ref, sine_ref, *rest
 ):
     parts, rest = rest[:width_devices], rest[width_devices:]
     outs, (turned_ref, piece_ref) = rest[:head_devices], rest[head_devices:]
@@ -208,13 +231,13 @@
             outs[shift][g] = piece_ref[...].astype(jnp.bfloat16)
 
 
-def finish(parts, cosine, sine, index, head_devices, token_size, head_dim):
+def finish(parts, cosine, sine, early, index, head_devices, token_size, head_dim):
     groups, rows, width = parts[0].shape
     heads = width // head_dim - 1
     piece_rows = (heads - 2) * token_size + 2 * (-(-token_size // 16) * 16)
     return pl.pallas_call(
         functools.partial(finish_kernel, len(parts), head_devices, token_size, head_dim),
-        in_specs=[SMEM] + [VMEM] * (2 + len(parts)),
+        in_specs=[SMEM, pl.BlockSpec(memory_space=pl.ANY)] + [VMEM] * (2 + len(parts)),
         out_specs=[VMEM] * head_devices,
         out_shape=[jax.ShapeDtypeStruct((groups, piece_rows, head_dim), jnp.bfloat16)]
         * head_devices,
@@ -224,11 +247,13 @@
         ],
         compiler_params=pltpu.CompilerParams(vmem_limit_bytes=SMALL_LIMIT),
         name="finish",
-    )(index, cosine, sine, *parts)
+    )(index, early, cosine, sine, *parts)
 
 
 def attend_kernel(head_devices, query_rows, index_ref, length_ref, cache_ref, *rest):
-    pieces, outs = rest[:head_devices], rest[head_devices:]
+    pieces, rest = rest[:head_devices], rest[head_devices:]
+    outs, rest = rest[:head_devices], rest[head_devices:]
+    old_ref, new_ref, old_weight_ref, new_weight_ref = rest
     groups, piece_rows, head_dim = pieces[0].shape
     rows_local, _, _, slots, _ = cache_ref.shape
     pad = (piece_rows - query_rows) // 2
@@ -245,46 +270,61 @@
     causal = (other // 2 == token // 2) & (other <= token)
     row_out = lax.rem(lax.broadcasted_iota(jnp.int32, (query_rows, head_dim), 0), token_size) // 2
     last = (((1,), (1,)), ((), ()))
+    jobs = []
     for shift in range(head_devices):
         source = wrap(index_ref[1] + head_devices - shift, head_devices)
-        for g in range(groups):
-            group = source * groups + g
-            queries = pieces[shift][g, :query_rows, :]
-            key_new = pieces[shift][g, query_rows : query_rows + pad, :]
-            value_new = pieces[shift][g, query_rows + pad :, :]
-            old = None
-            for r in range(rows_local):
-                term = lax.dot_general(
-                    queries, cache_ref[r, 0, group], last, preferred_element_type=jnp.float32
-                )
-                old = term if old is None else jnp.where(token_old // 2 == r, term, old)
-            old = jnp.where(visible, old * scale, -1e30)
-            new = lax.dot_general(queries, key_new, last, preferred_element_type=jnp.float32)
-            new = jnp.where(causal, new * scale, -1e30)
-            highest = jnp.maximum(
-                jnp.max(old, axis=1, keepdims=True), jnp.max(new, axis=1, keepdims=True)
+        jobs += [(shift, g, source * groups + g) for g in range(groups)]
+    for job, (shift, g, group) in enumerate(jobs):
+        queries = pieces[shift][g, :query_rows, :]
+        old = None
+        for r in range(rows_local):
+            term = lax.dot_general(
+                queries, cache_ref[r, 0, group], last, preferred_element_type=jnp.float32
             )
-            old = jnp.exp(old - highest)
-            new = jnp.exp(new - highest)
-            total = jnp.sum(old, axis=1, keepdims=True) + jnp.sum(new, axis=1, keepdims=True)
-            old = (old / total).astype(jnp.bfloat16)
-            new = (new / total).astype(jnp.bfloat16)
-            attended = None
-            for r in range(rows_local):
-                term = jnp.dot(old, cache_ref[r, 1, group], preferred_element_type=jnp.float32)
-                attended = term if attended is None else jnp.where(row_out == r, term, attended)
-            attended = attended + jnp.dot(new, value_new, preferred_element_type=jnp.float32)
-            outs[shift][g] = attended.astype(jnp.bfloat16)
+            old = term if old is None else jnp.where(token_old // 2 == r, term, old)
+        old_ref[job] = jnp.where(visible, old * scale, -1e30)
+        key_new = pieces[shift][g, query_rows : query_rows + pad, :]
+        new = lax.dot_general(queries, key_new, last, preferred_element_type=jnp.float32)
+        new_ref[job] = jnp.where(causal, new * scale, -1e30)
+    old = old_ref[...]
+    new = new_ref[...]
+    highest = jnp.maximum(
+        jnp.max(old, axis=2, keepdims=True), jnp.max(new, axis=2, keepdims=True)
+    )
+    old = jnp.exp(old - highest)
+    new = jnp.exp(new - highest)
+    total = jnp.sum(old, axis=2, keepdims=True) + jnp.sum(new, axis=2, keepdims=True)
+    inverse = 1.0 / total
+    old_weight_ref[...] = (old * inverse).astype(jnp.bfloat16)
+    new_weight_ref[...] = (new * inverse).astype(jnp.bfloat16)
+    for job, (shift, g, group) in enumerate(jobs):
+        attended = None
+        for r in range(rows_local):
+            term = jnp.dot(
+                old_weight_ref[job], cache_ref[r, 1, group], preferred_element_type=jnp.float32
+            )
+            attended = term if attended is None else jnp.where(row_out == r, term, attended)
+        value_new = pieces[shift][g, query_rows + pad :, :]
+        attended = attended + jnp.dot(
+            new_weight_ref[job], value_new, preferred_element_type=jnp.float32
+        )
+        outs[shift][g] = attended.astype(jnp.bfloat16)
 
 
 def attend(pieces, cache, lengths, index, query_rows):
-    groups, _, head_dim = pieces[0].shape
+    groups, piece_rows, head_dim = pieces[0].shape
+    slots, pad = cache.shape[3], (piece_rows - query_rows) // 2
     return pl.pallas_call(
         functools.partial(attend_kernel, len(pieces), query_rows),
         in_specs=[SMEM, SMEM] + [VMEM] * (1 + len(pieces)),
         out_specs=[VMEM] * len(pieces),
         out_shape=[jax.ShapeDtypeStruct((groups, query_rows, head_dim), jnp.bfloat16)]
         * len(pieces),
+        scratch_shapes=[
+            pltpu.VMEM((len(pieces) * groups, query_rows, count), kind)
+            for kind in (jnp.float32, jnp.bfloat16)
+            for count in (slots, pad)
+        ],
         compiler_params=pltpu.CompilerParams(vmem_limit_bytes=SMALL_LIMIT),
         name="attend",
     )(index, lengths, cache, *pieces)
@@ -323,88 +363,143 @@
     )(index, *pieces)
 
 
-def outward_kernel(block_count, axis_size, index_ref, *rest):
-    blocks, weight_ref, rest = rest[:block_count], rest[block_count], rest[block_count + 1 :]
-    outs, (left_ref, total_ref) = rest[:axis_size], rest[axis_size:]
+def hold_kernel(first, after_ref, through_ref, source_ref, held_ref, same_ref, arrived):
+    rows = pl.ds(first, held_ref.shape[0])
+    copy = pltpu.make_async_copy(source_ref.at[rows], held_ref, arrived)
+    copy.start()
+    copy.wait()
+
+
+def hold(source, first, count, after, through):
+    return pl.pallas_call(
+        functools.partial(hold_kernel, first),
+        in_specs=[pl.BlockSpec(memory_space=space) for space in (pl.ANY, pl.ANY, pltpu.HBM)],
+        out_specs=[VMEM, pl.BlockSpec(memory_space=pl.ANY)],
+        out_shape=[
+            pltpu.VMEM((count, source.shape[1]), source.dtype),
+            jax.ShapeDtypeStruct(through.shape, through.dtype),
+        ],
+        input_output_aliases={1: 1},
+        scratch_shapes=[pltpu.SemaphoreType.DMA],
+        compiler_params=pltpu.CompilerParams(vmem_limit_bytes=2**20),
+        cost_estimate=pl.CostEstimate(
+            flops=0, bytes_accessed=count * source.shape[1] * 2, transcendentals=0
+        ),
+        name="hold",
+    )(after, through, in_hbm(source))
+
+
+def outward_kernel(block_count, axis_size, begin, held_count, index_ref, weight_ref, *rest):
+    held, rest = rest[:held_count], rest[held_count:]
+    blocks, rest = rest[:block_count], rest[block_count:]
+    outs, (left_ref, total_ref, buffer, arrived) = rest[:axis_size], rest[axis_size:]
     token_count, depth = left_ref.shape
     size = token_count // block_count
-
-    @pl.when(pl.program_id(0) == 0)
-    def _():
-        for shift in range(block_count):
-            source = wrap(index_ref[0] + block_count - shift, block_count)
-            left_ref[pl.ds(pl.multiple_of(source * size, size), size), :] = blocks[shift][...]
-
-    rows = token_count // axis_size
-    step = pick_block(depth)
-    for k in range(0, depth, step):
+    slots, step, width = buffer.shape
+    kept = sum(part.shape[0] for part in held)
+    steps = (depth - kept) // step
+
+    def fetch(k, slot):
+        return pltpu.make_async_copy(
+            weight_ref.at[pl.ds(kept + k * step, step), pl.ds(begin, width)],
+            buffer.at[slot],
+            arrived.at[slot],
+        )
+
+    for k in range(min(slots, steps)):
+        fetch(k, k).start()
+    for shift in range(block_count):
+        source = wrap(index_ref[0] + block_count - shift, block_count)
+        left_ref[pl.ds(pl.multiple_of(source * size, size), size), :] = blocks[shift][...]
+    first = 0
+    for part in held:
         term = jnp.dot(
-            left_ref[:, k : k + step],
-            weight_ref[k : k + step, :],
+            left_ref[:, first : first + part.shape[0]],
+            part[:, begin : begin + width],
             preferred_element_type=jnp.float32,
         )
-        if k == 0:
+        if first == 0:
             total_ref[...] = term
         else:
             total_ref[...] += term
+        first += part.shape[0]
+
+    @pl.loop(0, steps)
+    def _(k):
+        slot = lax.rem(k, slots)
+        fetch(k, slot).wait()
+        total_ref[...] += jnp.dot(
+            left_ref[:, pl.ds(pl.multiple_of(kept + k * step, step), step)],
+            buffer[slot],
+            preferred_element_type=jnp.float32,
+        )
+
+        @pl.when(k + slots < steps)
+        def _():
+            fetch(k + slots, slot).start()
+
+    rows = token_count // axis_size
     for shift in range(axis_size):
         first = pl.multiple_of(wrap(index_ref[1] + shift, axis_size) * rows, rows)
         outs[shift][...] = total_ref[pl.ds(first, rows), :].astype(outs[shift].dtype)
 
 
-def outward(blocks, weight, axis_size, index):
+def outward(blocks, weight, held, begin, width, axis_size, index):
     size, depth = blocks[0].shape
     token_count = size * len(blocks)
-    width = weight.shape[1]
-    block = pick_block(width)
     rows = token_count // axis_size
-    return pl.pallas_call(
-        functools.partial(outward_kernel, len(blocks), axis_size),
-        grid=(width // block,),
-        in_specs=[SMEM]
-        + [VMEM] * len(blocks)
-        + [pl.BlockSpec((depth, block), lambda j: (0, j))],
-        out_specs=[pl.BlockSpec((rows, block), lambda j: (0, j))] * axis_size,
+    step = math.gcd(depth - sum(part.shape[0] for part in held), OUTWARD_STEP)
+    return pl.pallas_call(
+        functools.partial(outward_kernel, len(blocks), axis_size, begin, len(held)),
+        in_specs=[SMEM, pl.BlockSpec(memory_space=pltpu.HBM)] + [VMEM] * (len(held) + len(blocks)),
+        out_specs=[VMEM] * axis_size,
         scratch_shapes=[
             pltpu.VMEM((token_count, depth), jnp.bfloat16),
-            pltpu.VMEM((token_count, block), jnp.float32),
+            pltpu.VMEM((token_count, width), jnp.float32),
+            pltpu.VMEM((OUTWARD_SLOTS, step, width), weight.dtype),
+            pltpu.SemaphoreType.DMA((OUTWARD_SLOTS,)),
         ],
         out_shape=[
             jax.ShapeDtypeStruct((rows, width), jnp.bfloat16 if s else jnp.float32)
             for s in range(axis_size)
         ],
-        compiler_params=pltpu.CompilerParams(vmem_limit_bytes=48 * 2**20),
+        compiler_params=pltpu.CompilerParams(vmem_limit_bytes=OUTWARD_LIMIT),
         cost_estimate=pl.CostEstimate(
-            flops=2 * weight.size * token_count,
-            bytes_accessed=weight.size * 2,
+            flops=2 * depth * width * token_count,
+            bytes_accessed=2 * depth * width,
             transcendentals=0,
         ),
         name="outward",
-    )(index, *blocks, weight)
-
-
-def close_kernel(index_ref, tokens_ref, *rest):
+    )(
+        index,
+        in_hbm(weight),
+        *[pltpu.with_memory_space_constraint(part, pltpu.VMEM) for part in held],
+        *blocks,
+    )
+
+
+def close_kernel(count, index_ref, tokens_ref, *rest):
     parts, out_ref = rest[:-1], rest[-1]
     rows, tokens, _ = out_ref.shape
     lanes = 128
-    width = parts[0].shape[1]
-    for lane in range(0, out_ref.shape[2], lanes):
-        column, at = lane // width, lane % width
-        total = None
-        for part in parts[column * len(parts) * width // out_ref.shape[2] :][
-            : len(parts) * width // out_ref.shape[2]
-        ]:
-            term = part[:, at : at + lanes].astype(jnp.float32)
-            total = term if total is None else total + term
-        residual = tokens_ref[:, :, lane : lane + lanes].astype(jnp.float32)
-        out_ref[:, :, lane : lane + lanes] = residual + total.reshape(rows, tokens, lanes)
+    begin = 0
+    for span in range(0, len(parts), count):
+        width = parts[span].shape[1]
+        for lane in range(0, width, lanes):
+            total = parts[span][:, lane : lane + lanes]
+            for part in parts[span + 1 : span + count]:
+                total = total + part[:, lane : lane + lanes].astype(jnp.float32)
+            at = begin + lane
+            residual = tokens_ref[:, :, at : at + lanes].astype(jnp.float32)
+            out_ref[:, :, at : at + lanes] = residual + total.reshape(rows, tokens, lanes)
+        begin += width
 
 
 def close(tokens, parts, head_devices, index):
     rows = tokens.shape[0] // head_devices
     shape = (rows,) + tokens.shape[1:]
     return pl.pallas_call(
-        close_kernel,
+        functools.partial(close_kernel, head_devices),
         grid_spec=pltpu.PrefetchScalarGridSpec(
             num_scalar_prefetch=1,
             grid=(1,),
@@ -445,17 +540,36 @@
     sine = jnp.concatenate([-sine, sine], axis=1)
     cache = jnp.transpose(kv_cache, (0, 2, 3, 1, 4))
 
-    parts = project(tokens, norm_gain, qkv_weight, width_devices, index)
+    parts = list(project(tokens, norm_gain, qkv_weight, width_devices, index))
+    out_flat = out_weight.reshape(-1, local_width)
+    cuts = [0]
+    for share in HELD_SHARES:
+        cuts.append(cuts[-1] + out_flat.shape[0] * share // 16)
+    sizes = [end - begin for begin, end in zip(cuts, cuts[1:])]
+    held = []
     parts = exchange(parts, "gx")
-    pieces = finish(parts, cosine, sine, index, head_devices, token_size, head_dim)
+    pieces = list(
+        finish(parts, cosine, sine, cache, index, head_devices, token_size, head_dim)
+    )
+    if sizes[0]:
+        part, pieces[0] = hold(out_flat, cuts[0], sizes[0], pieces[1], pieces[0])
+        held.append(part)
     pieces = exchange(pieces, "gy")
-    attended = attend(pieces, cache, lengths, index, group_size * token_size)
+    attended = list(attend(pieces, cache, lengths, index, group_size * token_size))
+    if sizes[1]:
+        part, attended[0] = hold(out_flat, cuts[1], sizes[1], attended[1], attended[0])
+        held.append(part)
     attended = exchange(attended, "gy", -1)
     block = gather(attended, index, token_size)
+    part, late = hold(out_flat, cuts[2], sizes[2], block, index + 0)
+    held.append(part)
     blocks = exchange([block] * width_devices, "gx")
-    out_flat = out_weight.reshape(-1, local_width)
-    sums = outward(blocks, out_flat, head_devices, index)
-    return close(tokens, exchange(sums, "gy"), head_devices, index)
+    cut = local_width * OUTWARD_SHARE // 16 // 128 * 128
+    sums = []
+    for begin, end in ((0, cut), (cut, local_width)):
+        part = outward(blocks, out_flat, held, begin, end - begin, head_devices, late)
+        sums += exchange(part, "gy")
+    return close(tokens, sums, head_devices, index)
 
 
 def solution(mesh):

time: 86.1 us -> 77.9 us (0.905)
  waiting for transfers between devices: 25.8 us -> 9.17 us
  Pallas kernels: 36.6 us -> 41.7 us
  starting transfers between devices: 18.4 us -> 23.3 us
  local copies, waits for them, and re-layouts: 4.56 us -> 2.82 us
    ppermute x15 -> x18, waiting for transfers between devices: 25.8 us -> 9.17 us  [exchange(): lax.ppermute(pieces[s], axis, shift_pairs(count, sign * s))]
    pallas_call x2 -> x6, Pallas kernels: 14.1 us -> 21.4 us  [the longest x3 11.4 us: hold(): pl.pallas_call(functools.partial(hold_kernel, first), in_specs=[pl.BlockS...]
    ppermute x15 -> x18, starting transfers between devices: 18.4 us -> 23.3 us  [exchange(): lax.ppermute(pieces[s], axis, shift_pairs(count, sign * s))]
    pallas_call x1, Pallas kernels: 4.12 us -> 1.83 us  [attend(): pl.pallas_call(functools.partial(attend_kernel, len(pieces), query_rows),...]
    unnamed x11 -> x8, local copies, waits for them, and re-layouts: 4.45 us -> 2.71 us
  transfers between devices with their start and end apart: 15 -> 18, of which waited for: 13 -> 8; matrix products, arithmetic and copies ran while one was open for 4% -> 4% of each run, Pallas kernels for 0% -> 20%
where the time goes in v4:
time: 77.9 us; the launch traced here: 77.6 us
  Pallas kernels  41.7 us (54%)
  starting transfers between devices  23.3 us (30%)
  waiting for transfers between devices  9.17 us (12%)
  local copies, waits for them, and re-layouts  2.82 us (4%)
    ppermute x18, starting transfers between devices, exchange(): lax.ppermute(pieces[s], axis, shift_pairs(count, sign * s))  23.3 us
    pallas_call x1, Pallas kernels, project(): pl.pallas_call(functools.partial(project_kernel, axis_size, block, slots)...  16.9 us
    pallas_call x3, Pallas kernels, hold(): pl.pallas_call(functools.partial(hold_kernel, first), in_specs=[pl.BlockS...  11.4 us
    ppermute x18, waiting for transfers between devices, exchange(): lax.ppermute(pieces[s], axis, shift_pairs(count, sign * s))  9.17 us
    pallas_call x2, Pallas kernels, outward(): pl.pallas_call(functools.partial(outward_kernel, len(blocks), axis_size,...  8.6 us
    unnamed x8, local copies, waits for them, and re-layouts  2.71 us
    pallas_call x1, Pallas kernels, attend(): pl.pallas_call(functools.partial(attend_kernel, len(pieces), query_rows),...  1.83 us
  transfers between devices with their start and end apart: 18, of which 8 were waited for; matrix products, arithmetic and copies ran while one was open for 4% of the time, Pallas kernels for 20%

profile of v4, /device:TPU:0, one launch (start us, length us, event | category | flops | bytes accessed | tf_op | source)
XLA Modules:
  0.0 77.6 jit_solution(13607403306442024871)
XLA Ops:
  0.1 16.9 %project.1 = (f32[2,16,2432]{2,1,0:T(8,128)S(1)}, bf16[2,16,2432]{2,1,0:T(8,128)(2,1)S(1)}, bf16[2,16,2432]{2,1,0:T(8,128)(2,1)S(1)}, bf16[2,16,2432]{2,1,0:T(8,128)(2,1)S(1)}) custom-call(s32[2]{0:T(128)S(1)} %pad_add_fusion.index_ref, bf16[32,2,4096]{2,1,0:T(2,128)(2,1)} %tokens_ref.1, bf16[32,128]{1,0:T(8,128)(2,1)} %bitcast.18, ...), custom_call_target="tpu_custom_call" | custom-call | flops 2415919104 | bytes 37748736 | tf_op jit(solution)/shard_map/project/pallas_call | solution.py:153
  17.0 0.6 collective-permute-start
  17.5 2.5 %collective-permute-start.1 = (bf16[2,16,2432]{2,1,0:T(8,128)(2,1)S(1)}, bf16[2,16,2432]{2,1,0:T(8,128)(2,1)S(1)}, u32[]{:S(2)}, u32[]{:S(2)}) collective-permute-start(bf16[2,16,2432]{2,1,0:T(8,128)(2,1)S(1)} %get-tuple-element.33), channel_id=1, source_target_pairs={{0,8},{4,12},{8,0},{12,4},{1,9},{5,13},{9,1},{13,5},{2,10},{6,14},... | collective-permute-start | bytes 466952 | tf_op jit(solution)/shard_map/ppermute | solution.py:519
  20.1 1.4 %collective-permute-start.2 = (bf16[2,16,2432]{2,1,0:T(8,128)(2,1)S(1)}, bf16[2,16,2432]{2,1,0:T(8,128)(2,1)S(1)}, u32[]{:S(2)}, u32[]{:S(2)}) collective-permute-start(bf16[2,16,2432]{2,1,0:T(8,128)(2,1)S(1)} %get-tuple-element.34), channel_id=1, source_target_pairs={{0,12},{4,0},{8,4},{12,8},{1,13},{5,1},{9,5},{13,9},{2,14},{6,2},{... | collective-permute-start | bytes 466952 | tf_op jit(solution)/shard_map/ppermute | solution.py:519
  21.8 2.7 %copy.14 = bf16[2,384,2,8,128]{4,1,3,2,0:T(8,128)(2,1)S(1)} copy(bf16[2,384,2,8,128]{4,3,2,1,0:T(8,128)(2,1)} %param.11) | data formatting | bytes 6291456 | tf_op args[4]
  24.9 2.2 %collective-permute-done.2.rest_3_ = bf16[2,16,2432]{2,1,0:T(8,128)(2,1)S(1)} collective-permute-done((bf16[2,16,2432]{2,1,0:T(8,128)(2,1)S(1)}, bf16[2,16,2432]{2,1,0:T(8,128)(2,1)S(1)}, u32[]{:S(2)}, u32[]{:S(2)}) %collective-permute-start.2) | collective-permute-done | bytes 155680 | tf_op jit(solution)/shard_map/ppermute | solution.py:519
  27.2 1.0 %finish.1 = (bf16[2,96,128]{2,1,0:T(8,128)(2,1)S(1)}, bf16[2,96,128]{2,1,0:T(8,128)(2,1)S(1)}, bf16[2,96,128]{2,1,0:T(8,128)(2,1)S(1)}, bf16[2,96,128]{2,1,0:T(8,128)(2,1)S(1)}) custom-call(s32[2]{0:T(128)S(1)} %pad_add_fusion.index_ref, bf16[2,2,8,384,128]{4,3,2,1,0:T(8,128)(2,1)S(1)} %bitcast.10, f32[64,128]{1,0:T(8,128)S(1)} %get-tuple-element.60.cosine_ref, ...), custom_call_target="tpu_custom_call" | custom-call | tf_op jit(solution)/shard_map/finish/pallas_call | solution.py:238
  28.1 1.6 %collective-permute-start.3 = (bf16[2,96,128]{2,1,0:T(8,128)(2,1)S(1)}, bf16[2,96,128]{2,1,0:T(8,128)(2,1)S(1)}, u32[]{:S(2)}, u32[]{:S(2)}) collective-permute-start(bf16[2,96,128]{2,1,0:T(8,128)(2,1)S(1)} %get-tuple-element.35.after_ref), channel_id=1, source_target_pairs={{0,1},{1,2},{2,3},{3,0},{4,5},{5,6},{6,7},{7,4},{8,9},{9,10},{10,1... | collective-permute-start | bytes 147464 | tf_op jit(solution)/shard_map/ppermute | solution.py:519
  29.8 2.6 %collective-permute-start.4 = (bf16[2,96,128]{2,1,0:T(8,128)(2,1)S(1)}, bf16[2,96,128]{2,1,0:T(8,128)(2,1)S(1)}, u32[]{:S(2)}, u32[]{:S(2)}) collective-permute-start(bf16[2,96,128]{2,1,0:T(8,128)(2,1)S(1)} %get-tuple-element.38), channel_id=1, source_target_pairs={{0,2},{1,3},{2,0},{3,1},{4,6},{5,7},{6,4},{7,5},{8,10},{9,11},{10,... | collective-permute-start | bytes 147464 | tf_op jit(solution)/shard_map/ppermute | solution.py:519
  32.3 1.3 %collective-permute-start.5 = (bf16[2,96,128]{2,1,0:T(8,128)(2,1)S(1)}, bf16[2,96,128]{2,1,0:T(8,128)(2,1)S(1)}, u32[]{:S(2)}, u32[]{:S(2)}) collective-permute-start(bf16[2,96,128]{2,1,0:T(8,128)(2,1)S(1)} %get-tuple-element.39), channel_id=1, source_target_pairs={{0,3},{1,0},{2,1},{3,2},{4,7},{5,4},{6,5},{7,6},{8,11},{9,8},{10,9... | collective-permute-start | bytes 147464 | tf_op jit(solution)/shard_map/ppermute | solution.py:519
  33.7 3.4 %hold.3 = (bf16[1024,4096]{1,0:T(8,128)(2,1)S(1)}, bf16[2,96,128]{2,1,0:T(8,128)(2,1)S(1)}) custom-call(bf16[2,96,128]{2,1,0:T(8,128)(2,1)S(1)} %get-tuple-element.35.after_ref, bf16[2,96,128]{2,1,0:T(8,128)(2,1)S(1)} %get-tuple-element.36.through_ref, bf16[4096,4096]{1,0:T(8,128)(2,1)} %bitcast.12), custom_call_target="tpu_custom_call", output_to_operand_aliasing={{1}: (1, {})} | custom-call | bytes 8388608 | tf_op jit(solution)/shard_map/hold/pallas_call | solution.py:374
  37.1 1.8 %attend.1 = (bf16[2,64,128]{2,1,0:T(8,128)(2,1)S(1)}, bf16[2,64,128]{2,1,0:T(8,128)(2,1)S(1)}, bf16[2,64,128]{2,1,0:T(8,128)(2,1)S(1)}, bf16[2,64,128]{2,1,0:T(8,128)(2,1)S(1)}) custom-call(s32[2]{0:T(128)S(1)} %pad_add_fusion.index_ref, s32[2]{0:T(128)S(1)} %copy-done.1, bf16[2,2,8,384,128]{4,3,2,1,0:T(8,128)(2,1)S(1)} %bitcast.11, ...), custom_call_target="tpu_custom_call" | custom-call | tf_op jit(solution)/shard_map/attend/pallas_call | solution.py:317
  39.0 2.5 %collective-permute-start.6 = (bf16[2,64,128]{2,1,0:T(8,128)(2,1)S(1)}, bf16[2,64,128]{2,1,0:T(8,128)(2,1)S(1)}, u32[]{:S(2)}, u32[]{:S(2)}) collective-permute-start(bf16[2,64,128]{2,1,0:T(8,128)(2,1)S(1)} %get-tuple-element.40.after_ref), channel_id=1, source_target_pairs={{0,3},{1,0},{2,1},{3,2},{4,7},{5,4},{6,5},{7,6},{8,11},{9,8},{10,9... | collective-permute-start | bytes 98312 | tf_op jit(solution)/shard_map/ppermute | solution.py:519
  41.5 0.6 collective-permute-start.8
  42.1 3.4 %hold.4 = (bf16[1024,4096]{1,0:T(8,128)(2,1)S(1)}, bf16[2,64,128]{2,1,0:T(8,128)(2,1)S(1)}) custom-call(bf16[2,64,128]{2,1,0:T(8,128)(2,1)S(1)} %get-tuple-element.40.after_ref, bf16[2,64,128]{2,1,0:T(8,128)(2,1)S(1)} %get-tuple-element.41.through_ref, bf16[4096,4096]{1,0:T(8,128)(2,1)} %bitcast.13), custom_call_target="tpu_custom_call", output_to_operand_aliasing={{1}: (1, {})} | custom-call | bytes 8388608 | tf_op jit(solution)/shard_map/hold/pallas_call | solution.py:374
  45.5 0.8 collective-permute-done.7.rest_2_
  46.3 1.0 %collective-permute-done.8.rest_3_ = bf16[2,64,128]{2,1,0:T(8,128)(2,1)S(1)} collective-permute-done((bf16[2,64,128]{2,1,0:T(8,128)(2,1)S(1)}, bf16[2,64,128]{2,1,0:T(8,128)(2,1)S(1)}, u32[]{:S(2)}, u32[]{:S(2)}) %collective-permute-start.8) | collective-permute-done | bytes 32800 | tf_op jit(solution)/shard_map/ppermute | solution.py:519
  47.2 0.6 gather.1.after_ref.rest_3_
  47.9 0.8 collective-permute-start.10
  48.6 0.5 collective-permute-start.9
  49.1 4.6 %hold.5 = (bf16[1536,4096]{1,0:T(8,128)(2,1)S(1)}, s32[2]{0:T(128)S(1)}) custom-call(bf16[16,4096]{1,0:T(8,128)(2,1)S(1)} %gather.1.after_ref.rest_3_, s32[2]{0:T(128)S(1)} %copy.17.through_ref, bf16[4096,4096]{1,0:T(8,128)(2,1)} %bitcast.14), custom_call_target="tpu_custom_call", output_to_operand_aliasing={{1}: (1, {})} | custom-call | bytes 12582912 | tf_op jit(solution)/shard_map/hold/pallas_call | solution.py:374
  53.7 0.4 collective-permute-done.10.rest_5_
  54.4 4.3 %outward.3 = (f32[16,2048]{1,0:T(8,128)S(1)}, bf16[16,2048]{1,0:T(8,128)(2,1)S(1)}, bf16[16,2048]{1,0:T(8,128)(2,1)S(1)}, bf16[16,2048]{1,0:T(8,128)(2,1)S(1)}) custom-call(s32[2]{0:T(128)S(1)} %get-tuple-element.45.index_ref, bf16[4096,4096]{1,0:T(8,128)(2,1)} %bitcast.15, bf16[1024,4096]{1,0:T(8,128)(2,1)S(1)} %get-tuple-element.46.rest_0_, ...), custom_call_target="tpu_custom_call" | custom-call | flops 1073741824 | bytes 16777216 | tf_op jit(solution)/shard_map/outward/pallas_call | solution.py:452
  58.7 1.3 %collective-permute-start.15 = (bf16[16,2048]{1,0:T(8,128)(2,1)S(1)}, bf16[16,2048]{1,0:T(8,128)(2,1)S(1)}, u32[]{:S(2)}, u32[]{:S(2)}) collective-permute-start(bf16[16,2048]{1,0:T(8,128)(2,1)S(1)} %get-tuple-element.54), channel_id=1, source_target_pairs={{0,1},{1,2},{2,3},{3,0},{4,5},{5,6},{6,7},{7,4},{8,9},{9,10},{10,1... | collective-permute-start | bytes 196616 | tf_op jit(solution)/shard_map/ppermute | solution.py:519
  60.0 0.9 %collective-permute-start.16 = (bf16[16,2048]{1,0:T(8,128)(2,1)S(1)}, bf16[16,2048]{1,0:T(8,128)(2,1)S(1)}, u32[]{:S(2)}, u32[]{:S(2)}) collective-permute-start(bf16[16,2048]{1,0:T(8,128)(2,1)S(1)} %get-tuple-element.55), channel_id=1, source_target_pairs={{0,2},{1,3},{2,0},{3,1},{4,6},{5,7},{6,4},{7,5},{8,10},{9,11},{10,... | collective-permute-start | bytes 196616 | tf_op jit(solution)/shard_map/ppermute | solution.py:519
  60.9 1.9 %collective-permute-start.17 = (bf16[16,2048]{1,0:T(8,128)(2,1)S(1)}, bf16[16,2048]{1,0:T(8,128)(2,1)S(1)}, u32[]{:S(2)}, u32[]{:S(2)}) collective-permute-start(bf16[16,2048]{1,0:T(8,128)(2,1)S(1)} %get-tuple-element.56), channel_id=1, source_target_pairs={{0,3},{1,0},{2,1},{3,2},{4,7},{5,4},{6,5},{7,6},{8,11},{9,8},{10,9... | collective-permute-start | bytes 196616 | tf_op jit(solution)/shard_map/ppermute | solution.py:519
  62.8 4.3 %outward.2 = (f32[16,2048]{1,0:T(8,128)S(1)}, bf16[16,2048]{1,0:T(8,128)(2,1)S(1)}, bf16[16,2048]{1,0:T(8,128)(2,1)S(1)}, bf16[16,2048]{1,0:T(8,128)(2,1)S(1)}) custom-call(s32[2]{0:T(128)S(1)} %get-tuple-element.45.index_ref, bf16[4096,4096]{1,0:T(8,128)(2,1)} %bitcast.16, bf16[1024,4096]{1,0:T(8,128)(2,1)S(1)} %get-tuple-element.46.rest_0_, ...), custom_call_target="tpu_custom_call" | custom-call | flops 1073741824 | bytes 16777216 | tf_op jit(solution)/shard_map/outward/pallas_call | solution.py:452
  67.5 1.8 %collective-permute-start.13 = (bf16[16,2048]{1,0:T(8,128)(2,1)S(1)}, bf16[16,2048]{1,0:T(8,128)(2,1)S(1)}, u32[]{:S(2)}, u32[]{:S(2)}) collective-permute-start(bf16[16,2048]{1,0:T(8,128)(2,1)S(1)} %get-tuple-element.51), channel_id=1, source_target_pairs={{0,2},{1,3},{2,0},{3,1},{4,6},{5,7},{6,4},{7,5},{8,10},{9,11},{10,... | collective-permute-start | bytes 196616 | tf_op jit(solution)/shard_map/ppermute | solution.py:519
  69.3 2.6 %collective-permute-start.14 = (bf16[16,2048]{1,0:T(8,128)(2,1)S(1)}, bf16[16,2048]{1,0:T(8,128)(2,1)S(1)}, u32[]{:S(2)}, u32[]{:S(2)}) collective-permute-start(bf16[16,2048]{1,0:T(8,128)(2,1)S(1)} %get-tuple-element.52), channel_id=1, source_target_pairs={{0,3},{1,0},{2,1},{3,2},{4,7},{5,4},{6,5},{7,6},{8,11},{9,8},{10,9... | collective-permute-start | bytes 196616 | tf_op jit(solution)/shard_map/ppermute | solution.py:519
  71.9 2.1 %collective-permute-done.12.rest_1_ = bf16[16,2048]{1,0:T(8,128)(2,1)S(1)} collective-permute-done((bf16[16,2048]{1,0:T(8,128)(2,1)S(1)}, bf16[16,2048]{1,0:T(8,128)(2,1)S(1)}, u32[]{:S(2)}, u32[]{:S(2)}) %collective-permute-start.12) | collective-permute-done | bytes 65568 | tf_op jit(solution)/shard_map/ppermute | solution.py:519
  74.0 2.1 %collective-permute-done.13.rest_2_ = bf16[16,2048]{1,0:T(8,128)(2,1)S(1)} collective-permute-done((bf16[16,2048]{1,0:T(8,128)(2,1)S(1)}, bf16[16,2048]{1,0:T(8,128)(2,1)S(1)}, u32[]{:S(2)}, u32[]{:S(2)}) %collective-permute-start.13) | collective-permute-done | bytes 65568 | tf_op jit(solution)/shard_map/ppermute | solution.py:519
  76.2 1.4 %close.1 = f32[8,2,4096]{2,1,0:T(2,128)} custom-call(s32[2]{0:T(128)S(1)} %pad_add_fusion.index_ref, bf16[32,2,4096]{2,1,0:T(2,128)(2,1)S(1)} %copy-done, f32[16,2048]{1,0:T(8,128)S(1)} %get-tuple-element.49.rest_0_, bf16[16,2048]{1,0:T(8,128)(2,1)S(1)} %collective-permute-done.12.rest_1_, bf16[16,2048]{1,0:T(8,128)(2,1)S(1)} %collective-permute-done.13.rest_2_, ...), custom_call_target="tpu_custom_call" | custom-call | tf_op jit(solution)/shard_map/close/pallas_call | solution.py:501
  (28 shorter events, 1.6 us)
Async XLA Ops:
  0.1 21.4 %copy-start.2 = (s32[32]{0:T(128)S(1)}, s32[32]{0:T(128)}, u32[]{:S(2)}) copy-start(s32[32]{0:T(128)} %param.13) | copy-start | bytes 388
  17.0 7.7 %collective-permute-start = (bf16[2,16,2432]{2,1,0:T(8,128)(2,1)S(1)}, bf16[2,16,2432]{2,1,0:T(8,128)(2,1)S(1)}, u32[]{:S(2)}, u32[]{:S(2)}) collective-permute-start(bf16[2,16,2432]{2,1,0:T(8,128)(2,1)S(1)} %get-tuple-element.32), channel_id=1, source_target_pairs={{0,4},{4,8},{8,12},{12,0},{1,5},{5,9},{9,13},{13,1},{2,6},{6,10},{... | collective-permute-start | bytes 466952 | tf_op jit(solution)/shard_map/ppermute | solution.py:519
  17.5 7.4 %collective-permute-start.1 = (bf16[2,16,2432]{2,1,0:T(8,128)(2,1)S(1)}, bf16[2,16,2432]{2,1,0:T(8,128)(2,1)S(1)}, u32[]{:S(2)}, u32[]{:S(2)}) collective-permute-start(bf16[2,16,2432]{2,1,0:T(8,128)(2,1)S(1)} %get-tuple-element.33), channel_id=1, source_target_pairs={{0,8},{4,12},{8,0},{12,4},{1,9},{5,13},{9,1},{13,5},{2,10},{6,14},... | collective-permute-start | bytes 466952 | tf_op jit(solution)/shard_map/ppermute | solution.py:519
  20.1 7.1 %collective-permute-start.2 = (bf16[2,16,2432]{2,1,0:T(8,128)(2,1)S(1)}, bf16[2,16,2432]{2,1,0:T(8,128)(2,1)S(1)}, u32[]{:S(2)}, u32[]{:S(2)}) collective-permute-start(bf16[2,16,2432]{2,1,0:T(8,128)(2,1)S(1)} %get-tuple-element.34), channel_id=1, source_target_pairs={{0,12},{4,0},{8,4},{12,8},{1,13},{5,1},{9,5},{13,9},{2,14},{6,2},{... | collective-permute-start | bytes 466952 | tf_op jit(solution)/shard_map/ppermute | solution.py:519
  28.1 9.0 %collective-permute-start.3 = (bf16[2,96,128]{2,1,0:T(8,128)(2,1)S(1)}, bf16[2,96,128]{2,1,0:T(8,128)(2,1)S(1)}, u32[]{:S(2)}, u32[]{:S(2)}) collective-permute-start(bf16[2,96,128]{2,1,0:T(8,128)(2,1)S(1)} %get-tuple-element.35.after_ref), channel_id=1, source_target_pairs={{0,1},{1,2},{2,3},{3,0},{4,5},{5,6},{6,7},{7,4},{8,9},{9,10},{10,1... | collective-permute-start | bytes 147464 | tf_op jit(solution)/shard_map/ppermute | solution.py:519
  29.8 7.4 %collective-permute-start.4 = (bf16[2,96,128]{2,1,0:T(8,128)(2,1)S(1)}, bf16[2,96,128]{2,1,0:T(8,128)(2,1)S(1)}, u32[]{:S(2)}, u32[]{:S(2)}) collective-permute-start(bf16[2,96,128]{2,1,0:T(8,128)(2,1)S(1)} %get-tuple-element.38), channel_id=1, source_target_pairs={{0,2},{1,3},{2,0},{3,1},{4,6},{5,7},{6,4},{7,5},{8,10},{9,11},{10,... | collective-permute-start | bytes 147464 | tf_op jit(solution)/shard_map/ppermute | solution.py:519
  32.3 4.8 %collective-permute-start.5 = (bf16[2,96,128]{2,1,0:T(8,128)(2,1)S(1)}, bf16[2,96,128]{2,1,0:T(8,128)(2,1)S(1)}, u32[]{:S(2)}, u32[]{:S(2)}) collective-permute-start(bf16[2,96,128]{2,1,0:T(8,128)(2,1)S(1)} %get-tuple-element.39), channel_id=1, source_target_pairs={{0,3},{1,0},{2,1},{3,2},{4,7},{5,4},{6,5},{7,6},{8,11},{9,8},{10,9... | collective-permute-start | bytes 147464 | tf_op jit(solution)/shard_map/ppermute | solution.py:519
  33.7 3.4 %copy-start.1 = (s32[2]{0:T(128)S(1)}, s32[2]{0:T(128)}, u32[]{:S(2)}) copy-start(s32[2]{0:T(128)} %length_ref.1) | copy-start | bytes 28
  39.0 6.5 %collective-permute-start.6 = (bf16[2,64,128]{2,1,0:T(8,128)(2,1)S(1)}, bf16[2,64,128]{2,1,0:T(8,128)(2,1)S(1)}, u32[]{:S(2)}, u32[]{:S(2)}) collective-permute-start(bf16[2,64,128]{2,1,0:T(8,128)(2,1)S(1)} %get-tuple-element.40.after_ref), channel_id=1, source_target_pairs={{0,3},{1,0},{2,1},{3,2},{4,7},{5,4},{6,5},{7,6},{8,11},{9,8},{10,9... | collective-permute-start | bytes 98312 | tf_op jit(solution)/shard_map/ppermute | solution.py:519
  41.5 4.8 %collective-permute-start.7 = (bf16[2,64,128]{2,1,0:T(8,128)(2,1)S(1)}, bf16[2,64,128]{2,1,0:T(8,128)(2,1)S(1)}, u32[]{:S(2)}, u32[]{:S(2)}) collective-permute-start(bf16[2,64,128]{2,1,0:T(8,128)(2,1)S(1)} %get-tuple-element.43), channel_id=1, source_target_pairs={{0,2},{1,3},{2,0},{3,1},{4,6},{5,7},{6,4},{7,5},{8,10},{9,11},{10,... | collective-permute-start | bytes 98312 | tf_op jit(solution)/shard_map/ppermute | solution.py:519
  41.5 5.7 %collective-permute-start.8 = (bf16[2,64,128]{2,1,0:T(8,128)(2,1)S(1)}, bf16[2,64,128]{2,1,0:T(8,128)(2,1)S(1)}, u32[]{:S(2)}, u32[]{:S(2)}) collective-permute-start(bf16[2,64,128]{2,1,0:T(8,128)(2,1)S(1)} %get-tuple-element.44), channel_id=1, source_target_pairs={{0,1},{1,2},{2,3},{3,0},{4,5},{5,6},{6,7},{7,4},{8,9},{9,10},{10,1... | collective-permute-start | bytes 98312 | tf_op jit(solution)/shard_map/ppermute | solution.py:519
  47.9 6.3 %collective-permute-start.10 = (bf16[16,4096]{1,0:T(8,128)(2,1)S(1)}, bf16[16,4096]{1,0:T(8,128)(2,1)S(1)}, u32[]{:S(2)}, u32[]{:S(2)}) collective-permute-start(bf16[16,4096]{1,0:T(8,128)(2,1)S(1)} %gather.1.after_ref.rest_3_), channel_id=1, source_target_pairs={{0,8},{4,12},{8,0},{12,4},{1,9},{5,13},{9,1},{13,5},{2,10},{6,14},... | collective-permute-start | bytes 393224 | tf_op jit(solution)/shard_map/ppermute | solution.py:519
  48.6 5.6 %collective-permute-start.11 = (bf16[16,4096]{1,0:T(8,128)(2,1)S(1)}, bf16[16,4096]{1,0:T(8,128)(2,1)S(1)}, u32[]{:S(2)}, u32[]{:S(2)}) collective-permute-start(bf16[16,4096]{1,0:T(8,128)(2,1)S(1)} %gather.1.after_ref.rest_3_), channel_id=1, source_target_pairs={{0,12},{4,0},{8,4},{12,8},{1,13},{5,1},{9,5},{13,9},{2,14},{6,2},{... | collective-permute-start | bytes 393224 | tf_op jit(solution)/shard_map/ppermute | solution.py:519
  48.6 5.8 %collective-permute-start.9 = (bf16[16,4096]{1,0:T(8,128)(2,1)S(1)}, bf16[16,4096]{1,0:T(8,128)(2,1)S(1)}, u32[]{:S(2)}, u32[]{:S(2)}) collective-permute-start(bf16[16,4096]{1,0:T(8,128)(2,1)S(1)} %gather.1.after_ref.rest_3_), channel_id=1, source_target_pairs={{0,4},{4,8},{8,12},{12,0},{1,5},{5,9},{9,13},{13,1},{2,6},{6,10},{... | collective-permute-start | bytes 393224 | tf_op jit(solution)/shard_map/ppermute | solution.py:519
  58.7 10.6 %collective-permute-start.15 = (bf16[16,2048]{1,0:T(8,128)(2,1)S(1)}, bf16[16,2048]{1,0:T(8,128)(2,1)S(1)}, u32[]{:S(2)}, u32[]{:S(2)}) collective-permute-start(bf16[16,2048]{1,0:T(8,128)(2,1)S(1)} %get-tuple-element.54), channel_id=1, source_target_pairs={{0,1},{1,2},{2,3},{3,0},{4,5},{5,6},{6,7},{7,4},{8,9},{9,10},{10,1... | collective-permute-start | bytes 196616 | tf_op jit(solution)/shard_map/ppermute | solution.py:519
  60.0 11.9 %collective-permute-start.16 = (bf16[16,2048]{1,0:T(8,128)(2,1)S(1)}, bf16[16,2048]{1,0:T(8,128)(2,1)S(1)}, u32[]{:S(2)}, u32[]{:S(2)}) collective-permute-start(bf16[16,2048]{1,0:T(8,128)(2,1)S(1)} %get-tuple-element.55), channel_id=1, source_target_pairs={{0,2},{1,3},{2,0},{3,1},{4,6},{5,7},{6,4},{7,5},{8,10},{9,11},{10,... | collective-permute-start | bytes 196616 | tf_op jit(solution)/shard_map/ppermute | solution.py:519
  60.9 15.3 %copy-start = (bf16[32,2,4096]{2,1,0:T(2,128)(2,1)S(1)}, bf16[32,2,4096]{2,1,0:T(2,128)(2,1)}, u32[]{:S(2)}) copy-start(bf16[32,2,4096]{2,1,0:T(2,128)(2,1)} %tokens_ref.1) | copy-start | bytes 1572868
  60.9 11.0 %collective-permute-start.17 = (bf16[16,2048]{1,0:T(8,128)(2,1)S(1)}, bf16[16,2048]{1,0:T(8,128)(2,1)S(1)}, u32[]{:S(2)}, u32[]{:S(2)}) collective-permute-start(bf16[16,2048]{1,0:T(8,128)(2,1)S(1)} %get-tuple-element.56), channel_id=1, source_target_pairs={{0,3},{1,0},{2,1},{3,2},{4,7},{5,4},{6,5},{7,6},{8,11},{9,8},{10,9... | collective-permute-start | bytes 196616 | tf_op jit(solution)/shard_map/ppermute | solution.py:519
  67.1 6.9 %collective-permute-start.12 = (bf16[16,2048]{1,0:T(8,128)(2,1)S(1)}, bf16[16,2048]{1,0:T(8,128)(2,1)S(1)}, u32[]{:S(2)}, u32[]{:S(2)}) collective-permute-start(bf16[16,2048]{1,0:T(8,128)(2,1)S(1)} %get-tuple-element.50), channel_id=1, source_target_pairs={{0,1},{1,2},{2,3},{3,0},{4,5},{5,6},{6,7},{7,4},{8,9},{9,10},{10,1... | collective-permute-start | bytes 196616 | tf_op jit(solution)/shard_map/ppermute | solution.py:519
  67.5 8.6 %collective-permute-start.13 = (bf16[16,2048]{1,0:T(8,128)(2,1)S(1)}, bf16[16,2048]{1,0:T(8,128)(2,1)S(1)}, u32[]{:S(2)}, u32[]{:S(2)}) collective-permute-start(bf16[16,2048]{1,0:T(8,128)(2,1)S(1)} %get-tuple-element.51), channel_id=1, source_target_pairs={{0,2},{1,3},{2,0},{3,1},{4,6},{5,7},{6,4},{7,5},{8,10},{9,11},{10,... | collective-permute-start | bytes 196616 | tf_op jit(solution)/shard_map/ppermute | solution.py:519
  69.3 6.9 %collective-permute-start.14 = (bf16[16,2048]{1,0:T(8,128)(2,1)S(1)}, bf16[16,2048]{1,0:T(8,128)(2,1)S(1)}, u32[]{:S(2)}, u32[]{:S(2)}) collective-permute-start(bf16[16,2048]{1,0:T(8,128)(2,1)S(1)} %get-tuple-element.52), channel_id=1, source_target_pairs={{0,3},{1,0},{2,1},{3,2},{4,7},{5,4},{6,5},{7,6},{8,11},{9,8},{10,9... | collective-permute-start | bytes 196616 | tf_op jit(solution)/shard_map/ppermute | solution.py:519

commit v5 on v4

--- a/solution.py
+++ b/solution.py
@@ -17,10 +17,9 @@
 PROJECT_SLOTS = 3
 SMALL_LIMIT = 12 * 2**20
 OUTWARD_SHARE = 8
-OUTWARD_STEP = 512
-OUTWARD_SLOTS = 6
-OUTWARD_LIMIT = 20 * 2**20
-HELD_SHARES = (4, 4, 6)
+OUTWARD_STEP = 1024
+OUTWARD_LIMIT = 12 * 2**20
+HELD_SHARES = (2, 4, 2, 7)
 PAIR_GROUP = 4
 
 
@@ -395,19 +394,19 @@
     outs, (left_ref, total_ref, buffer, arrived) = rest[:axis_size], rest[axis_size:]
     token_count, depth = left_ref.shape
     size = token_count // block_count
-    slots, step, width = buffer.shape
+    steps, step, width = buffer.shape
     kept = sum(part.shape[0] for part in held)
-    steps = (depth - kept) // step
-
-    def fetch(k, slot):
-        return pltpu.make_async_copy(
+
+    copies = [
+        pltpu.make_async_copy(
             weight_ref.at[pl.ds(kept + k * step, step), pl.ds(begin, width)],
-            buffer.at[slot],
-            arrived.at[slot],
+            buffer.at[k],
+            arrived.at[k],
         )
-
-    for k in range(min(slots, steps)):
-        fetch(k, k).start()
+        for k in range(steps)
+    ]
+    for copy in copies:
+        copy.start()
     for shift in range(block_count):
         source = wrap(index_ref[0] + block_count - shift, block_count)
         left_ref[pl.ds(pl.multiple_of(source * size, size), size), :] = blocks[shift][...]
@@ -424,20 +423,13 @@
             total_ref[...] += term
         first += part.shape[0]
 
-    @pl.loop(0, steps)
-    def _(k):
-        slot = lax.rem(k, slots)
-        fetch(k, slot).wait()
+    for k in range(steps):
+        copies[k].wait()
         total_ref[...] += jnp.dot(
-            left_ref[:, pl.ds(pl.multiple_of(kept + k * step, step), step)],
-            buffer[slot],
+            left_ref[:, first + k * step : first + (k + 1) * step],
+            buffer[k],
             preferred_element_type=jnp.float32,
         )
-
-        @pl.when(k + slots < steps)
-        def _():
-            fetch(k + slots, slot).start()
-
     rows = token_count // axis_size
     for shift in range(axis_size):
         first = pl.multiple_of(wrap(index_ref[1] + shift, axis_size) * rows, rows)
@@ -448,7 +440,9 @@
     size, depth = blocks[0].shape
     token_count = size * len(blocks)
     rows = token_count // axis_size
-    step = math.gcd(depth - sum(part.shape[0] for part in held), OUTWARD_STEP)
+    streamed = depth - sum(part.shape[0] for part in held)
+    steps = -(-streamed // OUTWARD_STEP)
+    step = streamed // steps
     return pl.pallas_call(
         functools.partial(outward_kernel, len(blocks), axis_size, begin, len(held)),
         in_specs=[SMEM, pl.BlockSpec(memory_space=pltpu.HBM)] + [VMEM] * (len(held) + len(blocks)),
@@ -456,8 +450,8 @@
         scratch_shapes=[
             pltpu.VMEM((token_count, depth), jnp.bfloat16),
             pltpu.VMEM((token_count, width), jnp.float32),
-            pltpu.VMEM((OUTWARD_SLOTS, step, width), weight.dtype),
-            pltpu.SemaphoreType.DMA((OUTWARD_SLOTS,)),
+            pltpu.VMEM((steps, step, width), weight.dtype),
+            pltpu.SemaphoreType.DMA((steps,)),
         ],
         out_shape=[
             jax.ShapeDtypeStruct((rows, width), jnp.bfloat16 if s else jnp.float32)
@@ -547,22 +541,24 @@
         cuts.append(cuts[-1] + out_flat.shape[0] * share // 16)
     sizes = [end - begin for begin, end in zip(cuts, cuts[1:])]
     held = []
+
+    def hold_beside(window, after, through):
+        part, through = hold(out_flat, cuts[window], sizes[window], after, through)
+        held.append(part)
+        return through
+
+    parts[0] = hold_beside(0, parts[1], parts[0])
     parts = exchange(parts, "gx")
     pieces = list(
         finish(parts, cosine, sine, cache, index, head_devices, token_size, head_dim)
     )
-    if sizes[0]:
-        part, pieces[0] = hold(out_flat, cuts[0], sizes[0], pieces[1], pieces[0])
-        held.append(part)
+    pieces[0] = hold_beside(1, pieces[1], pieces[0])
     pieces = exchange(pieces, "gy")
     attended = list(attend(pieces, cache, lengths, index, group_size * token_size))
-    if sizes[1]:
-        part, attended[0] = hold(out_flat, cuts[1], sizes[1], attended[1], attended[0])
-        held.append(part)
+    attended[0] = hold_beside(2, attended[1], attended[0])
     attended = exchange(attended, "gy", -1)
     block = gather(attended, index, token_size)
-    part, late = hold(out_flat, cuts[2], sizes[2], block, index + 0)
-    held.append(part)
+    late = hold_beside(3, block, index + 0)
     blocks = exchange([block] * width_devices, "gx")
     cut = local_width * OUTWARD_SHARE // 16 // 128 * 128
     sums = []

time: 77.9 us -> 76.4 us (0.981)
  waiting for transfers between devices: 9.17 us -> 7.54 us
    ppermute x18, waiting for transfers between devices: 9.17 us -> 7.54 us  [exchange(): lax.ppermute(pieces[s], axis, shift_pairs(count, sign * s))]
    pallas_call x3 -> x4, Pallas kernels: 11.4 us -> 13 us  [hold(): pl.pallas_call(functools.partial(hold_kernel, first), in_specs=[pl.BlockS...]
    pallas_call x2, Pallas kernels: 8.6 us -> 7.5 us  [outward(): pl.pallas_call(functools.partial(outward_kernel, len(blocks), axis_size,...]
  transfers between devices with their start and end apart: 18 -> 18, of which waited for: 8 -> 6; matrix products, arithmetic and copies ran while one was open for 4% -> 4% of each run, Pallas kernels for 20% -> 22%
where the time goes in v5:
time: 76.4 us; the launch traced here: 76.1 us
  Pallas kernels  41.8 us (55%)
  starting transfers between devices  23.3 us (30%)
  waiting for transfers between devices  7.54 us (10%)
  local copies, waits for them, and re-layouts  2.82 us (4%)
    ppermute x18, starting transfers between devices, exchange(): lax.ppermute(pieces[s], axis, shift_pairs(count, sign * s))  23.3 us
    pallas_call x1, Pallas kernels, project(): pl.pallas_call(functools.partial(project_kernel, axis_size, block, slots)...  16.5 us
    pallas_call x4, Pallas kernels, hold(): pl.pallas_call(functools.partial(hold_kernel, first), in_specs=[pl.BlockS...  13 us
    ppermute x18, waiting for transfers between devices, exchange(): lax.ppermute(pieces[s], axis, shift_pairs(count, sign * s))  7.54 us
    pallas_call x2, Pallas kernels, outward(): pl.pallas_call(functools.partial(outward_kernel, len(blocks), axis_size,...  7.5 us
    unnamed x8, local copies, waits for them, and re-layouts  2.71 us
    pallas_call x1, Pallas kernels, attend(): pl.pallas_call(functools.partial(attend_kernel, len(pieces), query_rows),...  1.83 us
  transfers between devices with their start and end apart: 18, of which 6 were waited for; matrix products, arithmetic and copies ran while one was open for 4% of the time, Pallas kernels for 22%

profile of v5, /device:TPU:0, one launch (start us, length us, event | category | flops | bytes accessed | tf_op | source)
XLA Modules:
  0.0 76.1 jit_solution(933672326188985404)
XLA Ops:
  0.1 16.5 %project.1 = (f32[2,16,2432]{2,1,0:T(8,128)S(1)}, bf16[2,16,2432]{2,1,0:T(8,128)(2,1)S(1)}, bf16[2,16,2432]{2,1,0:T(8,128)(2,1)S(1)}, bf16[2,16,2432]{2,1,0:T(8,128)(2,1)S(1)}) custom-call(s32[2]{0:T(128)S(1)} %pad_add_fusion.index_ref, bf16[32,2,4096]{2,1,0:T(2,128)(2,1)} %tokens_ref.1, bf16[32,128]{1,0:T(8,128)(2,1)} %bitcast.19, ...), custom_call_target="tpu_custom_call" | custom-call | flops 2415919104 | bytes 37748736 | tf_op jit(solution)/shard_map/project/pallas_call | solution.py:152
  16.6 0.5 collective-permute-start
  17.0 2.6 %collective-permute-start.1 = (bf16[2,16,2432]{2,1,0:T(8,128)(2,1)S(1)}, bf16[2,16,2432]{2,1,0:T(8,128)(2,1)S(1)}, u32[]{:S(2)}, u32[]{:S(2)}) collective-permute-start(bf16[2,16,2432]{2,1,0:T(8,128)(2,1)S(1)} %get-tuple-element.36), channel_id=1, source_target_pairs={{0,8},{4,12},{8,0},{12,4},{1,9},{5,13},{9,1},{13,5},{2,10},{6,14},... | collective-permute-start | bytes 466952 | tf_op jit(solution)/shard_map/ppermute | solution.py:513
  19.7 1.4 %collective-permute-start.2 = (bf16[2,16,2432]{2,1,0:T(8,128)(2,1)S(1)}, bf16[2,16,2432]{2,1,0:T(8,128)(2,1)S(1)}, u32[]{:S(2)}, u32[]{:S(2)}) collective-permute-start(bf16[2,16,2432]{2,1,0:T(8,128)(2,1)S(1)} %get-tuple-element.37), channel_id=1, source_target_pairs={{0,12},{4,0},{8,4},{12,8},{1,13},{5,1},{9,5},{13,9},{2,14},{6,2},{... | collective-permute-start | bytes 466952 | tf_op jit(solution)/shard_map/ppermute | solution.py:513
  21.5 2.7 %copy.15 = bf16[2,384,2,8,128]{4,1,3,2,0:T(8,128)(2,1)S(1)} copy(bf16[2,384,2,8,128]{4,3,2,1,0:T(8,128)(2,1)} %param.11) | data formatting | bytes 6291456 | tf_op args[4]
  24.2 2.2 %hold.4 = (bf16[512,4096]{1,0:T(8,128)(2,1)S(1)}, f32[2,16,2432]{2,1,0:T(8,128)S(1)}) custom-call(bf16[2,16,2432]{2,1,0:T(8,128)(2,1)S(1)} %get-tuple-element.33.after_ref, f32[2,16,2432]{2,1,0:T(8,128)S(1)} %get-tuple-element.34.through_ref, bf16[4096,4096]{1,0:T(8,128)(2,1)} %bitcast.12), custom_call_target="tpu_custom_call", output_to_operand_aliasing={{1}: (1, {})} | custom-call | bytes 4194304 | tf_op jit(solution)/shard_map/hold/pallas_call | solution.py:373
  26.5 0.3 collective-permute-done.2.rest_3_
  26.8 1.0 %finish.1 = (bf16[2,96,128]{2,1,0:T(8,128)(2,1)S(1)}, bf16[2,96,128]{2,1,0:T(8,128)(2,1)S(1)}, bf16[2,96,128]{2,1,0:T(8,128)(2,1)S(1)}, bf16[2,96,128]{2,1,0:T(8,128)(2,1)S(1)}) custom-call(s32[2]{0:T(128)S(1)} %pad_add_fusion.index_ref, bf16[2,2,8,384,128]{4,3,2,1,0:T(8,128)(2,1)S(1)} %bitcast.10, f32[64,128]{1,0:T(8,128)S(1)} %get-tuple-element.64.cosine_ref, ...), custom_call_target="tpu_custom_call" | custom-call | tf_op jit(solution)/shard_map/finish/pallas_call | solution.py:237
  27.7 1.7 %collective-permute-start.3 = (bf16[2,96,128]{2,1,0:T(8,128)(2,1)S(1)}, bf16[2,96,128]{2,1,0:T(8,128)(2,1)S(1)}, u32[]{:S(2)}, u32[]{:S(2)}) collective-permute-start(bf16[2,96,128]{2,1,0:T(8,128)(2,1)S(1)} %get-tuple-element.38.after_ref), channel_id=1, source_target_pairs={{0,1},{1,2},{2,3},{3,0},{4,5},{5,6},{6,7},{7,4},{8,9},{9,10},{10,1... | collective-permute-start | bytes 147464 | tf_op jit(solution)/shard_map/ppermute | solution.py:513
  29.4 2.5 %collective-permute-start.4 = (bf16[2,96,128]{2,1,0:T(8,128)(2,1)S(1)}, bf16[2,96,128]{2,1,0:T(8,128)(2,1)S(1)}, u32[]{:S(2)}, u32[]{:S(2)}) collective-permute-start(bf16[2,96,128]{2,1,0:T(8,128)(2,1)S(1)} %get-tuple-element.41), channel_id=1, source_target_pairs={{0,2},{1,3},{2,0},{3,1},{4,6},{5,7},{6,4},{7,5},{8,10},{9,11},{10,... | collective-permute-start | bytes 147464 | tf_op jit(solution)/shard_map/ppermute | solution.py:513
  31.9 1.3 %collective-permute-start.5 = (bf16[2,96,128]{2,1,0:T(8,128)(2,1)S(1)}, bf16[2,96,128]{2,1,0:T(8,128)(2,1)S(1)}, u32[]{:S(2)}, u32[]{:S(2)}) collective-permute-start(bf16[2,96,128]{2,1,0:T(8,128)(2,1)S(1)} %get-tuple-element.42), channel_id=1, source_target_pairs={{0,3},{1,0},{2,1},{3,2},{4,7},{5,4},{6,5},{7,6},{8,11},{9,8},{10,9... | collective-permute-start | bytes 147464 | tf_op jit(solution)/shard_map/ppermute | solution.py:513
  33.3 3.4 %hold.5 = (bf16[1024,4096]{1,0:T(8,128)(2,1)S(1)}, bf16[2,96,128]{2,1,0:T(8,128)(2,1)S(1)}) custom-call(bf16[2,96,128]{2,1,0:T(8,128)(2,1)S(1)} %get-tuple-element.38.after_ref, bf16[2,96,128]{2,1,0:T(8,128)(2,1)S(1)} %get-tuple-element.39.through_ref, bf16[4096,4096]{1,0:T(8,128)(2,1)} %bitcast.13), custom_call_target="tpu_custom_call", output_to_operand_aliasing={{1}: (1, {})} | custom-call | bytes 8388608 | tf_op jit(solution)/shard_map/hold/pallas_call | solution.py:373
  36.7 1.8 %attend.1 = (bf16[2,64,128]{2,1,0:T(8,128)(2,1)S(1)}, bf16[2,64,128]{2,1,0:T(8,128)(2,1)S(1)}, bf16[2,64,128]{2,1,0:T(8,128)(2,1)S(1)}, bf16[2,64,128]{2,1,0:T(8,128)(2,1)S(1)}) custom-call(s32[2]{0:T(128)S(1)} %pad_add_fusion.index_ref, s32[2]{0:T(128)S(1)} %copy-done.1, bf16[2,2,8,384,128]{4,3,2,1,0:T(8,128)(2,1)S(1)} %bitcast.11, ...), custom_call_target="tpu_custom_call" | custom-call | tf_op jit(solution)/shard_map/attend/pallas_call | solution.py:316
  38.6 2.5 %collective-permute-start.6 = (bf16[2,64,128]{2,1,0:T(8,128)(2,1)S(1)}, bf16[2,64,128]{2,1,0:T(8,128)(2,1)S(1)}, u32[]{:S(2)}, u32[]{:S(2)}) collective-permute-start(bf16[2,64,128]{2,1,0:T(8,128)(2,1)S(1)} %get-tuple-element.43.after_ref), channel_id=1, source_target_pairs={{0,3},{1,0},{2,1},{3,2},{4,7},{5,4},{6,5},{7,6},{8,11},{9,8},{10,9... | collective-permute-start | bytes 98312 | tf_op jit(solution)/shard_map/ppermute | solution.py:513
  41.1 0.6 collective-permute-start.8
  41.7 2.2 %hold.6 = (bf16[512,4096]{1,0:T(8,128)(2,1)S(1)}, bf16[2,64,128]{2,1,0:T(8,128)(2,1)S(1)}) custom-call(bf16[2,64,128]{2,1,0:T(8,128)(2,1)S(1)} %get-tuple-element.43.after_ref, bf16[2,64,128]{2,1,0:T(8,128)(2,1)S(1)} %get-tuple-element.44.through_ref, bf16[4096,4096]{1,0:T(8,128)(2,1)} %bitcast.14), custom_call_target="tpu_custom_call", output_to_operand_aliasing={{1}: (1, {})} | custom-call | bytes 4194304 | tf_op jit(solution)/shard_map/hold/pallas_call | solution.py:373
  43.9 2.0 %collective-permute-done.7.rest_2_ = bf16[2,64,128]{2,1,0:T(8,128)(2,1)S(1)} collective-permute-done((bf16[2,64,128]{2,1,0:T(8,128)(2,1)S(1)}, bf16[2,64,128]{2,1,0:T(8,128)(2,1)S(1)}, u32[]{:S(2)}, u32[]{:S(2)}) %collective-permute-start.7) | collective-permute-done | bytes 32800 | tf_op jit(solution)/shard_map/ppermute | solution.py:513
  45.9 1.0 %collective-permute-done.8.rest_3_ = bf16[2,64,128]{2,1,0:T(8,128)(2,1)S(1)} collective-permute-done((bf16[2,64,128]{2,1,0:T(8,128)(2,1)S(1)}, bf16[2,64,128]{2,1,0:T(8,128)(2,1)S(1)}, u32[]{:S(2)}, u32[]{:S(2)}) %collective-permute-start.8) | collective-permute-done | bytes 32800 | tf_op jit(solution)/shard_map/ppermute | solution.py:513
  46.8 0.6 gather.1.after_ref.rest_4_
  47.5 0.8 %collective-permute-start.10 = (bf16[16,4096]{1,0:T(8,128)(2,1)S(1)}, bf16[16,4096]{1,0:T(8,128)(2,1)S(1)}, u32[]{:S(2)}, u32[]{:S(2)}) collective-permute-start(bf16[16,4096]{1,0:T(8,128)(2,1)S(1)} %gather.1.after_ref.rest_4_), channel_id=1, source_target_pairs={{0,8},{4,12},{8,0},{12,4},{1,9},{5,13},{9,1},{13,5},{2,10},{6,14},... | collective-permute-start | bytes 393224 | tf_op jit(solution)/shard_map/ppermute | solution.py:513
  48.2 0.5 collective-permute-start.9
  48.7 5.2 %hold.7 = (bf16[1792,4096]{1,0:T(8,128)(2,1)S(1)}, s32[2]{0:T(128)S(1)}) custom-call(bf16[16,4096]{1,0:T(8,128)(2,1)S(1)} %gather.1.after_ref.rest_4_, s32[2]{0:T(128)S(1)} %copy.19.through_ref, bf16[4096,4096]{1,0:T(8,128)(2,1)} %bitcast.15), custom_call_target="tpu_custom_call", output_to_operand_aliasing={{1}: (1, {})} | custom-call | bytes 14680064 | tf_op jit(solution)/shard_map/hold/pallas_call | solution.py:373
  54.0 3.8 %outward.3 = (f32[16,2048]{1,0:T(8,128)S(1)}, bf16[16,2048]{1,0:T(8,128)(2,1)S(1)}, bf16[16,2048]{1,0:T(8,128)(2,1)S(1)}, bf16[16,2048]{1,0:T(8,128)(2,1)S(1)}) custom-call(s32[2]{0:T(128)S(1)} %get-tuple-element.48.index_ref, bf16[4096,4096]{1,0:T(8,128)(2,1)} %bitcast.16, bf16[512,4096]{1,0:T(8,128)(2,1)S(1)} %get-tuple-element.49.rest_0_, ...), custom_call_target="tpu_custom_call" | custom-call | flops 1073741824 | bytes 16777216 | tf_op jit(solution)/shard_map/outward/pallas_call | solution.py:446
  57.9 1.2 %collective-permute-start.16 = (bf16[16,2048]{1,0:T(8,128)(2,1)S(1)}, bf16[16,2048]{1,0:T(8,128)(2,1)S(1)}, u32[]{:S(2)}, u32[]{:S(2)}) collective-permute-start(bf16[16,2048]{1,0:T(8,128)(2,1)S(1)} %get-tuple-element.59), channel_id=1, source_target_pairs={{0,2},{1,3},{2,0},{3,1},{4,6},{5,7},{6,4},{7,5},{8,10},{9,11},{10,... | collective-permute-start | bytes 196616 | tf_op jit(solution)/shard_map/ppermute | solution.py:513
  59.0 2.8 %collective-permute-start.17 = (bf16[16,2048]{1,0:T(8,128)(2,1)S(1)}, bf16[16,2048]{1,0:T(8,128)(2,1)S(1)}, u32[]{:S(2)}, u32[]{:S(2)}) collective-permute-start(bf16[16,2048]{1,0:T(8,128)(2,1)S(1)} %get-tuple-element.60), channel_id=1, source_target_pairs={{0,3},{1,0},{2,1},{3,2},{4,7},{5,4},{6,5},{7,6},{8,11},{9,8},{10,9... | collective-permute-start | bytes 196616 | tf_op jit(solution)/shard_map/ppermute | solution.py:513
  61.9 3.8 %outward.2 = (f32[16,2048]{1,0:T(8,128)S(1)}, bf16[16,2048]{1,0:T(8,128)(2,1)S(1)}, bf16[16,2048]{1,0:T(8,128)(2,1)S(1)}, bf16[16,2048]{1,0:T(8,128)(2,1)S(1)}) custom-call(s32[2]{0:T(128)S(1)} %get-tuple-element.48.index_ref, bf16[4096,4096]{1,0:T(8,128)(2,1)} %bitcast.17, bf16[512,4096]{1,0:T(8,128)(2,1)S(1)} %get-tuple-element.49.rest_0_, ...), custom_call_target="tpu_custom_call" | custom-call | flops 1073741824 | bytes 16777216 | tf_op jit(solution)/shard_map/outward/pallas_call | solution.py:446
  65.7 0.4 collective-permute-start.12
  66.0 1.5 %collective-permute-start.13 = (bf16[16,2048]{1,0:T(8,128)(2,1)S(1)}, bf16[16,2048]{1,0:T(8,128)(2,1)S(1)}, u32[]{:S(2)}, u32[]{:S(2)}) collective-permute-start(bf16[16,2048]{1,0:T(8,128)(2,1)S(1)} %get-tuple-element.55), channel_id=1, source_target_pairs={{0,2},{1,3},{2,0},{3,1},{4,6},{5,7},{6,4},{7,5},{8,10},{9,11},{10,... | collective-permute-start | bytes 196616 | tf_op jit(solution)/shard_map/ppermute | solution.py:513
  67.6 2.8 %collective-permute-start.14 = (bf16[16,2048]{1,0:T(8,128)(2,1)S(1)}, bf16[16,2048]{1,0:T(8,128)(2,1)S(1)}, u32[]{:S(2)}, u32[]{:S(2)}) collective-permute-start(bf16[16,2048]{1,0:T(8,128)(2,1)S(1)} %get-tuple-element.56), channel_id=1, source_target_pairs={{0,3},{1,0},{2,1},{3,2},{4,7},{5,4},{6,5},{7,6},{8,11},{9,8},{10,9... | collective-permute-start | bytes 196616 | tf_op jit(solution)/shard_map/ppermute | solution.py:513
  70.4 2.1 %collective-permute-done.12.rest_1_ = bf16[16,2048]{1,0:T(8,128)(2,1)S(1)} collective-permute-done((bf16[16,2048]{1,0:T(8,128)(2,1)S(1)}, bf16[16,2048]{1,0:T(8,128)(2,1)S(1)}, u32[]{:S(2)}, u32[]{:S(2)}) %collective-permute-start.12) | collective-permute-done | bytes 65568 | tf_op jit(solution)/shard_map/ppermute | solution.py:513
  72.5 2.1 %collective-permute-done.13.rest_2_ = bf16[16,2048]{1,0:T(8,128)(2,1)S(1)} collective-permute-done((bf16[16,2048]{1,0:T(8,128)(2,1)S(1)}, bf16[16,2048]{1,0:T(8,128)(2,1)S(1)}, u32[]{:S(2)}, u32[]{:S(2)}) %collective-permute-start.13) | collective-permute-done | bytes 65568 | tf_op jit(solution)/shard_map/ppermute | solution.py:513
  74.7 1.4 %close.1 = f32[8,2,4096]{2,1,0:T(2,128)} custom-call(s32[2]{0:T(128)S(1)} %pad_add_fusion.index_ref, bf16[32,2,4096]{2,1,0:T(2,128)(2,1)S(1)} %copy-done, f32[16,2048]{1,0:T(8,128)S(1)} %get-tuple-element.53.rest_0_, bf16[16,2048]{1,0:T(8,128)(2,1)S(1)} %collective-permute-done.12.rest_1_, bf16[16,2048]{1,0:T(8,128)(2,1)S(1)} %collective-permute-done.13.rest_2_, ...), custom_call_target="tpu_custom_call" | custom-call | tf_op jit(solution)/shard_map/close/pallas_call | solution.py:495
  (29 shorter events, 0.8 us)
Async XLA Ops:
  0.1 21.0 %copy-start.2 = (s32[32]{0:T(128)S(1)}, s32[32]{0:T(128)}, u32[]{:S(2)}) copy-start(s32[32]{0:T(128)} %param.13) | copy-start | bytes 388
  16.6 9.9 %collective-permute-start = (bf16[2,16,2432]{2,1,0:T(8,128)(2,1)S(1)}, bf16[2,16,2432]{2,1,0:T(8,128)(2,1)S(1)}, u32[]{:S(2)}, u32[]{:S(2)}) collective-permute-start(bf16[2,16,2432]{2,1,0:T(8,128)(2,1)S(1)} %get-tuple-element.33.after_ref), channel_id=1, source_target_pairs={{0,4},{4,8},{8,12},{12,0},{1,5},{5,9},{9,13},{13,1},{2,6},{6,10},{... | collective-permute-start | bytes 466952 | tf_op jit(solution)/shard_map/ppermute | solution.py:513
  17.0 9.4 %collective-permute-start.1 = (bf16[2,16,2432]{2,1,0:T(8,128)(2,1)S(1)}, bf16[2,16,2432]{2,1,0:T(8,128)(2,1)S(1)}, u32[]{:S(2)}, u32[]{:S(2)}) collective-permute-start(bf16[2,16,2432]{2,1,0:T(8,128)(2,1)S(1)} %get-tuple-element.36), channel_id=1, source_target_pairs={{0,8},{4,12},{8,0},{12,4},{1,9},{5,13},{9,1},{13,5},{2,10},{6,14},... | collective-permute-start | bytes 466952 | tf_op jit(solution)/shard_map/ppermute | solution.py:513
  19.7 7.1 %collective-permute-start.2 = (bf16[2,16,2432]{2,1,0:T(8,128)(2,1)S(1)}, bf16[2,16,2432]{2,1,0:T(8,128)(2,1)S(1)}, u32[]{:S(2)}, u32[]{:S(2)}) collective-permute-start(bf16[2,16,2432]{2,1,0:T(8,128)(2,1)S(1)} %get-tuple-element.37), channel_id=1, source_target_pairs={{0,12},{4,0},{8,4},{12,8},{1,13},{5,1},{9,5},{13,9},{2,14},{6,2},{... | collective-permute-start | bytes 466952 | tf_op jit(solution)/shard_map/ppermute | solution.py:513
  27.7 9.0 %collective-permute-start.3 = (bf16[2,96,128]{2,1,0:T(8,128)(2,1)S(1)}, bf16[2,96,128]{2,1,0:T(8,128)(2,1)S(1)}, u32[]{:S(2)}, u32[]{:S(2)}) collective-permute-start(bf16[2,96,128]{2,1,0:T(8,128)(2,1)S(1)} %get-tuple-element.38.after_ref), channel_id=1, source_target_pairs={{0,1},{1,2},{2,3},{3,0},{4,5},{5,6},{6,7},{7,4},{8,9},{9,10},{10,1... | collective-permute-start | bytes 147464 | tf_op jit(solution)/shard_map/ppermute | solution.py:513
  29.4 7.3 %collective-permute-start.4 = (bf16[2,96,128]{2,1,0:T(8,128)(2,1)S(1)}, bf16[2,96,128]{2,1,0:T(8,128)(2,1)S(1)}, u32[]{:S(2)}, u32[]{:S(2)}) collective-permute-start(bf16[2,96,128]{2,1,0:T(8,128)(2,1)S(1)} %get-tuple-element.41), channel_id=1, source_target_pairs={{0,2},{1,3},{2,0},{3,1},{4,6},{5,7},{6,4},{7,5},{8,10},{9,11},{10,... | collective-permute-start | bytes 147464 | tf_op jit(solution)/shard_map/ppermute | solution.py:513
  31.9 4.8 %collective-permute-start.5 = (bf16[2,96,128]{2,1,0:T(8,128)(2,1)S(1)}, bf16[2,96,128]{2,1,0:T(8,128)(2,1)S(1)}, u32[]{:S(2)}, u32[]{:S(2)}) collective-permute-start(bf16[2,96,128]{2,1,0:T(8,128)(2,1)S(1)} %get-tuple-element.42), channel_id=1, source_target_pairs={{0,3},{1,0},{2,1},{3,2},{4,7},{5,4},{6,5},{7,6},{8,11},{9,8},{10,9... | collective-permute-start | bytes 147464 | tf_op jit(solution)/shard_map/ppermute | solution.py:513
  33.3 3.4 %copy-start.1 = (s32[2]{0:T(128)S(1)}, s32[2]{0:T(128)}, u32[]{:S(2)}) copy-start(s32[2]{0:T(128)} %length_ref.1) | copy-start | bytes 28
  38.6 5.3 %collective-permute-start.6 = (bf16[2,64,128]{2,1,0:T(8,128)(2,1)S(1)}, bf16[2,64,128]{2,1,0:T(8,128)(2,1)S(1)}, u32[]{:S(2)}, u32[]{:S(2)}) collective-permute-start(bf16[2,64,128]{2,1,0:T(8,128)(2,1)S(1)} %get-tuple-element.43.after_ref), channel_id=1, source_target_pairs={{0,3},{1,0},{2,1},{3,2},{4,7},{5,4},{6,5},{7,6},{8,11},{9,8},{10,9... | collective-permute-start | bytes 98312 | tf_op jit(solution)/shard_map/ppermute | solution.py:513
  41.1 4.8 %collective-permute-start.7 = (bf16[2,64,128]{2,1,0:T(8,128)(2,1)S(1)}, bf16[2,64,128]{2,1,0:T(8,128)(2,1)S(1)}, u32[]{:S(2)}, u32[]{:S(2)}) collective-permute-start(bf16[2,64,128]{2,1,0:T(8,128)(2,1)S(1)} %get-tuple-element.46), channel_id=1, source_target_pairs={{0,2},{1,3},{2,0},{3,1},{4,6},{5,7},{6,4},{7,5},{8,10},{9,11},{10,... | collective-permute-start | bytes 98312 | tf_op jit(solution)/shard_map/ppermute | solution.py:513
  41.1 5.7 %collective-permute-start.8 = (bf16[2,64,128]{2,1,0:T(8,128)(2,1)S(1)}, bf16[2,64,128]{2,1,0:T(8,128)(2,1)S(1)}, u32[]{:S(2)}, u32[]{:S(2)}) collective-permute-start(bf16[2,64,128]{2,1,0:T(8,128)(2,1)S(1)} %get-tuple-element.47), channel_id=1, source_target_pairs={{0,1},{1,2},{2,3},{3,0},{4,5},{5,6},{6,7},{7,4},{8,9},{9,10},{10,1... | collective-permute-start | bytes 98312 | tf_op jit(solution)/shard_map/ppermute | solution.py:513
  47.5 6.5 %collective-permute-start.10 = (bf16[16,4096]{1,0:T(8,128)(2,1)S(1)}, bf16[16,4096]{1,0:T(8,128)(2,1)S(1)}, u32[]{:S(2)}, u32[]{:S(2)}) collective-permute-start(bf16[16,4096]{1,0:T(8,128)(2,1)S(1)} %gather.1.after_ref.rest_4_), channel_id=1, source_target_pairs={{0,8},{4,12},{8,0},{12,4},{1,9},{5,13},{9,1},{13,5},{2,10},{6,14},... | collective-permute-start | bytes 393224 | tf_op jit(solution)/shard_map/ppermute | solution.py:513
  48.2 5.7 %collective-permute-start.11 = (bf16[16,4096]{1,0:T(8,128)(2,1)S(1)}, bf16[16,4096]{1,0:T(8,128)(2,1)S(1)}, u32[]{:S(2)}, u32[]{:S(2)}) collective-permute-start(bf16[16,4096]{1,0:T(8,128)(2,1)S(1)} %gather.1.after_ref.rest_4_), channel_id=1, source_target_pairs={{0,12},{4,0},{8,4},{12,8},{1,13},{5,1},{9,5},{13,9},{2,14},{6,2},{... | collective-permute-start | bytes 393224 | tf_op jit(solution)/shard_map/ppermute | solution.py:513
  48.2 5.8 %collective-permute-start.9 = (bf16[16,4096]{1,0:T(8,128)(2,1)S(1)}, bf16[16,4096]{1,0:T(8,128)(2,1)S(1)}, u32[]{:S(2)}, u32[]{:S(2)}) collective-permute-start(bf16[16,4096]{1,0:T(8,128)(2,1)S(1)} %gather.1.after_ref.rest_4_), channel_id=1, source_target_pairs={{0,4},{4,8},{8,12},{12,0},{1,5},{5,9},{9,13},{13,1},{2,6},{6,10},{... | collective-permute-start | bytes 393224 | tf_op jit(solution)/shard_map/ppermute | solution.py:513
  57.8 9.8 %collective-permute-start.15 = (bf16[16,2048]{1,0:T(8,128)(2,1)S(1)}, bf16[16,2048]{1,0:T(8,128)(2,1)S(1)}, u32[]{:S(2)}, u32[]{:S(2)}) collective-permute-start(bf16[16,2048]{1,0:T(8,128)(2,1)S(1)} %get-tuple-element.58), channel_id=1, source_target_pairs={{0,1},{1,2},{2,3},{3,0},{4,5},{5,6},{6,7},{7,4},{8,9},{9,10},{10,1... | collective-permute-start | bytes 196616 | tf_op jit(solution)/shard_map/ppermute | solution.py:513
  57.9 12.6 %collective-permute-start.16 = (bf16[16,2048]{1,0:T(8,128)(2,1)S(1)}, bf16[16,2048]{1,0:T(8,128)(2,1)S(1)}, u32[]{:S(2)}, u32[]{:S(2)}) collective-permute-start(bf16[16,2048]{1,0:T(8,128)(2,1)S(1)} %get-tuple-element.59), channel_id=1, source_target_pairs={{0,2},{1,3},{2,0},{3,1},{4,6},{5,7},{6,4},{7,5},{8,10},{9,11},{10,... | collective-permute-start | bytes 196616 | tf_op jit(solution)/shard_map/ppermute | solution.py:513
  59.0 15.6 %copy-start = (bf16[32,2,4096]{2,1,0:T(2,128)(2,1)S(1)}, bf16[32,2,4096]{2,1,0:T(2,128)(2,1)}, u32[]{:S(2)}) copy-start(bf16[32,2,4096]{2,1,0:T(2,128)(2,1)} %tokens_ref.1) | copy-start | bytes 1572868
  59.0 11.4 %collective-permute-start.17 = (bf16[16,2048]{1,0:T(8,128)(2,1)S(1)}, bf16[16,2048]{1,0:T(8,128)(2,1)S(1)}, u32[]{:S(2)}, u32[]{:S(2)}) collective-permute-start(bf16[16,2048]{1,0:T(8,128)(2,1)S(1)} %get-tuple-element.60), channel_id=1, source_target_pairs={{0,3},{1,0},{2,1},{3,2},{4,7},{5,4},{6,5},{7,6},{8,11},{9,8},{10,9... | collective-permute-start | bytes 196616 | tf_op jit(solution)/shard_map/ppermute | solution.py:513
  65.7 6.9 %collective-permute-start.12 = (bf16[16,2048]{1,0:T(8,128)(2,1)S(1)}, bf16[16,2048]{1,0:T(8,128)(2,1)S(1)}, u32[]{:S(2)}, u32[]{:S(2)}) collective-permute-start(bf16[16,2048]{1,0:T(8,128)(2,1)S(1)} %get-tuple-element.54), channel_id=1, source_target_pairs={{0,1},{1,2},{2,3},{3,0},{4,5},{5,6},{6,7},{7,4},{8,9},{9,10},{10,1... | collective-permute-start | bytes 196616 | tf_op jit(solution)/shard_map/ppermute | solution.py:513
  66.0 8.6 %collective-permute-start.13 = (bf16[16,2048]{1,0:T(8,128)(2,1)S(1)}, bf16[16,2048]{1,0:T(8,128)(2,1)S(1)}, u32[]{:S(2)}, u32[]{:S(2)}) collective-permute-start(bf16[16,2048]{1,0:T(8,128)(2,1)S(1)} %get-tuple-element.55), channel_id=1, source_target_pairs={{0,2},{1,3},{2,0},{3,1},{4,6},{5,7},{6,4},{7,5},{8,10},{9,11},{10,... | collective-permute-start | bytes 196616 | tf_op jit(solution)/shard_map/ppermute | solution.py:513
  67.6 7.1 %collective-permute-start.14 = (bf16[16,2048]{1,0:T(8,128)(2,1)S(1)}, bf16[16,2048]{1,0:T(8,128)(2,1)S(1)}, u32[]{:S(2)}, u32[]{:S(2)}) collective-permute-start(bf16[16,2048]{1,0:T(8,128)(2,1)S(1)} %get-tuple-element.56), channel_id=1, source_target_pairs={{0,3},{1,0},{2,1},{3,2},{4,7},{5,4},{6,5},{7,6},{8,11},{9,8},{10,9... | collective-permute-start | bytes 196616 | tf_op jit(solution)/shard_map/ppermute | solution.py:513

commit v6 on v5

--- a/solution.py
+++ b/solution.py
@@ -432,7 +432,7 @@
         )
     rows = token_count // axis_size
     for shift in range(axis_size):
-        first = pl.multiple_of(wrap(index_ref[1] + shift, axis_size) * rows, rows)
+        first = pl.multiple_of(wrap(index_ref[1] + axis_size - shift, axis_size) * rows, rows)
         outs[shift][...] = total_ref[pl.ds(first, rows), :].astype(outs[shift].dtype)
 
 
@@ -564,7 +564,7 @@
     sums = []
     for begin, end in ((0, cut), (cut, local_width)):
         part = outward(blocks, out_flat, held, begin, end - begin, head_devices, late)
-        sums += exchange(part, "gy")
+        sums += exchange(part, "gy", -1)
     return close(tokens, sums, head_devices, index)
 
 

time: 76.4 us -> 76 us (level)
  starting transfers between devices: 23.3 us -> 21.5 us
  waiting for transfers between devices: 7.54 us -> 8.92 us
    ppermute x18, starting transfers between devices: 23.3 us -> 21.5 us  [exchange(): lax.ppermute(pieces[s], axis, shift_pairs(count, sign * s))]
    ppermute x18, waiting for transfers between devices: 7.54 us -> 8.92 us  [exchange(): lax.ppermute(pieces[s], axis, shift_pairs(count, sign * s))]
where the time goes in v6:
time: 76 us; the launch traced here: 75.7 us
  Pallas kernels  41.8 us (55%)
  starting transfers between devices  21.5 us (28%)
  waiting for transfers between devices  8.92 us (12%)
  local copies, waits for them, and re-layouts  2.82 us (4%)
    ppermute x18, starting transfers between devices, exchange(): lax.ppermute(pieces[s], axis, shift_pairs(count, sign * s))  21.5 us
    pallas_call x1, Pallas kernels, project(): pl.pallas_call(functools.partial(project_kernel, axis_size, block, slots)...  16.5 us
    pallas_call x4, Pallas kernels, hold(): pl.pallas_call(functools.partial(hold_kernel, first), in_specs=[pl.BlockS...  13 us
    ppermute x18, waiting for transfers between devices, exchange(): lax.ppermute(pieces[s], axis, shift_pairs(count, sign * s))  8.92 us
    pallas_call x2, Pallas kernels, outward(): pl.pallas_call(functools.partial(outward_kernel, len(blocks), axis_size,...  7.5 us
    unnamed x8, local copies, waits for them, and re-layouts  2.71 us
    pallas_call x1, Pallas kernels, attend(): pl.pallas_call(functools.partial(attend_kernel, len(pieces), query_rows),...  1.83 us
  transfers between devices with their start and end apart: 18, of which 6 were waited for; matrix products, arithmetic and copies ran while one was open for 4% of the time, Pallas kernels for 22%

profile of v6, /device:TPU:0, one launch (start us, length us, event | category | flops | bytes accessed | tf_op | source)
XLA Modules:
  0.0 75.7 jit_solution(13452819121770085519)
XLA Ops:
  0.1 16.5 %project.1 = (f32[2,16,2432]{2,1,0:T(8,128)S(1)}, bf16[2,16,2432]{2,1,0:T(8,128)(2,1)S(1)}, bf16[2,16,2432]{2,1,0:T(8,128)(2,1)S(1)}, bf16[2,16,2432]{2,1,0:T(8,128)(2,1)S(1)}) custom-call(s32[2]{0:T(128)S(1)} %pad_add_fusion.index_ref, bf16[32,2,4096]{2,1,0:T(2,128)(2,1)} %tokens_ref.1, bf16[32,128]{1,0:T(8,128)(2,1)} %bitcast.19, ...), custom_call_target="tpu_custom_call" | custom-call | flops 2415919104 | bytes 37748736 | tf_op jit(solution)/shard_map/project/pallas_call | solution.py:152
  16.6 0.5 collective-permute-start
  17.0 2.6 %collective-permute-start.1 = (bf16[2,16,2432]{2,1,0:T(8,128)(2,1)S(1)}, bf16[2,16,2432]{2,1,0:T(8,128)(2,1)S(1)}, u32[]{:S(2)}, u32[]{:S(2)}) collective-permute-start(bf16[2,16,2432]{2,1,0:T(8,128)(2,1)S(1)} %get-tuple-element.36), channel_id=1, source_target_pairs={{0,8},{4,12},{8,0},{12,4},{1,9},{5,13},{9,1},{13,5},{2,10},{6,14},... | collective-permute-start | bytes 466952 | tf_op jit(solution)/shard_map/ppermute | solution.py:513
  19.7 1.4 %collective-permute-start.2 = (bf16[2,16,2432]{2,1,0:T(8,128)(2,1)S(1)}, bf16[2,16,2432]{2,1,0:T(8,128)(2,1)S(1)}, u32[]{:S(2)}, u32[]{:S(2)}) collective-permute-start(bf16[2,16,2432]{2,1,0:T(8,128)(2,1)S(1)} %get-tuple-element.37), channel_id=1, source_target_pairs={{0,12},{4,0},{8,4},{12,8},{1,13},{5,1},{9,5},{13,9},{2,14},{6,2},{... | collective-permute-start | bytes 466952 | tf_op jit(solution)/shard_map/ppermute | solution.py:513
  21.5 2.7 %copy.15 = bf16[2,384,2,8,128]{4,1,3,2,0:T(8,128)(2,1)S(1)} copy(bf16[2,384,2,8,128]{4,3,2,1,0:T(8,128)(2,1)} %param.11) | data formatting | bytes 6291456 | tf_op args[4]
  24.2 2.2 %hold.4 = (bf16[512,4096]{1,0:T(8,128)(2,1)S(1)}, f32[2,16,2432]{2,1,0:T(8,128)S(1)}) custom-call(bf16[2,16,2432]{2,1,0:T(8,128)(2,1)S(1)} %get-tuple-element.33.after_ref, f32[2,16,2432]{2,1,0:T(8,128)S(1)} %get-tuple-element.34.through_ref, bf16[4096,4096]{1,0:T(8,128)(2,1)} %bitcast.12), custom_call_target="tpu_custom_call", output_to_operand_aliasing={{1}: (1, {})} | custom-call | bytes 4194304 | tf_op jit(solution)/shard_map/hold/pallas_call | solution.py:373
  26.5 0.3 collective-permute-done.2.rest_3_
  26.8 1.0 %finish.1 = (bf16[2,96,128]{2,1,0:T(8,128)(2,1)S(1)}, bf16[2,96,128]{2,1,0:T(8,128)(2,1)S(1)}, bf16[2,96,128]{2,1,0:T(8,128)(2,1)S(1)}, bf16[2,96,128]{2,1,0:T(8,128)(2,1)S(1)}) custom-call(s32[2]{0:T(128)S(1)} %pad_add_fusion.index_ref, bf16[2,2,8,384,128]{4,3,2,1,0:T(8,128)(2,1)S(1)} %bitcast.10, f32[64,128]{1,0:T(8,128)S(1)} %get-tuple-element.64.cosine_ref, ...), custom_call_target="tpu_custom_call" | custom-call | tf_op jit(solution)/shard_map/finish/pallas_call | solution.py:237
  27.7 1.7 %collective-permute-start.3 = (bf16[2,96,128]{2,1,0:T(8,128)(2,1)S(1)}, bf16[2,96,128]{2,1,0:T(8,128)(2,1)S(1)}, u32[]{:S(2)}, u32[]{:S(2)}) collective-permute-start(bf16[2,96,128]{2,1,0:T(8,128)(2,1)S(1)} %get-tuple-element.38.after_ref), channel_id=1, source_target_pairs={{0,1},{1,2},{2,3},{3,0},{4,5},{5,6},{6,7},{7,4},{8,9},{9,10},{10,1... | collective-permute-start | bytes 147464 | tf_op jit(solution)/shard_map/ppermute | solution.py:513
  29.4 2.5 %collective-permute-start.4 = (bf16[2,96,128]{2,1,0:T(8,128)(2,1)S(1)}, bf16[2,96,128]{2,1,0:T(8,128)(2,1)S(1)}, u32[]{:S(2)}, u32[]{:S(2)}) collective-permute-start(bf16[2,96,128]{2,1,0:T(8,128)(2,1)S(1)} %get-tuple-element.41), channel_id=1, source_target_pairs={{0,2},{1,3},{2,0},{3,1},{4,6},{5,7},{6,4},{7,5},{8,10},{9,11},{10,... | collective-permute-start | bytes 147464 | tf_op jit(solution)/shard_map/ppermute | solution.py:513
  31.9 1.3 %collective-permute-start.5 = (bf16[2,96,128]{2,1,0:T(8,128)(2,1)S(1)}, bf16[2,96,128]{2,1,0:T(8,128)(2,1)S(1)}, u32[]{:S(2)}, u32[]{:S(2)}) collective-permute-start(bf16[2,96,128]{2,1,0:T(8,128)(2,1)S(1)} %get-tuple-element.42), channel_id=1, source_target_pairs={{0,3},{1,0},{2,1},{3,2},{4,7},{5,4},{6,5},{7,6},{8,11},{9,8},{10,9... | collective-permute-start | bytes 147464 | tf_op jit(solution)/shard_map/ppermute | solution.py:513
  33.3 3.4 %hold.5 = (bf16[1024,4096]{1,0:T(8,128)(2,1)S(1)}, bf16[2,96,128]{2,1,0:T(8,128)(2,1)S(1)}) custom-call(bf16[2,96,128]{2,1,0:T(8,128)(2,1)S(1)} %get-tuple-element.38.after_ref, bf16[2,96,128]{2,1,0:T(8,128)(2,1)S(1)} %get-tuple-element.39.through_ref, bf16[4096,4096]{1,0:T(8,128)(2,1)} %bitcast.13), custom_call_target="tpu_custom_call", output_to_operand_aliasing={{1}: (1, {})} | custom-call | bytes 8388608 | tf_op jit(solution)/shard_map/hold/pallas_call | solution.py:373
  36.7 1.8 %attend.1 = (bf16[2,64,128]{2,1,0:T(8,128)(2,1)S(1)}, bf16[2,64,128]{2,1,0:T(8,128)(2,1)S(1)}, bf16[2,64,128]{2,1,0:T(8,128)(2,1)S(1)}, bf16[2,64,128]{2,1,0:T(8,128)(2,1)S(1)}) custom-call(s32[2]{0:T(128)S(1)} %pad_add_fusion.index_ref, s32[2]{0:T(128)S(1)} %copy-done.1, bf16[2,2,8,384,128]{4,3,2,1,0:T(8,128)(2,1)S(1)} %bitcast.11, ...), custom_call_target="tpu_custom_call" | custom-call | tf_op jit(solution)/shard_map/attend/pallas_call | solution.py:316
  38.6 2.5 %collective-permute-start.6 = (bf16[2,64,128]{2,1,0:T(8,128)(2,1)S(1)}, bf16[2,64,128]{2,1,0:T(8,128)(2,1)S(1)}, u32[]{:S(2)}, u32[]{:S(2)}) collective-permute-start(bf16[2,64,128]{2,1,0:T(8,128)(2,1)S(1)} %get-tuple-element.43.after_ref), channel_id=1, source_target_pairs={{0,3},{1,0},{2,1},{3,2},{4,7},{5,4},{6,5},{7,6},{8,11},{9,8},{10,9... | collective-permute-start | bytes 98312 | tf_op jit(solution)/shard_map/ppermute | solution.py:513
  41.1 0.6 collective-permute-start.8
  41.7 2.2 %hold.6 = (bf16[512,4096]{1,0:T(8,128)(2,1)S(1)}, bf16[2,64,128]{2,1,0:T(8,128)(2,1)S(1)}) custom-call(bf16[2,64,128]{2,1,0:T(8,128)(2,1)S(1)} %get-tuple-element.43.after_ref, bf16[2,64,128]{2,1,0:T(8,128)(2,1)S(1)} %get-tuple-element.44.through_ref, bf16[4096,4096]{1,0:T(8,128)(2,1)} %bitcast.14), custom_call_target="tpu_custom_call", output_to_operand_aliasing={{1}: (1, {})} | custom-call | bytes 4194304 | tf_op jit(solution)/shard_map/hold/pallas_call | solution.py:373
  43.9 2.0 %collective-permute-done.7.rest_2_ = bf16[2,64,128]{2,1,0:T(8,128)(2,1)S(1)} collective-permute-done((bf16[2,64,128]{2,1,0:T(8,128)(2,1)S(1)}, bf16[2,64,128]{2,1,0:T(8,128)(2,1)S(1)}, u32[]{:S(2)}, u32[]{:S(2)}) %collective-permute-start.7) | collective-permute-done | bytes 32800 | tf_op jit(solution)/shard_map/ppermute | solution.py:513
  45.9 1.0 %collective-permute-done.8.rest_3_ = bf16[2,64,128]{2,1,0:T(8,128)(2,1)S(1)} collective-permute-done((bf16[2,64,128]{2,1,0:T(8,128)(2,1)S(1)}, bf16[2,64,128]{2,1,0:T(8,128)(2,1)S(1)}, u32[]{:S(2)}, u32[]{:S(2)}) %collective-permute-start.8) | collective-permute-done | bytes 32800 | tf_op jit(solution)/shard_map/ppermute | solution.py:513
  46.8 0.6 gather.1.after_ref.rest_4_
  47.5 0.8 %collective-permute-start.10 = (bf16[16,4096]{1,0:T(8,128)(2,1)S(1)}, bf16[16,4096]{1,0:T(8,128)(2,1)S(1)}, u32[]{:S(2)}, u32[]{:S(2)}) collective-permute-start(bf16[16,4096]{1,0:T(8,128)(2,1)S(1)} %gather.1.after_ref.rest_4_), channel_id=1, source_target_pairs={{0,8},{4,12},{8,0},{12,4},{1,9},{5,13},{9,1},{13,5},{2,10},{6,14},... | collective-permute-start | bytes 393224 | tf_op jit(solution)/shard_map/ppermute | solution.py:513
  48.2 0.5 collective-permute-start.9
  48.7 5.2 %hold.7 = (bf16[1792,4096]{1,0:T(8,128)(2,1)S(1)}, s32[2]{0:T(128)S(1)}) custom-call(bf16[16,4096]{1,0:T(8,128)(2,1)S(1)} %gather.1.after_ref.rest_4_, s32[2]{0:T(128)S(1)} %copy.19.through_ref, bf16[4096,4096]{1,0:T(8,128)(2,1)} %bitcast.15), custom_call_target="tpu_custom_call", output_to_operand_aliasing={{1}: (1, {})} | custom-call | bytes 14680064 | tf_op jit(solution)/shard_map/hold/pallas_call | solution.py:373
  54.0 3.8 %outward.3 = (f32[16,2048]{1,0:T(8,128)S(1)}, bf16[16,2048]{1,0:T(8,128)(2,1)S(1)}, bf16[16,2048]{1,0:T(8,128)(2,1)S(1)}, bf16[16,2048]{1,0:T(8,128)(2,1)S(1)}) custom-call(s32[2]{0:T(128)S(1)} %get-tuple-element.48.index_ref, bf16[4096,4096]{1,0:T(8,128)(2,1)} %bitcast.16, bf16[512,4096]{1,0:T(8,128)(2,1)S(1)} %get-tuple-element.49.rest_0_, ...), custom_call_target="tpu_custom_call" | custom-call | flops 1073741824 | bytes 16777216 | tf_op jit(solution)/shard_map/outward/pallas_call | solution.py:446
  57.8 0.6 collective-permute-start.15
  58.4 0.9 %collective-permute-start.16 = (bf16[16,2048]{1,0:T(8,128)(2,1)S(1)}, bf16[16,2048]{1,0:T(8,128)(2,1)S(1)}, u32[]{:S(2)}, u32[]{:S(2)}) collective-permute-start(bf16[16,2048]{1,0:T(8,128)(2,1)S(1)} %get-tuple-element.59), channel_id=1, source_target_pairs={{0,2},{1,3},{2,0},{3,1},{4,6},{5,7},{6,4},{7,5},{8,10},{9,11},{10,... | collective-permute-start | bytes 196616 | tf_op jit(solution)/shard_map/ppermute | solution.py:513
  59.3 1.7 %collective-permute-start.17 = (bf16[16,2048]{1,0:T(8,128)(2,1)S(1)}, bf16[16,2048]{1,0:T(8,128)(2,1)S(1)}, u32[]{:S(2)}, u32[]{:S(2)}) collective-permute-start(bf16[16,2048]{1,0:T(8,128)(2,1)S(1)} %get-tuple-element.60), channel_id=1, source_target_pairs={{0,1},{1,2},{2,3},{3,0},{4,5},{5,6},{6,7},{7,4},{8,9},{9,10},{10,1... | collective-permute-start | bytes 196616 | tf_op jit(solution)/shard_map/ppermute | solution.py:513
  61.0 3.7 %outward.2 = (f32[16,2048]{1,0:T(8,128)S(1)}, bf16[16,2048]{1,0:T(8,128)(2,1)S(1)}, bf16[16,2048]{1,0:T(8,128)(2,1)S(1)}, bf16[16,2048]{1,0:T(8,128)(2,1)S(1)}) custom-call(s32[2]{0:T(128)S(1)} %get-tuple-element.48.index_ref, bf16[4096,4096]{1,0:T(8,128)(2,1)} %bitcast.17, bf16[512,4096]{1,0:T(8,128)(2,1)S(1)} %get-tuple-element.49.rest_0_, ...), custom_call_target="tpu_custom_call" | custom-call | flops 1073741824 | bytes 16777216 | tf_op jit(solution)/shard_map/outward/pallas_call | solution.py:446
  64.8 2.2 %collective-permute-start.12 = (bf16[16,2048]{1,0:T(8,128)(2,1)S(1)}, bf16[16,2048]{1,0:T(8,128)(2,1)S(1)}, u32[]{:S(2)}, u32[]{:S(2)}) collective-permute-start(bf16[16,2048]{1,0:T(8,128)(2,1)S(1)} %get-tuple-element.54), channel_id=1, source_target_pairs={{0,3},{1,0},{2,1},{3,2},{4,7},{5,4},{6,5},{7,6},{8,11},{9,8},{10,9... | collective-permute-start | bytes 196616 | tf_op jit(solution)/shard_map/ppermute | solution.py:513
  67.2 1.5 %collective-permute-start.14 = (bf16[16,2048]{1,0:T(8,128)(2,1)S(1)}, bf16[16,2048]{1,0:T(8,128)(2,1)S(1)}, u32[]{:S(2)}, u32[]{:S(2)}) collective-permute-start(bf16[16,2048]{1,0:T(8,128)(2,1)S(1)} %get-tuple-element.56), channel_id=1, source_target_pairs={{0,1},{1,2},{2,3},{3,0},{4,5},{5,6},{6,7},{7,4},{8,9},{9,10},{10,1... | collective-permute-start | bytes 196616 | tf_op jit(solution)/shard_map/ppermute | solution.py:513
  68.6 0.8 %collective-permute-done.12.rest_1_ = bf16[16,2048]{1,0:T(8,128)(2,1)S(1)} collective-permute-done((bf16[16,2048]{1,0:T(8,128)(2,1)S(1)}, bf16[16,2048]{1,0:T(8,128)(2,1)S(1)}, u32[]{:S(2)}, u32[]{:S(2)}) %collective-permute-start.12) | collective-permute-done | bytes 65568 | tf_op jit(solution)/shard_map/ppermute | solution.py:513
  69.5 4.8 %collective-permute-done.13.rest_2_ = bf16[16,2048]{1,0:T(8,128)(2,1)S(1)} collective-permute-done((bf16[16,2048]{1,0:T(8,128)(2,1)S(1)}, bf16[16,2048]{1,0:T(8,128)(2,1)S(1)}, u32[]{:S(2)}, u32[]{:S(2)}) %collective-permute-start.13) | collective-permute-done | bytes 65568 | tf_op jit(solution)/shard_map/ppermute | solution.py:513
  74.2 1.4 %close.1 = f32[8,2,4096]{2,1,0:T(2,128)} custom-call(s32[2]{0:T(128)S(1)} %pad_add_fusion.index_ref, bf16[32,2,4096]{2,1,0:T(2,128)(2,1)S(1)} %copy-done, f32[16,2048]{1,0:T(8,128)S(1)} %get-tuple-element.53.rest_0_, bf16[16,2048]{1,0:T(8,128)(2,1)S(1)} %collective-permute-done.12.rest_1_, bf16[16,2048]{1,0:T(8,128)(2,1)S(1)} %collective-permute-done.13.rest_2_, ...), custom_call_target="tpu_custom_call" | custom-call | tf_op jit(solution)/shard_map/close/pallas_call | solution.py:495
  (29 shorter events, 1.0 us)
Async XLA Ops:
  0.1 21.0 %copy-start.2 = (s32[32]{0:T(128)S(1)}, s32[32]{0:T(128)}, u32[]{:S(2)}) copy-start(s32[32]{0:T(128)} %param.13) | copy-start | bytes 388
  16.6 9.9 %collective-permute-start = (bf16[2,16,2432]{2,1,0:T(8,128)(2,1)S(1)}, bf16[2,16,2432]{2,1,0:T(8,128)(2,1)S(1)}, u32[]{:S(2)}, u32[]{:S(2)}) collective-permute-start(bf16[2,16,2432]{2,1,0:T(8,128)(2,1)S(1)} %get-tuple-element.33.after_ref), channel_id=1, source_target_pairs={{0,4},{4,8},{8,12},{12,0},{1,5},{5,9},{9,13},{13,1},{2,6},{6,10},{... | collective-permute-start | bytes 466952 | tf_op jit(solution)/shard_map/ppermute | solution.py:513
  17.0 9.4 %collective-permute-start.1 = (bf16[2,16,2432]{2,1,0:T(8,128)(2,1)S(1)}, bf16[2,16,2432]{2,1,0:T(8,128)(2,1)S(1)}, u32[]{:S(2)}, u32[]{:S(2)}) collective-permute-start(bf16[2,16,2432]{2,1,0:T(8,128)(2,1)S(1)} %get-tuple-element.36), channel_id=1, source_target_pairs={{0,8},{4,12},{8,0},{12,4},{1,9},{5,13},{9,1},{13,5},{2,10},{6,14},... | collective-permute-start | bytes 466952 | tf_op jit(solution)/shard_map/ppermute | solution.py:513
  19.7 7.1 %collective-permute-start.2 = (bf16[2,16,2432]{2,1,0:T(8,128)(2,1)S(1)}, bf16[2,16,2432]{2,1,0:T(8,128)(2,1)S(1)}, u32[]{:S(2)}, u32[]{:S(2)}) collective-permute-start(bf16[2,16,2432]{2,1,0:T(8,128)(2,1)S(1)} %get-tuple-element.37), channel_id=1, source_target_pairs={{0,12},{4,0},{8,4},{12,8},{1,13},{5,1},{9,5},{13,9},{2,14},{6,2},{... | collective-permute-start | bytes 466952 | tf_op jit(solution)/shard_map/ppermute | solution.py:513
  27.7 9.0 %collective-permute-start.3 = (bf16[2,96,128]{2,1,0:T(8,128)(2,1)S(1)}, bf16[2,96,128]{2,1,0:T(8,128)(2,1)S(1)}, u32[]{:S(2)}, u32[]{:S(2)}) collective-permute-start(bf16[2,96,128]{2,1,0:T(8,128)(2,1)S(1)} %get-tuple-element.38.after_ref), channel_id=1, source_target_pairs={{0,1},{1,2},{2,3},{3,0},{4,5},{5,6},{6,7},{7,4},{8,9},{9,10},{10,1... | collective-permute-start | bytes 147464 | tf_op jit(solution)/shard_map/ppermute | solution.py:513
  29.4 7.3 %collective-permute-start.4 = (bf16[2,96,128]{2,1,0:T(8,128)(2,1)S(1)}, bf16[2,96,128]{2,1,0:T(8,128)(2,1)S(1)}, u32[]{:S(2)}, u32[]{:S(2)}) collective-permute-start(bf16[2,96,128]{2,1,0:T(8,128)(2,1)S(1)} %get-tuple-element.41), channel_id=1, source_target_pairs={{0,2},{1,3},{2,0},{3,1},{4,6},{5,7},{6,4},{7,5},{8,10},{9,11},{10,... | collective-permute-start | bytes 147464 | tf_op jit(solution)/shard_map/ppermute | solution.py:513
  31.9 4.8 %collective-permute-start.5 = (bf16[2,96,128]{2,1,0:T(8,128)(2,1)S(1)}, bf16[2,96,128]{2,1,0:T(8,128)(2,1)S(1)}, u32[]{:S(2)}, u32[]{:S(2)}) collective-permute-start(bf16[2,96,128]{2,1,0:T(8,128)(2,1)S(1)} %get-tuple-element.42), channel_id=1, source_target_pairs={{0,3},{1,0},{2,1},{3,2},{4,7},{5,4},{6,5},{7,6},{8,11},{9,8},{10,9... | collective-permute-start | bytes 147464 | tf_op jit(solution)/shard_map/ppermute | solution.py:513
  33.3 3.4 %copy-start.1 = (s32[2]{0:T(128)S(1)}, s32[2]{0:T(128)}, u32[]{:S(2)}) copy-start(s32[2]{0:T(128)} %length_ref.1) | copy-start | bytes 28
  38.6 5.3 %collective-permute-start.6 = (bf16[2,64,128]{2,1,0:T(8,128)(2,1)S(1)}, bf16[2,64,128]{2,1,0:T(8,128)(2,1)S(1)}, u32[]{:S(2)}, u32[]{:S(2)}) collective-permute-start(bf16[2,64,128]{2,1,0:T(8,128)(2,1)S(1)} %get-tuple-element.43.after_ref), channel_id=1, source_target_pairs={{0,3},{1,0},{2,1},{3,2},{4,7},{5,4},{6,5},{7,6},{8,11},{9,8},{10,9... | collective-permute-start | bytes 98312 | tf_op jit(solution)/shard_map/ppermute | solution.py:513
  41.1 4.8 %collective-permute-start.7 = (bf16[2,64,128]{2,1,0:T(8,128)(2,1)S(1)}, bf16[2,64,128]{2,1,0:T(8,128)(2,1)S(1)}, u32[]{:S(2)}, u32[]{:S(2)}) collective-permute-start(bf16[2,64,128]{2,1,0:T(8,128)(2,1)S(1)} %get-tuple-element.46), channel_id=1, source_target_pairs={{0,2},{1,3},{2,0},{3,1},{4,6},{5,7},{6,4},{7,5},{8,10},{9,11},{10,... | collective-permute-start | bytes 98312 | tf_op jit(solution)/shard_map/ppermute | solution.py:513
  41.1 5.7 %collective-permute-start.8 = (bf16[2,64,128]{2,1,0:T(8,128)(2,1)S(1)}, bf16[2,64,128]{2,1,0:T(8,128)(2,1)S(1)}, u32[]{:S(2)}, u32[]{:S(2)}) collective-permute-start(bf16[2,64,128]{2,1,0:T(8,128)(2,1)S(1)} %get-tuple-element.47), channel_id=1, source_target_pairs={{0,1},{1,2},{2,3},{3,0},{4,5},{5,6},{6,7},{7,4},{8,9},{9,10},{10,1... | collective-permute-start | bytes 98312 | tf_op jit(solution)/shard_map/ppermute | solution.py:513
  47.5 6.5 %collective-permute-start.10 = (bf16[16,4096]{1,0:T(8,128)(2,1)S(1)}, bf16[16,4096]{1,0:T(8,128)(2,1)S(1)}, u32[]{:S(2)}, u32[]{:S(2)}) collective-permute-start(bf16[16,4096]{1,0:T(8,128)(2,1)S(1)} %gather.1.after_ref.rest_4_), channel_id=1, source_target_pairs={{0,8},{4,12},{8,0},{12,4},{1,9},{5,13},{9,1},{13,5},{2,10},{6,14},... | collective-permute-start | bytes 393224 | tf_op jit(solution)/shard_map/ppermute | solution.py:513
  48.2 5.7 %collective-permute-start.11 = (bf16[16,4096]{1,0:T(8,128)(2,1)S(1)}, bf16[16,4096]{1,0:T(8,128)(2,1)S(1)}, u32[]{:S(2)}, u32[]{:S(2)}) collective-permute-start(bf16[16,4096]{1,0:T(8,128)(2,1)S(1)} %gather.1.after_ref.rest_4_), channel_id=1, source_target_pairs={{0,12},{4,0},{8,4},{12,8},{1,13},{5,1},{9,5},{13,9},{2,14},{6,2},{... | collective-permute-start | bytes 393224 | tf_op jit(solution)/shard_map/ppermute | solution.py:513
  48.2 5.8 %collective-permute-start.9 = (bf16[16,4096]{1,0:T(8,128)(2,1)S(1)}, bf16[16,4096]{1,0:T(8,128)(2,1)S(1)}, u32[]{:S(2)}, u32[]{:S(2)}) collective-permute-start(bf16[16,4096]{1,0:T(8,128)(2,1)S(1)} %gather.1.after_ref.rest_4_), channel_id=1, source_target_pairs={{0,4},{4,8},{8,12},{12,0},{1,5},{5,9},{9,13},{13,1},{2,6},{6,10},{... | collective-permute-start | bytes 393224 | tf_op jit(solution)/shard_map/ppermute | solution.py:513
  57.8 9.4 %collective-permute-start.15 = (bf16[16,2048]{1,0:T(8,128)(2,1)S(1)}, bf16[16,2048]{1,0:T(8,128)(2,1)S(1)}, u32[]{:S(2)}, u32[]{:S(2)}) collective-permute-start(bf16[16,2048]{1,0:T(8,128)(2,1)S(1)} %get-tuple-element.58), channel_id=1, source_target_pairs={{0,3},{1,0},{2,1},{3,2},{4,7},{5,4},{6,5},{7,6},{8,11},{9,8},{10,9... | collective-permute-start | bytes 196616 | tf_op jit(solution)/shard_map/ppermute | solution.py:513
  58.4 10.2 %collective-permute-start.16 = (bf16[16,2048]{1,0:T(8,128)(2,1)S(1)}, bf16[16,2048]{1,0:T(8,128)(2,1)S(1)}, u32[]{:S(2)}, u32[]{:S(2)}) collective-permute-start(bf16[16,2048]{1,0:T(8,128)(2,1)S(1)} %get-tuple-element.59), channel_id=1, source_target_pairs={{0,2},{1,3},{2,0},{3,1},{4,6},{5,7},{6,4},{7,5},{8,10},{9,11},{10,... | collective-permute-start | bytes 196616 | tf_op jit(solution)/shard_map/ppermute | solution.py:513
  59.3 14.9 %copy-start = (bf16[32,2,4096]{2,1,0:T(2,128)(2,1)S(1)}, bf16[32,2,4096]{2,1,0:T(2,128)(2,1)}, u32[]{:S(2)}) copy-start(bf16[32,2,4096]{2,1,0:T(2,128)(2,1)} %tokens_ref.1) | copy-start | bytes 1572868
  59.3 9.3 %collective-permute-start.17 = (bf16[16,2048]{1,0:T(8,128)(2,1)S(1)}, bf16[16,2048]{1,0:T(8,128)(2,1)S(1)}, u32[]{:S(2)}, u32[]{:S(2)}) collective-permute-start(bf16[16,2048]{1,0:T(8,128)(2,1)S(1)} %get-tuple-element.60), channel_id=1, source_target_pairs={{0,1},{1,2},{2,3},{3,0},{4,5},{5,6},{6,7},{7,4},{8,9},{9,10},{10,1... | collective-permute-start | bytes 196616 | tf_op jit(solution)/shard_map/ppermute | solution.py:513
  64.8 4.7 %collective-permute-start.12 = (bf16[16,2048]{1,0:T(8,128)(2,1)S(1)}, bf16[16,2048]{1,0:T(8,128)(2,1)S(1)}, u32[]{:S(2)}, u32[]{:S(2)}) collective-permute-start(bf16[16,2048]{1,0:T(8,128)(2,1)S(1)} %get-tuple-element.54), channel_id=1, source_target_pairs={{0,3},{1,0},{2,1},{3,2},{4,7},{5,4},{6,5},{7,6},{8,11},{9,8},{10,9... | collective-permute-start | bytes 196616 | tf_op jit(solution)/shard_map/ppermute | solution.py:513
  67.0 7.3 %collective-permute-start.13 = (bf16[16,2048]{1,0:T(8,128)(2,1)S(1)}, bf16[16,2048]{1,0:T(8,128)(2,1)S(1)}, u32[]{:S(2)}, u32[]{:S(2)}) collective-permute-start(bf16[16,2048]{1,0:T(8,128)(2,1)S(1)} %get-tuple-element.55), channel_id=1, source_target_pairs={{0,2},{1,3},{2,0},{3,1},{4,6},{5,7},{6,4},{7,5},{8,10},{9,11},{10,... | collective-permute-start | bytes 196616 | tf_op jit(solution)/shard_map/ppermute | solution.py:513
  67.2 7.1 %collective-permute-start.14 = (bf16[16,2048]{1,0:T(8,128)(2,1)S(1)}, bf16[16,2048]{1,0:T(8,128)(2,1)S(1)}, u32[]{:S(2)}, u32[]{:S(2)}) collective-permute-start(bf16[16,2048]{1,0:T(8,128)(2,1)S(1)} %get-tuple-element.56), channel_id=1, source_target_pairs={{0,1},{1,2},{2,3},{3,0},{4,5},{5,6},{6,7},{7,4},{8,9},{9,10},{10,1... | collective-permute-start | bytes 196616 | tf_op jit(solution)/shard_map/ppermute | solution.py:513

commit v7 on v6

--- a/solution.py
+++ b/solution.py
@@ -19,7 +19,7 @@
 OUTWARD_SHARE = 8
 OUTWARD_STEP = 1024
 OUTWARD_LIMIT = 12 * 2**20
-HELD_SHARES = (2, 4, 2, 7)
+HELD_SHARES = (2, 3, 3, 7)
 PAIR_GROUP = 4
 
 

time: 76 us -> 76.3 us (level)
  transfers between devices with their start and end apart: 18 -> 18, of which waited for: 6 -> 8; matrix products, arithmetic and copies ran while one was open for 4% -> 4% of each run, Pallas kernels for 22% -> 22%
where the time goes in v7:
time: 76.3 us; the launch traced here: 75.9 us
  Pallas kernels  41.7 us (55%)
  starting transfers between devices  21.7 us (28%)
  waiting for transfers between devices  9.04 us (12%)
  local copies, waits for them, and re-layouts  2.82 us (4%)
    ppermute x18, starting transfers between devices, exchange(): lax.ppermute(pieces[s], axis, shift_pairs(count, sign * s))  21.7 us
    pallas_call x1, Pallas kernels, project(): pl.pallas_call(functools.partial(project_kernel, axis_size, block, slots)...  16.5 us
    pallas_call x4, Pallas kernels, hold(): pl.pallas_call(functools.partial(hold_kernel, first), in_specs=[pl.BlockS...  13 us
    ppermute x18, waiting for transfers between devices, exchange(): lax.ppermute(pieces[s], axis, shift_pairs(count, sign * s))  9.04 us
    pallas_call x2, Pallas kernels, outward(): pl.pallas_call(functools.partial(outward_kernel, len(blocks), axis_size,...  7.51 us
    unnamed x8, local copies, waits for them, and re-layouts  2.71 us
    pallas_call x1, Pallas kernels, attend(): pl.pallas_call(functools.partial(attend_kernel, len(pieces), query_rows),...  1.78 us
  transfers between devices with their start and end apart: 18, of which 8 were waited for; matrix products, arithmetic and copies ran while one was open for 4% of the time, Pallas kernels for 22%

profile of v7, /device:TPU:0, one launch (start us, length us, event | category | flops | bytes accessed | tf_op | source)
XLA Modules:
  0.0 75.9 jit_solution(13778420323491845198)
XLA Ops:
  0.1 16.5 %project.1 = (f32[2,16,2432]{2,1,0:T(8,128)S(1)}, bf16[2,16,2432]{2,1,0:T(8,128)(2,1)S(1)}, bf16[2,16,2432]{2,1,0:T(8,128)(2,1)S(1)}, bf16[2,16,2432]{2,1,0:T(8,128)(2,1)S(1)}) custom-call(s32[2]{0:T(128)S(1)} %pad_add_fusion.index_ref, bf16[32,2,4096]{2,1,0:T(2,128)(2,1)} %tokens_ref.1, bf16[32,128]{1,0:T(8,128)(2,1)} %bitcast.19, ...), custom_call_target="tpu_custom_call" | custom-call | flops 2415919104 | bytes 37748736 | tf_op jit(solution)/shard_map/project/pallas_call | solution.py:152
  16.6 0.5 collective-permute-start
  17.0 2.6 %collective-permute-start.1 = (bf16[2,16,2432]{2,1,0:T(8,128)(2,1)S(1)}, bf16[2,16,2432]{2,1,0:T(8,128)(2,1)S(1)}, u32[]{:S(2)}, u32[]{:S(2)}) collective-permute-start(bf16[2,16,2432]{2,1,0:T(8,128)(2,1)S(1)} %get-tuple-element.36), channel_id=1, source_target_pairs={{0,8},{4,12},{8,0},{12,4},{1,9},{5,13},{9,1},{13,5},{2,10},{6,14},... | collective-permute-start | bytes 466952 | tf_op jit(solution)/shard_map/ppermute | solution.py:513
  19.7 1.4 %collective-permute-start.2 = (bf16[2,16,2432]{2,1,0:T(8,128)(2,1)S(1)}, bf16[2,16,2432]{2,1,0:T(8,128)(2,1)S(1)}, u32[]{:S(2)}, u32[]{:S(2)}) collective-permute-start(bf16[2,16,2432]{2,1,0:T(8,128)(2,1)S(1)} %get-tuple-element.37), channel_id=1, source_target_pairs={{0,12},{4,0},{8,4},{12,8},{1,13},{5,1},{9,5},{13,9},{2,14},{6,2},{... | collective-permute-start | bytes 466952 | tf_op jit(solution)/shard_map/ppermute | solution.py:513
  21.5 2.7 %copy.15 = bf16[2,384,2,8,128]{4,1,3,2,0:T(8,128)(2,1)S(1)} copy(bf16[2,384,2,8,128]{4,3,2,1,0:T(8,128)(2,1)} %param.11) | data formatting | bytes 6291456 | tf_op args[4]
  24.2 2.2 %hold.4 = (bf16[512,4096]{1,0:T(8,128)(2,1)S(1)}, f32[2,16,2432]{2,1,0:T(8,128)S(1)}) custom-call(bf16[2,16,2432]{2,1,0:T(8,128)(2,1)S(1)} %get-tuple-element.33.after_ref, f32[2,16,2432]{2,1,0:T(8,128)S(1)} %get-tuple-element.34.through_ref, bf16[4096,4096]{1,0:T(8,128)(2,1)} %bitcast.12), custom_call_target="tpu_custom_call", output_to_operand_aliasing={{1}: (1, {})} | custom-call | bytes 4194304 | tf_op jit(solution)/shard_map/hold/pallas_call | solution.py:373
  26.8 1.0 %finish.1 = (bf16[2,96,128]{2,1,0:T(8,128)(2,1)S(1)}, bf16[2,96,128]{2,1,0:T(8,128)(2,1)S(1)}, bf16[2,96,128]{2,1,0:T(8,128)(2,1)S(1)}, bf16[2,96,128]{2,1,0:T(8,128)(2,1)S(1)}) custom-call(s32[2]{0:T(128)S(1)} %pad_add_fusion.index_ref, bf16[2,2,8,384,128]{4,3,2,1,0:T(8,128)(2,1)S(1)} %bitcast.10, f32[64,128]{1,0:T(8,128)S(1)} %get-tuple-element.64.cosine_ref, ...), custom_call_target="tpu_custom_call" | custom-call | tf_op jit(solution)/shard_map/finish/pallas_call | solution.py:237
  27.7 1.7 %collective-permute-start.3 = (bf16[2,96,128]{2,1,0:T(8,128)(2,1)S(1)}, bf16[2,96,128]{2,1,0:T(8,128)(2,1)S(1)}, u32[]{:S(2)}, u32[]{:S(2)}) collective-permute-start(bf16[2,96,128]{2,1,0:T(8,128)(2,1)S(1)} %get-tuple-element.38.after_ref), channel_id=1, source_target_pairs={{0,1},{1,2},{2,3},{3,0},{4,5},{5,6},{6,7},{7,4},{8,9},{9,10},{10,1... | collective-permute-start | bytes 147464 | tf_op jit(solution)/shard_map/ppermute | solution.py:513
  29.4 2.5 %collective-permute-start.4 = (bf16[2,96,128]{2,1,0:T(8,128)(2,1)S(1)}, bf16[2,96,128]{2,1,0:T(8,128)(2,1)S(1)}, u32[]{:S(2)}, u32[]{:S(2)}) collective-permute-start(bf16[2,96,128]{2,1,0:T(8,128)(2,1)S(1)} %get-tuple-element.41), channel_id=1, source_target_pairs={{0,2},{1,3},{2,0},{3,1},{4,6},{5,7},{6,4},{7,5},{8,10},{9,11},{10,... | collective-permute-start | bytes 147464 | tf_op jit(solution)/shard_map/ppermute | solution.py:513
  31.9 1.3 %collective-permute-start.5 = (bf16[2,96,128]{2,1,0:T(8,128)(2,1)S(1)}, bf16[2,96,128]{2,1,0:T(8,128)(2,1)S(1)}, u32[]{:S(2)}, u32[]{:S(2)}) collective-permute-start(bf16[2,96,128]{2,1,0:T(8,128)(2,1)S(1)} %get-tuple-element.42), channel_id=1, source_target_pairs={{0,3},{1,0},{2,1},{3,2},{4,7},{5,4},{6,5},{7,6},{8,11},{9,8},{10,9... | collective-permute-start | bytes 147464 | tf_op jit(solution)/shard_map/ppermute | solution.py:513
  33.3 2.8 %hold.5 = (bf16[768,4096]{1,0:T(8,128)(2,1)S(1)}, bf16[2,96,128]{2,1,0:T(8,128)(2,1)S(1)}) custom-call(bf16[2,96,128]{2,1,0:T(8,128)(2,1)S(1)} %get-tuple-element.38.after_ref, bf16[2,96,128]{2,1,0:T(8,128)(2,1)S(1)} %get-tuple-element.39.through_ref, bf16[4096,4096]{1,0:T(8,128)(2,1)} %bitcast.13), custom_call_target="tpu_custom_call", output_to_operand_aliasing={{1}: (1, {})} | custom-call | bytes 6291456 | tf_op jit(solution)/shard_map/hold/pallas_call | solution.py:373
  36.3 0.3 collective-permute-done.5.rest_3_
  36.6 1.8 %attend.1 = (bf16[2,64,128]{2,1,0:T(8,128)(2,1)S(1)}, bf16[2,64,128]{2,1,0:T(8,128)(2,1)S(1)}, bf16[2,64,128]{2,1,0:T(8,128)(2,1)S(1)}, bf16[2,64,128]{2,1,0:T(8,128)(2,1)S(1)}) custom-call(s32[2]{0:T(128)S(1)} %pad_add_fusion.index_ref, s32[2]{0:T(128)S(1)} %copy-done.1, bf16[2,2,8,384,128]{4,3,2,1,0:T(8,128)(2,1)S(1)} %bitcast.11, ...), custom_call_target="tpu_custom_call" | custom-call | tf_op jit(solution)/shard_map/attend/pallas_call | solution.py:316
  38.4 2.7 %collective-permute-start.6 = (bf16[2,64,128]{2,1,0:T(8,128)(2,1)S(1)}, bf16[2,64,128]{2,1,0:T(8,128)(2,1)S(1)}, u32[]{:S(2)}, u32[]{:S(2)}) collective-permute-start(bf16[2,64,128]{2,1,0:T(8,128)(2,1)S(1)} %get-tuple-element.43.after_ref), channel_id=1, source_target_pairs={{0,3},{1,0},{2,1},{3,2},{4,7},{5,4},{6,5},{7,6},{8,11},{9,8},{10,9... | collective-permute-start | bytes 98312 | tf_op jit(solution)/shard_map/ppermute | solution.py:513
  41.1 0.6 collective-permute-start.8
  41.7 2.8 %hold.6 = (bf16[768,4096]{1,0:T(8,128)(2,1)S(1)}, bf16[2,64,128]{2,1,0:T(8,128)(2,1)S(1)}) custom-call(bf16[2,64,128]{2,1,0:T(8,128)(2,1)S(1)} %get-tuple-element.43.after_ref, bf16[2,64,128]{2,1,0:T(8,128)(2,1)S(1)} %get-tuple-element.44.through_ref, bf16[4096,4096]{1,0:T(8,128)(2,1)} %bitcast.14), custom_call_target="tpu_custom_call", output_to_operand_aliasing={{1}: (1, {})} | custom-call | bytes 6291456 | tf_op jit(solution)/shard_map/hold/pallas_call | solution.py:373
  44.5 1.4 %collective-permute-done.7.rest_2_ = bf16[2,64,128]{2,1,0:T(8,128)(2,1)S(1)} collective-permute-done((bf16[2,64,128]{2,1,0:T(8,128)(2,1)S(1)}, bf16[2,64,128]{2,1,0:T(8,128)(2,1)S(1)}, u32[]{:S(2)}, u32[]{:S(2)}) %collective-permute-start.7) | collective-permute-done | bytes 32800 | tf_op jit(solution)/shard_map/ppermute | solution.py:513
  45.8 1.0 %collective-permute-done.8.rest_3_ = bf16[2,64,128]{2,1,0:T(8,128)(2,1)S(1)} collective-permute-done((bf16[2,64,128]{2,1,0:T(8,128)(2,1)S(1)}, bf16[2,64,128]{2,1,0:T(8,128)(2,1)S(1)}, u32[]{:S(2)}, u32[]{:S(2)}) %collective-permute-start.8) | collective-permute-done | bytes 32800 | tf_op jit(solution)/shard_map/ppermute | solution.py:513
  46.8 0.6 gather.1.after_ref.rest_4_
  47.4 0.8 %collective-permute-start.10 = (bf16[16,4096]{1,0:T(8,128)(2,1)S(1)}, bf16[16,4096]{1,0:T(8,128)(2,1)S(1)}, u32[]{:S(2)}, u32[]{:S(2)}) collective-permute-start(bf16[16,4096]{1,0:T(8,128)(2,1)S(1)} %gather.1.after_ref.rest_4_), channel_id=1, source_target_pairs={{0,8},{4,12},{8,0},{12,4},{1,9},{5,13},{9,1},{13,5},{2,10},{6,14},... | collective-permute-start | bytes 393224 | tf_op jit(solution)/shard_map/ppermute | solution.py:513
  48.2 0.5 collective-permute-start.9
  48.7 5.2 %hold.7 = (bf16[1792,4096]{1,0:T(8,128)(2,1)S(1)}, s32[2]{0:T(128)S(1)}) custom-call(bf16[16,4096]{1,0:T(8,128)(2,1)S(1)} %gather.1.after_ref.rest_4_, s32[2]{0:T(128)S(1)} %copy.19.through_ref, bf16[4096,4096]{1,0:T(8,128)(2,1)} %bitcast.15), custom_call_target="tpu_custom_call", output_to_operand_aliasing={{1}: (1, {})} | custom-call | bytes 14680064 | tf_op jit(solution)/shard_map/hold/pallas_call | solution.py:373
  54.0 3.8 %outward.3 = (f32[16,2048]{1,0:T(8,128)S(1)}, bf16[16,2048]{1,0:T(8,128)(2,1)S(1)}, bf16[16,2048]{1,0:T(8,128)(2,1)S(1)}, bf16[16,2048]{1,0:T(8,128)(2,1)S(1)}) custom-call(s32[2]{0:T(128)S(1)} %get-tuple-element.48.index_ref, bf16[4096,4096]{1,0:T(8,128)(2,1)} %bitcast.16, bf16[512,4096]{1,0:T(8,128)(2,1)S(1)} %get-tuple-element.49.rest_0_, ...), custom_call_target="tpu_custom_call" | custom-call | flops 1073741824 | bytes 16777216 | tf_op jit(solution)/shard_map/outward/pallas_call | solution.py:446
  57.8 1.0 %collective-permute-start.15 = (bf16[16,2048]{1,0:T(8,128)(2,1)S(1)}, bf16[16,2048]{1,0:T(8,128)(2,1)S(1)}, u32[]{:S(2)}, u32[]{:S(2)}) collective-permute-start(bf16[16,2048]{1,0:T(8,128)(2,1)S(1)} %get-tuple-element.58), channel_id=1, source_target_pairs={{0,3},{1,0},{2,1},{3,2},{4,7},{5,4},{6,5},{7,6},{8,11},{9,8},{10,9... | collective-permute-start | bytes 196616 | tf_op jit(solution)/shard_map/ppermute | solution.py:513
  58.8 1.1 %collective-permute-start.16 = (bf16[16,2048]{1,0:T(8,128)(2,1)S(1)}, bf16[16,2048]{1,0:T(8,128)(2,1)S(1)}, u32[]{:S(2)}, u32[]{:S(2)}) collective-permute-start(bf16[16,2048]{1,0:T(8,128)(2,1)S(1)} %get-tuple-element.59), channel_id=1, source_target_pairs={{0,2},{1,3},{2,0},{3,1},{4,6},{5,7},{6,4},{7,5},{8,10},{9,11},{10,... | collective-permute-start | bytes 196616 | tf_op jit(solution)/shard_map/ppermute | solution.py:513
  59.9 1.1 %collective-permute-start.17 = (bf16[16,2048]{1,0:T(8,128)(2,1)S(1)}, bf16[16,2048]{1,0:T(8,128)(2,1)S(1)}, u32[]{:S(2)}, u32[]{:S(2)}) collective-permute-start(bf16[16,2048]{1,0:T(8,128)(2,1)S(1)} %get-tuple-element.60), channel_id=1, source_target_pairs={{0,1},{1,2},{2,3},{3,0},{4,5},{5,6},{6,7},{7,4},{8,9},{9,10},{10,1... | collective-permute-start | bytes 196616 | tf_op jit(solution)/shard_map/ppermute | solution.py:513
  61.0 3.8 %outward.2 = (f32[16,2048]{1,0:T(8,128)S(1)}, bf16[16,2048]{1,0:T(8,128)(2,1)S(1)}, bf16[16,2048]{1,0:T(8,128)(2,1)S(1)}, bf16[16,2048]{1,0:T(8,128)(2,1)S(1)}) custom-call(s32[2]{0:T(128)S(1)} %get-tuple-element.48.index_ref, bf16[4096,4096]{1,0:T(8,128)(2,1)} %bitcast.17, bf16[512,4096]{1,0:T(8,128)(2,1)S(1)} %get-tuple-element.49.rest_0_, ...), custom_call_target="tpu_custom_call" | custom-call | flops 1073741824 | bytes 16777216 | tf_op jit(solution)/shard_map/outward/pallas_call | solution.py:446
  64.7 2.8 %collective-permute-start.12 = (bf16[16,2048]{1,0:T(8,128)(2,1)S(1)}, bf16[16,2048]{1,0:T(8,128)(2,1)S(1)}, u32[]{:S(2)}, u32[]{:S(2)}) collective-permute-start(bf16[16,2048]{1,0:T(8,128)(2,1)S(1)} %get-tuple-element.54), channel_id=1, source_target_pairs={{0,3},{1,0},{2,1},{3,2},{4,7},{5,4},{6,5},{7,6},{8,11},{9,8},{10,9... | collective-permute-start | bytes 196616 | tf_op jit(solution)/shard_map/ppermute | solution.py:513
  67.5 1.1 %collective-permute-start.14 = (bf16[16,2048]{1,0:T(8,128)(2,1)S(1)}, bf16[16,2048]{1,0:T(8,128)(2,1)S(1)}, u32[]{:S(2)}, u32[]{:S(2)}) collective-permute-start(bf16[16,2048]{1,0:T(8,128)(2,1)S(1)} %get-tuple-element.56), channel_id=1, source_target_pairs={{0,1},{1,2},{2,3},{3,0},{4,5},{5,6},{6,7},{7,4},{8,9},{9,10},{10,1... | collective-permute-start | bytes 196616 | tf_op jit(solution)/shard_map/ppermute | solution.py:513
  68.6 1.4 %collective-permute-done.12.rest_1_ = bf16[16,2048]{1,0:T(8,128)(2,1)S(1)} collective-permute-done((bf16[16,2048]{1,0:T(8,128)(2,1)S(1)}, bf16[16,2048]{1,0:T(8,128)(2,1)S(1)}, u32[]{:S(2)}, u32[]{:S(2)}) %collective-permute-start.12) | collective-permute-done | bytes 65568 | tf_op jit(solution)/shard_map/ppermute | solution.py:513
  70.0 4.5 %collective-permute-done.13.rest_2_ = bf16[16,2048]{1,0:T(8,128)(2,1)S(1)} collective-permute-done((bf16[16,2048]{1,0:T(8,128)(2,1)S(1)}, bf16[16,2048]{1,0:T(8,128)(2,1)S(1)}, u32[]{:S(2)}, u32[]{:S(2)}) %collective-permute-start.13) | collective-permute-done | bytes 65568 | tf_op jit(solution)/shard_map/ppermute | solution.py:513
  74.5 1.4 %close.1 = f32[8,2,4096]{2,1,0:T(2,128)} custom-call(s32[2]{0:T(128)S(1)} %pad_add_fusion.index_ref, bf16[32,2,4096]{2,1,0:T(2,128)(2,1)S(1)} %copy-done, f32[16,2048]{1,0:T(8,128)S(1)} %get-tuple-element.53.rest_0_, bf16[16,2048]{1,0:T(8,128)(2,1)S(1)} %collective-permute-done.12.rest_1_, bf16[16,2048]{1,0:T(8,128)(2,1)S(1)} %collective-permute-done.13.rest_2_, ...), custom_call_target="tpu_custom_call" | custom-call | tf_op jit(solution)/shard_map/close/pallas_call | solution.py:495
  (29 shorter events, 1.2 us)
Async XLA Ops:
  0.1 21.0 %copy-start.2 = (s32[32]{0:T(128)S(1)}, s32[32]{0:T(128)}, u32[]{:S(2)}) copy-start(s32[32]{0:T(128)} %param.13) | copy-start | bytes 388
  16.6 9.9 %collective-permute-start = (bf16[2,16,2432]{2,1,0:T(8,128)(2,1)S(1)}, bf16[2,16,2432]{2,1,0:T(8,128)(2,1)S(1)}, u32[]{:S(2)}, u32[]{:S(2)}) collective-permute-start(bf16[2,16,2432]{2,1,0:T(8,128)(2,1)S(1)} %get-tuple-element.33.after_ref), channel_id=1, source_target_pairs={{0,4},{4,8},{8,12},{12,0},{1,5},{5,9},{9,13},{13,1},{2,6},{6,10},{... | collective-permute-start | bytes 466952 | tf_op jit(solution)/shard_map/ppermute | solution.py:513
  17.0 9.4 %collective-permute-start.1 = (bf16[2,16,2432]{2,1,0:T(8,128)(2,1)S(1)}, bf16[2,16,2432]{2,1,0:T(8,128)(2,1)S(1)}, u32[]{:S(2)}, u32[]{:S(2)}) collective-permute-start(bf16[2,16,2432]{2,1,0:T(8,128)(2,1)S(1)} %get-tuple-element.36), channel_id=1, source_target_pairs={{0,8},{4,12},{8,0},{12,4},{1,9},{5,13},{9,1},{13,5},{2,10},{6,14},... | collective-permute-start | bytes 466952 | tf_op jit(solution)/shard_map/ppermute | solution.py:513
  19.7 7.1 %collective-permute-start.2 = (bf16[2,16,2432]{2,1,0:T(8,128)(2,1)S(1)}, bf16[2,16,2432]{2,1,0:T(8,128)(2,1)S(1)}, u32[]{:S(2)}, u32[]{:S(2)}) collective-permute-start(bf16[2,16,2432]{2,1,0:T(8,128)(2,1)S(1)} %get-tuple-element.37), channel_id=1, source_target_pairs={{0,12},{4,0},{8,4},{12,8},{1,13},{5,1},{9,5},{13,9},{2,14},{6,2},{... | collective-permute-start | bytes 466952 | tf_op jit(solution)/shard_map/ppermute | solution.py:513
  27.7 8.4 %collective-permute-start.3 = (bf16[2,96,128]{2,1,0:T(8,128)(2,1)S(1)}, bf16[2,96,128]{2,1,0:T(8,128)(2,1)S(1)}, u32[]{:S(2)}, u32[]{:S(2)}) collective-permute-start(bf16[2,96,128]{2,1,0:T(8,128)(2,1)S(1)} %get-tuple-element.38.after_ref), channel_id=1, source_target_pairs={{0,1},{1,2},{2,3},{3,0},{4,5},{5,6},{6,7},{7,4},{8,9},{9,10},{10,1... | collective-permute-start | bytes 147464 | tf_op jit(solution)/shard_map/ppermute | solution.py:513
  29.4 6.9 %collective-permute-start.4 = (bf16[2,96,128]{2,1,0:T(8,128)(2,1)S(1)}, bf16[2,96,128]{2,1,0:T(8,128)(2,1)S(1)}, u32[]{:S(2)}, u32[]{:S(2)}) collective-permute-start(bf16[2,96,128]{2,1,0:T(8,128)(2,1)S(1)} %get-tuple-element.41), channel_id=1, source_target_pairs={{0,2},{1,3},{2,0},{3,1},{4,6},{5,7},{6,4},{7,5},{8,10},{9,11},{10,... | collective-permute-start | bytes 147464 | tf_op jit(solution)/shard_map/ppermute | solution.py:513
  31.9 4.6 %collective-permute-start.5 = (bf16[2,96,128]{2,1,0:T(8,128)(2,1)S(1)}, bf16[2,96,128]{2,1,0:T(8,128)(2,1)S(1)}, u32[]{:S(2)}, u32[]{:S(2)}) collective-permute-start(bf16[2,96,128]{2,1,0:T(8,128)(2,1)S(1)} %get-tuple-element.42), channel_id=1, source_target_pairs={{0,3},{1,0},{2,1},{3,2},{4,7},{5,4},{6,5},{7,6},{8,11},{9,8},{10,9... | collective-permute-start | bytes 147464 | tf_op jit(solution)/shard_map/ppermute | solution.py:513
  33.3 3.3 %copy-start.1 = (s32[2]{0:T(128)S(1)}, s32[2]{0:T(128)}, u32[]{:S(2)}) copy-start(s32[2]{0:T(128)} %length_ref.1) | copy-start | bytes 28
  38.4 6.1 %collective-permute-start.6 = (bf16[2,64,128]{2,1,0:T(8,128)(2,1)S(1)}, bf16[2,64,128]{2,1,0:T(8,128)(2,1)S(1)}, u32[]{:S(2)}, u32[]{:S(2)}) collective-permute-start(bf16[2,64,128]{2,1,0:T(8,128)(2,1)S(1)} %get-tuple-element.43.after_ref), channel_id=1, source_target_pairs={{0,3},{1,0},{2,1},{3,2},{4,7},{5,4},{6,5},{7,6},{8,11},{9,8},{10,9... | collective-permute-start | bytes 98312 | tf_op jit(solution)/shard_map/ppermute | solution.py:513
  41.0 4.8 %collective-permute-start.7 = (bf16[2,64,128]{2,1,0:T(8,128)(2,1)S(1)}, bf16[2,64,128]{2,1,0:T(8,128)(2,1)S(1)}, u32[]{:S(2)}, u32[]{:S(2)}) collective-permute-start(bf16[2,64,128]{2,1,0:T(8,128)(2,1)S(1)} %get-tuple-element.46), channel_id=1, source_target_pairs={{0,2},{1,3},{2,0},{3,1},{4,6},{5,7},{6,4},{7,5},{8,10},{9,11},{10,... | collective-permute-start | bytes 98312 | tf_op jit(solution)/shard_map/ppermute | solution.py:513
  41.1 5.7 %collective-permute-start.8 = (bf16[2,64,128]{2,1,0:T(8,128)(2,1)S(1)}, bf16[2,64,128]{2,1,0:T(8,128)(2,1)S(1)}, u32[]{:S(2)}, u32[]{:S(2)}) collective-permute-start(bf16[2,64,128]{2,1,0:T(8,128)(2,1)S(1)} %get-tuple-element.47), channel_id=1, source_target_pairs={{0,1},{1,2},{2,3},{3,0},{4,5},{5,6},{6,7},{7,4},{8,9},{9,10},{10,1... | collective-permute-start | bytes 98312 | tf_op jit(solution)/shard_map/ppermute | solution.py:513
  47.4 6.5 %collective-permute-start.10 = (bf16[16,4096]{1,0:T(8,128)(2,1)S(1)}, bf16[16,4096]{1,0:T(8,128)(2,1)S(1)}, u32[]{:S(2)}, u32[]{:S(2)}) collective-permute-start(bf16[16,4096]{1,0:T(8,128)(2,1)S(1)} %gather.1.after_ref.rest_4_), channel_id=1, source_target_pairs={{0,8},{4,12},{8,0},{12,4},{1,9},{5,13},{9,1},{13,5},{2,10},{6,14},... | collective-permute-start | bytes 393224 | tf_op jit(solution)/shard_map/ppermute | solution.py:513
  48.2 5.7 %collective-permute-start.11 = (bf16[16,4096]{1,0:T(8,128)(2,1)S(1)}, bf16[16,4096]{1,0:T(8,128)(2,1)S(1)}, u32[]{:S(2)}, u32[]{:S(2)}) collective-permute-start(bf16[16,4096]{1,0:T(8,128)(2,1)S(1)} %gather.1.after_ref.rest_4_), channel_id=1, source_target_pairs={{0,12},{4,0},{8,4},{12,8},{1,13},{5,1},{9,5},{13,9},{2,14},{6,2},{... | collective-permute-start | bytes 393224 | tf_op jit(solution)/shard_map/ppermute | solution.py:513
  48.2 5.8 %collective-permute-start.9 = (bf16[16,4096]{1,0:T(8,128)(2,1)S(1)}, bf16[16,4096]{1,0:T(8,128)(2,1)S(1)}, u32[]{:S(2)}, u32[]{:S(2)}) collective-permute-start(bf16[16,4096]{1,0:T(8,128)(2,1)S(1)} %gather.1.after_ref.rest_4_), channel_id=1, source_target_pairs={{0,4},{4,8},{8,12},{12,0},{1,5},{5,9},{9,13},{13,1},{2,6},{6,10},{... | collective-permute-start | bytes 393224 | tf_op jit(solution)/shard_map/ppermute | solution.py:513
  57.8 9.8 %collective-permute-start.15 = (bf16[16,2048]{1,0:T(8,128)(2,1)S(1)}, bf16[16,2048]{1,0:T(8,128)(2,1)S(1)}, u32[]{:S(2)}, u32[]{:S(2)}) collective-permute-start(bf16[16,2048]{1,0:T(8,128)(2,1)S(1)} %get-tuple-element.58), channel_id=1, source_target_pairs={{0,3},{1,0},{2,1},{3,2},{4,7},{5,4},{6,5},{7,6},{8,11},{9,8},{10,9... | collective-permute-start | bytes 196616 | tf_op jit(solution)/shard_map/ppermute | solution.py:513
  58.8 9.9 %collective-permute-start.16 = (bf16[16,2048]{1,0:T(8,128)(2,1)S(1)}, bf16[16,2048]{1,0:T(8,128)(2,1)S(1)}, u32[]{:S(2)}, u32[]{:S(2)}) collective-permute-start(bf16[16,2048]{1,0:T(8,128)(2,1)S(1)} %get-tuple-element.59), channel_id=1, source_target_pairs={{0,2},{1,3},{2,0},{3,1},{4,6},{5,7},{6,4},{7,5},{8,10},{9,11},{10,... | collective-permute-start | bytes 196616 | tf_op jit(solution)/shard_map/ppermute | solution.py:513
  59.9 14.6 %copy-start = (bf16[32,2,4096]{2,1,0:T(2,128)(2,1)S(1)}, bf16[32,2,4096]{2,1,0:T(2,128)(2,1)}, u32[]{:S(2)}) copy-start(bf16[32,2,4096]{2,1,0:T(2,128)(2,1)} %tokens_ref.1) | copy-start | bytes 1572868
  59.9 8.7 %collective-permute-start.17 = (bf16[16,2048]{1,0:T(8,128)(2,1)S(1)}, bf16[16,2048]{1,0:T(8,128)(2,1)S(1)}, u32[]{:S(2)}, u32[]{:S(2)}) collective-permute-start(bf16[16,2048]{1,0:T(8,128)(2,1)S(1)} %get-tuple-element.60), channel_id=1, source_target_pairs={{0,1},{1,2},{2,3},{3,0},{4,5},{5,6},{6,7},{7,4},{8,9},{9,10},{10,1... | collective-permute-start | bytes 196616 | tf_op jit(solution)/shard_map/ppermute | solution.py:513
  64.7 5.3 %collective-permute-start.12 = (bf16[16,2048]{1,0:T(8,128)(2,1)S(1)}, bf16[16,2048]{1,0:T(8,128)(2,1)S(1)}, u32[]{:S(2)}, u32[]{:S(2)}) collective-permute-start(bf16[16,2048]{1,0:T(8,128)(2,1)S(1)} %get-tuple-element.54), channel_id=1, source_target_pairs={{0,3},{1,0},{2,1},{3,2},{4,7},{5,4},{6,5},{7,6},{8,11},{9,8},{10,9... | collective-permute-start | bytes 196616 | tf_op jit(solution)/shard_map/ppermute | solution.py:513
  67.5 7.0 %collective-permute-start.13 = (bf16[16,2048]{1,0:T(8,128)(2,1)S(1)}, bf16[16,2048]{1,0:T(8,128)(2,1)S(1)}, u32[]{:S(2)}, u32[]{:S(2)}) collective-permute-start(bf16[16,2048]{1,0:T(8,128)(2,1)S(1)} %get-tuple-element.55), channel_id=1, source_target_pairs={{0,2},{1,3},{2,0},{3,1},{4,6},{5,7},{6,4},{7,5},{8,10},{9,11},{10,... | collective-permute-start | bytes 196616 | tf_op jit(solution)/shard_map/ppermute | solution.py:513
  67.5 7.0 %collective-permute-start.14 = (bf16[16,2048]{1,0:T(8,128)(2,1)S(1)}, bf16[16,2048]{1,0:T(8,128)(2,1)S(1)}, u32[]{:S(2)}, u32[]{:S(2)}) collective-permute-start(bf16[16,2048]{1,0:T(8,128)(2,1)S(1)} %get-tuple-element.56), channel_id=1, source_target_pairs={{0,1},{1,2},{2,3},{3,0},{4,5},{5,6},{6,7},{7,4},{8,9},{9,10},{10,1... | collective-permute-start | bytes 196616 | tf_op jit(solution)/shard_map/ppermute | solution.py:513
